TPU v7x, 256 devices: a whole 4x4x8 slice. The times are simulated.
256 devices in a mesh: gx: 16 (over y, x), gy: 16 (over z, core).
Axes of the slice: x: 4, y: 4, z: 8, core: 2. Of those that a mesh axis runs over, the one named last changes fastest.
Arguments:
- pressure_source: float32 [16, 512, 2048], P(None, 'gx', 'gy'), may hold values from -0.5 to 1.5
- density: float32 [16, 512, 2048], P(None, 'gx', 'gy'), may hold values from 0.5 to 4
Outputs:
- pressure: float32 [16, 512, 2048], P(None, 'gx', 'gy')
All inputs are finite; a program needn't handle non-finite values.
Results may differ from a plain program's by a relative error of at most 0.0001.
Values sent between devices are 32-bit elements; how exact they have to be, the bound alone decides.
No kernel may reach another device: no remote copies, remote signals or barrier semaphores. Data moves between devices by JAX's collectives and lax.ppermute only.
A program may use at most 128 MiB of HBM per device.

v0:
```python
import jax
import jax.numpy as jnp
from jax import lax
from jax.experimental import pallas as pl
from jax.experimental.pallas import tpu as pltpu
from jax.sharding import PartitionSpec as P

NZ = 16
LANES = 128
SWEEPS = 6
VERTICAL = 0.015625
TINY = 2.0**-20
VMEM_BYTES = 48 * 1024 * 1024

ROW0 = (16, 8, 16, 8)
ROWS = (64, 32, 40, 24)
LANE0 = (0, 32, 16, 8)


def spacing(level):
    return 2.0 * 0.25**level


def lanes_of(shape=(8, LANES)):
    return lax.broadcasted_iota(jnp.int32, shape, 1)


def rows_of(shape=(8, LANES)):
    return lax.broadcasted_iota(jnp.int32, shape, 0)


def rcp(x):
    guess = pl.reciprocal(x, approx=True)
    return guess * (2.0 - x * guess)


def from_left(xs):
    rolled = [pltpu.roll(x, 1, 1) for x in xs]
    if len(xs) == 1:
        return rolled
    edge = lanes_of() == 0
    return [jnp.where(edge, rolled[1], rolled[0]), jnp.where(edge, rolled[0], rolled[1])]


def from_right(xs):
    rolled = [pltpu.roll(x, LANES - 1, 1) for x in xs]
    if len(xs) == 1:
        return rolled
    edge = lanes_of() == LANES - 1
    return [jnp.where(edge, rolled[1], rolled[0]), jnp.where(edge, rolled[0], rolled[1])]


def split_dot(x, matrix):
    high = x.astype(jnp.bfloat16)
    rest = x - high.astype(jnp.float32)
    middle = rest.astype(jnp.bfloat16)
    low = (rest - middle.astype(jnp.float32)).astype(jnp.bfloat16)
    dot = lambda part: jnp.dot(part, matrix, preferred_element_type=jnp.float32)
    return dot(high) + dot(middle) + dot(low)


def one_hot(rows, test, value):
    shape = (rows, LANES)
    source, target = lax.broadcasted_iota(jnp.int32, shape, 0), lax.broadcasted_iota(jnp.int32, shape, 1)
    return jnp.where(test(source, target), value, 0.0).astype(jnp.bfloat16)


def block_loop(starts, body):
    if len(starts) <= 3:
        for start in starts:
            body(start)
        return
    first, last = starts[0], starts[-1]

    def step(index, carry):
        body(jnp.minimum(first + 8 * index, last))
        return carry

    lax.fori_loop(0, len(starts), step, 0)


def starts_for(low, high):
    starts = list(range(low, high - 6, 8))
    if starts[-1] + 7 < high:
        starts.append(high - 7)
    return [min(s, high - 7) for s in starts]


class Level:
    def __init__(self, level, rho, ax, ay, d, e, g):
        self.level, self.rho, self.ax, self.ay, self.d, self.e, self.g = level, rho, ax, ay, d, e, g
        self.parts = range(len(ax))

    def faces(self, starts):
        scale = spacing(self.level)

        def body(r):
            for k in range(NZ):
                here = [ref[k, pl.ds(r, 8), :] for ref in self.rho]
                above = [ref[k, pl.ds(r - 1, 8), :] for ref in self.rho]
                left = from_left(here)
                for p in self.parts:
                    self.ax[p][k, pl.ds(r, 8), :] = scale * rcp(jnp.maximum(here[p] + above[p], TINY))
                    self.ay[p][k, pl.ds(r, 8), :] = scale * rcp(jnp.maximum(here[p] + left[p], TINY))

        block_loop(starts, body)

    def factor_and_first(self, starts, inside, f, v):
        def body(r):
            masks = [inside(r, p) for p in self.parts]
            ratio = [None for p in self.parts]
            partial = [[] for p in self.parts]
            ratios = [[] for p in self.parts]
            upper = [None for p in self.parts]
            rho = [ref[0, pl.ds(r, 8), :] for ref in self.rho]
            for p in self.parts:
                upper[p] = (2.0 * VERTICAL) * rcp(jnp.maximum(rho[p], TINY))
            for k in range(NZ):
                if k + 1 < NZ:
                    below = [ref[k + 1, pl.ds(r, 8), :] for ref in self.rho]
                    lower = [
                        (2.0 * VERTICAL) * rcp(jnp.maximum(rho[p] + below[p], TINY)) for p in self.parts
                    ]
                ay = [ref[k, pl.ds(r, 8), :] for ref in self.ay]
                right = from_right(ay)
                for p in self.parts:
                    center = (
                        self.ax[p][k, pl.ds(r, 8), :]
                        + self.ax[p][k, pl.ds(r + 1, 8), :]
                        + ay[p]
                        + right[p]
                        + upper[p]
                    )
                    if k + 1 < NZ:
                        center = center + lower[p]
                    pivot = center if k == 0 else center - upper[p] * ratio[p]
                    inverse = jnp.where(masks[p], rcp(pivot), 0.0)
                    scaled = 0.8 * inverse
                    self.d[p][k, pl.ds(r, 8), :] = scaled
                    value = scaled * f[p][k, pl.ds(r, 8), :]
                    if k > 0:
                        weight = upper[p] * inverse
                        self.e[p][k, pl.ds(r, 8), :] = weight
                        value = value + weight * partial[p][-1]
                    partial[p].append(value)
                    if k + 1 < NZ:
                        ratio[p] = lower[p] * inverse
                        self.g[p][k, pl.ds(r, 8), :] = ratio[p]
                        ratios[p].append(ratio[p])
                if k + 1 < NZ:
                    rho, upper = below, lower
            for p in self.parts:
                w = partial[p][-1]
                v[p][NZ - 1, pl.ds(r, 8), :] = w
                for k in range(NZ - 2, -1, -1):
                    w = partial[p][k] + ratios[p][k] * w
                    v[p][k, pl.ds(r, 8), :] = w

        block_loop(starts, body)

    def pull(self, v, k, r, wanted):
        here = [ref[k, pl.ds(r, 8), :] for ref in v]
        ay = [ref[k, pl.ds(r, 8), :] for ref in self.ay]
        left = from_left(here)
        right = from_right([a * x for a, x in zip(ay, here)])
        return here, [
            self.ax[p][k, pl.ds(r, 8), :] * v[p][k, pl.ds(r - 1, 8), :]
            + self.ax[p][k, pl.ds(r + 1, 8), :] * v[p][k, pl.ds(r + 1, 8), :]
            + ay[p] * left[p]
            + right[p]
            for p in wanted
        ]

    def relax(self, starts, f, v, out, u=None, wanted=None, shift=0):
        wanted = self.parts if wanted is None else wanted

        def body(r):
            partial = [[] for p in wanted]
            for k in range(NZ):
                _, pulls = self.pull(v, k, r, wanted)
                for n, p in enumerate(wanted):
                    value = self.d[p][k, pl.ds(r, 8), :] * (f[p][k, pl.ds(r, 8), :] + pulls[n])
                    if k > 0:
                        value = value + self.e[p][k, pl.ds(r, 8), :] * partial[n][-1]
                    partial[n].append(value)
            for n, p in enumerate(wanted):
                w = None
                for k in range(NZ - 1, -1, -1):
                    w = partial[n][k] if w is None else partial[n][k] + self.g[p][k, pl.ds(r, 8), :] * w
                    old = v[p][k, pl.ds(r, 8), :]
                    out[p][k, pl.ds(r - shift, 8), :] = 0.2 * old + w
                    if u is not None:
                        u[p][k, pl.ds(r, 8), :] = w - 0.6 * old

        block_loop(starts, body)

    def residual(self, starts, f, u, out):
        def body(r):
            for k in range(NZ):
                _, pulls = self.pull(u, k, r, self.parts)
                for p in self.parts:
                    out[p][k, pl.ds(r, 8), :] = 0.04 * f[p][k, pl.ds(r, 8), :] + pulls[p]

        block_loop(starts, body)


def inside_of(level, ix, iy, shape):
    grid_rows, grid_lanes, tile_rows, tile_lanes = shape
    lane = lanes_of()
    if level == 0:
        low_side = jnp.logical_and(lane < 64, iy * tile_lanes + tile_lanes < grid_lanes)
        sides = [None, jnp.logical_or(low_side, jnp.logical_and(lane >= 64, iy > 0))]
    else:
        column = iy * tile_lanes + lane - LANE0[level]
        sides = [jnp.logical_and(column >= 0, column < grid_lanes)]

    def inside(r, part):
        row = rows_of() + (r + ix * tile_rows - ROW0[level])
        good = jnp.logical_and(row >= 0, row < grid_rows)
        return good if sides[part] is None else jnp.logical_and(good, sides[part])

    return inside


def pair_rows(ref, k, start, count):
    layer = ref.at[k]
    return layer[pl.ds(start, count, stride=2), :] + layer[pl.ds(start + 1, count, stride=2), :]


def stack_rows(blocks):
    return jnp.concatenate(blocks, axis=0)


def down_kernel(ref, level, f, v, u, res, plan, inside):
    ref.faces(plan["faces"])
    ref.factor_and_first(plan["first"], inside, f, u)
    ref.relax(plan["second"], f, u, v, u=res)


def edges_kernel(f_ref, rho_ref, up_ref, dn_ref, left_ref, right_ref):
    lane = lanes_of()
    slot = lane // 16
    for field, own in enumerate((f_ref, rho_ref)):
        for block in range(8):
            for half in range(2):
                lefts, rights = None, None
                for q in range(8):
                    k = half * 8 + q
                    if block < 2:
                        x = up_ref[field * NZ + k, pl.ds(block * 8, 8), :]
                    elif block < 6:
                        x = own[k, pl.ds(block * 8 - 16, 8), :]
                    else:
                        x = dn_ref[field * NZ + k, pl.ds(block * 8 - 48, 8), :]
                    a = x if q == 0 else pltpu.roll(x, 16 * q, 1)
                    b = pltpu.roll(x, 16 * q + 16, 1) if q < 7 else x
                    lefts = a if q == 0 else jnp.where(slot == q, a, lefts)
                    rights = b if q == 0 else jnp.where(slot == q, b, rights)
                left_ref[field * 2 + half, pl.ds(block * 8, 8), :] = lefts
                right_ref[field * 2 + half, pl.ds(block * 8, 8), :] = rights


def fine_kernel(
    grid, index_ref, f_ref, rho_ref, up_ref, dn_ref, from_left_ref, from_right_ref,
    pack_ref, fm, fh, vm, vh, axm, axh, aym, ayh, dm, dh, em, eh, gm, gh, f1, v1, ax1, ay1, d1, e1, g1,
    rm, rh, firstm, firsth, um, uh, rho1, first1, u1, res1,
):
    ix, iy = index_ref[0], index_ref[1]
    grid_rows, grid_lanes = grid
    lane = lanes_of()
    inside = inside_of(0, ix, iy, (grid_rows, grid_lanes, 32, 128))

    for field, (own, main, side) in enumerate(((f_ref, fm, fh), (rho_ref, rm, rh))):
        for block in range(8):
            good = [inside(block * 8, part) for part in range(2)]
            for k in range(NZ):
                if block < 2:
                    x = up_ref[field * NZ + k, pl.ds(block * 8, 8), :]
                elif block < 6:
                    x = own[k, pl.ds(block * 8 - 16, 8), :]
                else:
                    x = dn_ref[field * NZ + k, pl.ds(block * 8 - 48, 8), :]
                q, half = k % 8, k // 8
                a = from_right_ref[field * 2 + half, pl.ds(block * 8, 8), :]
                a = a if q == 0 else pltpu.roll(a, LANES - 16 * q, 1)
                b = from_left_ref[field * 2 + half, pl.ds(block * 8, 8), :]
                b = b if q == 7 else pltpu.roll(b, 112 - 16 * q, 1)
                y = jnp.where(lane < 16, a, jnp.where(lane >= 112, b, 0.0))
                if field == 1:
                    y = jnp.where(good[1], y, 0.0)
                    if block < 2 or block >= 6:
                        x = jnp.where(good[0], x, 0.0)
                main[k, pl.ds(block * 8, 8), :] = x
                side[k, pl.ds(block * 8, 8), :] = y

    fine = Level(0, [rm, rh], [axm, axh], [aym, ayh], [dm, dh], [em, eh], [gm, gh])
    fine.faces(starts_for(6, 58))
    fine.factor_and_first(starts_for(6, 57), inside, [fm, fh], [firstm, firsth])
    fine.relax(starts_for(7, 56), [fm, fh], [firstm, firsth], [vm, vh], u=[um, uh])
    fine.residual(starts_for(8, 55), [fm, fh], [um, uh], [firstm, firsth])

    main_matrix = one_hot(LANES, lambda s, t: s // 2 + 32 == t, 0.25)
    side_matrix = one_hot(
        LANES,
        lambda s, t: jnp.logical_or(
            jnp.logical_and(s < 64, s // 2 + 96 == t), jnp.logical_and(s >= 64, s // 2 - 32 == t)
        ),
        0.25,
    )
    for first in range(0, NZ, 4):
        ks = range(first, first + 4)
        total = split_dot(stack_rows([pair_rows(firstm, k, 8, 24) for k in ks]), main_matrix)
        total = total + split_dot(stack_rows([pair_rows(firsth, k, 8, 24) for k in ks]), side_matrix)
        for n, k in enumerate(ks):
            f1[k, pl.ds(4, 24), :] = total[n * 24 : (n + 1) * 24]
        total = split_dot(stack_rows([pair_rows(rm, k, 0, 32) for k in ks]), main_matrix)
        total = total + split_dot(stack_rows([pair_rows(rh, k, 0, 32) for k in ks]), side_matrix)
        for n, k in enumerate(ks):
            rho1[k, :, :] = total[n * 32 : (n + 1) * 32]

    middle = Level(1, [rho1], [ax1], [ay1], [d1], [e1], [g1])
    inside = inside_of(1, ix, iy, (grid_rows // 2, grid_lanes // 2, 16, 64))
    middle.faces(starts_for(4, 28))
    middle.factor_and_first(starts_for(4, 27), inside, [f1], [first1])
    middle.relax(starts_for(5, 26), [f1], [first1], [v1], u=[u1])
    middle.residual(starts_for(8, 23), [f1], [u1], [res1])

    pack_matrix = one_hot(
        4 * LANES,
        lambda s, t: jnp.logical_and(
            (s % LANES) // 2 - 16 + 32 * (s // LANES) == t,
            jnp.logical_and(s % LANES >= 32, s % LANES < 96),
        ),
        0.25,
    )
    blocks = []
    for ref in (res1, rho1):
        for group in range(4):
            blocks.append(jnp.concatenate([pair_rows(ref, 4 * group + q, 8, 8) for q in range(4)], axis=1))
    packed = split_dot(stack_rows(blocks), pack_matrix)
    for n in range(8):
        pack_ref[n, :, :] = packed[n * 8 : (n + 1) * 8]


def coarser_kernel(
    grid, index_ref, own_ref, from_left_ref, from_right_ref,
    pack_ref, f2, v2, ax2, ay2, d2, e2, g2, f3, v3, ax3, ay3, d3, e3, g3,
    rho2, first2, u2, res2, rho3, first3, u3, res3,
):
    ix, iy = index_ref[0], index_ref[1]
    grid_rows, grid_lanes = grid
    lane = lanes_of()
    inside = inside_of(2, ix, iy, (grid_rows // 4, grid_lanes // 4, 8, 32))

    for field, target in enumerate((f2, rho2)):
        for block in range(5):
            good = inside(block * 8, 0)
            for k in range(NZ):
                group, q = field * 4 + k // 4, k % 4
                rolled = []
                for ref, amount in (
                    (from_left_ref, LANES - q * 32 - 16),
                    (own_ref, LANES + 16 - 32 * q),
                    (from_right_ref, LANES + 48 - 32 * q),
                ):
                    x = ref[group, pl.ds(block * 8, 8), :]
                    rolled.append(pltpu.roll(x, amount % LANES, 1))
                y = jnp.where(lane < 16, rolled[0], jnp.where(lane < 48, rolled[1], rolled[2]))
                if field == 1:
                    y = jnp.where(good, y, 0.0)
                target[k, pl.ds(block * 8, 8), :] = jnp.where(lane < 64, y, 0.0)

    level2 = Level(2, [rho2], [ax2], [ay2], [d2], [e2], [g2])
    level2.faces(starts_for(4, 36))
    level2.factor_and_first(starts_for(4, 35), inside, [f2], [first2])
    level2.relax(starts_for(5, 34), [f2], [first2], [v2], u=[u2])
    level2.residual(starts_for(6, 33), [f2], [u2], [res2])

    halve = one_hot(LANES, lambda s, t: s // 2 == t, 0.25)
    for ref, target, first, count in ((res2, f3, 4, 16), (rho2, rho3, 4, 16)):
        total = split_dot(stack_rows([pair_rows(ref, k, first, count) for k in range(NZ)]), halve)
        for k in range(NZ):
            target[k, pl.ds(first // 2, count), :] = total[k * count : (k + 1) * count]

    level3 = Level(3, [rho3], [ax3], [ay3], [d3], [e3], [g3])
    inside = inside_of(3, ix, iy, (grid_rows // 8, grid_lanes // 8, 4, 16))
    level3.faces(starts_for(3, 17))
    level3.factor_and_first(starts_for(3, 16), inside, [f3], [first3])
    level3.relax(starts_for(4, 15), [f3], [first3], [v3], u=[u3])
    level3.residual([6], [f3], [u3], [res3])

    spread = one_hot(
        LANES,
        lambda s, t: jnp.logical_and(s // 2 - 4 == t % 8, jnp.logical_and(s >= 8, s < 24)),
        0.25,
    )
    for field, ref in enumerate((res3, rho3)):
        total = split_dot(stack_rows([pair_rows(ref, k, 8, 8) for k in range(NZ)]), spread)
        merged = total[0:8]
        for k in range(1, NZ):
            merged = jnp.where(lane // 8 == k, total[k * 8 : (k + 1) * 8], merged)
        pack_ref[pl.ds(2 * field, 2), :] = merged[0:2]


def prolong(coarse, first_row, count, ref, old, target, target_row, matrix):
    rows = stack_rows([coarse(k) for k in range(NZ)])
    for part in range(len(target)):
        fine = split_dot(rows, matrix[part])
        for k in range(NZ):
            x = fine[k * count : (k + 1) * count]
            for odd in range(2):
                where = pl.ds(target_row + odd, count, stride=2)
                target[part].at[k][where, :] = old[part].at[k][where, :] + x


def top_kernel(
    grid, tiles, index_ref, gathered, fm, fh, vm, vh, axm, axh, aym, ayh, dm, dh, em, eh, gm, gh,
    f1, v1, ax1, ay1, d1, e1, g1, f2, v2, ax2, ay2, d2, e2, g2, f3, v3, ax3, ay3, d3, e3, g3,
    out_ref,
    rho4, f4, ax4, ay4, d4, e4, g4, q4, va4, vb4, va3, vb3, va2, vb2, va1, vb1, vam, vah, vbm, vbh,
):
    ix, iy = index_ref[0], index_ref[1]
    grid_rows, grid_lanes = grid
    lane = lanes_of()
    rows4 = grid_rows // 16
    tiles_x, tiles_y = tiles

    zero = jnp.zeros((8, LANES), jnp.float32)
    for ref in (rho4, va4, vb4):
        for k in range(NZ):
            ref[k, pl.ds(0, 8), :] = zero
            ref[k, pl.ds(8 + rows4, 8), :] = zero

    count = min(8, tiles_x)
    for field, target in enumerate((f4, rho4)):
        for r in range(2):
            for base in range(0, tiles_x, count):
                xs = [
                    gathered[pl.ds((base * tiles_y + t) * 4 + field * 2 + r, count, stride=4 * tiles_y), :]
                    for t in range(16)
                ]
                column = lax.broadcasted_iota(jnp.int32, (count, LANES), 1) // 8
                for bit in (1, 2, 4, 8):
                    high = (column & bit) != 0
                    for i in range(16):
                        if i & bit:
                            continue
                        a, b = xs[i], xs[i | bit]
                        xs[i] = jnp.where(high, pltpu.roll(b, 8 * bit, 1), a)
                        xs[i | bit] = jnp.where(high, b, pltpu.roll(a, LANES - 8 * bit, 1))
                for k in range(NZ):
                    target.at[k][pl.ds(8 + 2 * base + r, count, stride=2), :] = xs[k]

    scale = spacing(4)
    first_lane, last_lane = lane == 0, lane == LANES - 1
    starts = list(range(8, 8 + rows4, 8))
    for r in starts + [rows4 + 1]:
        for k in range(NZ):
            here = rho4[k, pl.ds(r, 8), :]
            above = rho4[k, pl.ds(r - 1, 8), :]
            left = jnp.where(first_lane, 0.0, pltpu.roll(here, 1, 1))
            ax4[k, pl.ds(r, 8), :] = scale * rcp(jnp.maximum(here + above, TINY))
            if r in starts:
                ay4[k, pl.ds(r, 8), :] = scale * rcp(jnp.maximum(here + left, TINY))

    centers = [None] * NZ
    for r in starts:
        rho = rho4[0, pl.ds(r, 8), :]
        upper = (2.0 * VERTICAL) * rcp(rho)
        partial, ratios, ratio = [], [], None
        for k in range(NZ):
            ay = ay4[k, pl.ds(r, 8), :]
            right = jnp.where(last_lane, scale * rcp(rho), pltpu.roll(ay, LANES - 1, 1))
            center = ax4[k, pl.ds(r, 8), :] + ax4[k, pl.ds(r + 1, 8), :] + ay + right + upper
            if k + 1 < NZ:
                below = rho4[k + 1, pl.ds(r, 8), :]
                lower = (2.0 * VERTICAL) * rcp(rho + below)
                center = center + lower
            centers[k] = center if centers[k] is None else centers[k] + center
            pivot = center if k == 0 else center - upper * ratio
            inverse = rcp(pivot)
            scaled = 0.8 * inverse
            d4[k, pl.ds(r, 8), :] = scaled
            source = f4[k, pl.ds(r, 8), :]
            q4[k, pl.ds(r, 8), :] = 0.8 * source
            value = scaled * source
            if k > 0:
                weight = upper * inverse
                e4[k, pl.ds(r, 8), :] = weight
                value = value + weight * partial[-1]
            partial.append(value)
            if k + 1 < NZ:
                ratio = lower * inverse
                g4[k, pl.ds(r, 8), :] = ratio
                ratios.append(ratio)
                rho, upper = below, lower
        w = partial[-1]
        va4[NZ - 1, pl.ds(r, 8), :] = w
        for k in range(NZ - 2, -1, -1):
            w = partial[k] + ratios[k] * w
            va4[k, pl.ds(r, 8), :] = w

    def pull4(v, k, r):
        here = v[k, pl.ds(r, 8), :]
        ay = ay4[k, pl.ds(r, 8), :]
        left = jnp.where(first_lane, 0.0, pltpu.roll(here, 1, 1))
        right = jnp.where(last_lane, 0.0, pltpu.roll(ay * here, LANES - 1, 1))
        return (
            f4[k, pl.ds(r, 8), :]
            + ax4[k, pl.ds(r, 8), :] * v[k, pl.ds(r - 1, 8), :]
            + ax4[k, pl.ds(r + 1, 8), :] * v[k, pl.ds(r + 1, 8), :]
            + ay * left
            + right
        )

    def sweep(v, out):
        for r in starts:
            partial = []
            for k in range(NZ):
                pulled = pull4(v, k, r)
                q4[k, pl.ds(r, 8), :] = 0.2 * q4[k, pl.ds(r, 8), :] + 0.8 * pulled
                value = d4[k, pl.ds(r, 8), :] * pulled
                if k > 0:
                    value = value + e4[k, pl.ds(r, 8), :] * partial[-1]
                partial.append(value)
            w = None
            for k in range(NZ - 1, -1, -1):
                w = partial[k] if w is None else partial[k] + g4[k, pl.ds(r, 8), :] * w
                out[k, pl.ds(r, 8), :] = 0.2 * v[k, pl.ds(r, 8), :] + w

    ends = [va4, vb4]
    for number in range(SWEEPS - 1):
        sweep(ends[number % 2], ends[(number + 1) % 2])
    final = ends[(SWEEPS - 1) % 2]
    shifts = []
    for k in range(NZ):
        total = None
        for r in starts:
            part = pull4(final, k, r) - q4[k, pl.ds(r, 8), :]
            total = part if total is None else total + part
        raised = jnp.sum(total, axis=(0, 1), keepdims=True)
        shifts.append(raised / jnp.sum(centers[k], axis=(0, 1), keepdims=True))

    row = rows_of() + (ix * 2 - 4)
    column = lane + (iy * 8 - 4)
    good = jnp.logical_and(
        jnp.logical_and(row >= 0, row < rows4),
        jnp.logical_and(jnp.logical_and(column >= 0, column < grid_lanes // 16), lane < 16),
    )
    amount = lax.rem(132 - iy * 8, LANES)

    def coarsest(k):
        x = final[k, pl.ds(4 + 2 * ix, 8), :] + shifts[k]
        return jnp.where(good, pltpu.roll(x, amount, 1), 0.0)

    repeat = one_hot(LANES, lambda s, t: s == t // 2, 1.0)
    prolong(coarsest, 0, 8, None, [v3], [va3], 0, [repeat])
    level3 = Level(3, None, [ax3], [ay3], [d3], [e3], [g3])
    level3.relax(starts_for(5, 14), [f3], [va3], [vb3])
    level3.relax([6], [f3], [vb3], [va3])

    prolong(lambda k: va3[k, pl.ds(6, 8), :], 0, 8, None, [v2], [va2], 12, [repeat])
    level2 = Level(2, None, [ax2], [ay2], [d2], [e2], [g2])
    level2.relax(starts_for(13, 26), [f2], [va2], [vb2])
    level2.relax(starts_for(14, 25), [f2], [vb2], [va2])

    prolong(lambda k: va2[k, pl.ds(12, 16), :], 0, 16, None, [v1], [va1], 0, [repeat])
    level1 = Level(1, None, [ax1], [ay1], [d1], [e1], [g1])
    level1.relax(starts_for(6, 25), [f1], [va1], [vb1])
    level1.relax(starts_for(7, 24), [f1], [vb1], [va1])

    to_main = one_hot(LANES, lambda s, t: s == t // 2 + 32, 1.0)
    to_side = one_hot(
        LANES,
        lambda s, t: jnp.logical_or(
            jnp.logical_and(t < 64, s == t // 2 + 96), jnp.logical_and(t >= 64, s == t // 2 - 32)
        ),
        1.0,
    )
    prolong(lambda k: va1[k, pl.ds(4, 24), :], 0, 24, None, [vm, vh], [vam, vah], 8, [to_main, to_side])
    fine = Level(0, None, [axm, axh], [aym, ayh], [dm, dh], [em, eh], [gm, gh])
    fine.relax(starts_for(15, 48), [fm, fh], [vam, vah], [vbm, vbh])
    fine.relax(starts_for(16, 47), [fm, fh], [vbm, vbh], [out_ref], wanted=[0], shift=16)


def ring(x, axis, step):
    size = lax.axis_size(axis)
    return lax.ppermute(x, axis, [(i, (i + step) % size) for i in range(size)])


def array(*shape):
    return jax.ShapeDtypeStruct(shape, jnp.float32)


def call(kernel, name, outs, scratch, index, *operands):
    vmem = pl.BlockSpec(memory_space=pltpu.VMEM)
    ins = [vmem] * len(operands)
    if index is not None:
        ins, operands = [pl.BlockSpec(memory_space=pltpu.SMEM)] + ins, (index,) + operands
    return pl.pallas_call(
        kernel,
        out_shape=outs,
        in_specs=ins,
        out_specs=[vmem] * len(outs),
        scratch_shapes=[pltpu.VMEM(shape, jnp.float32) for shape in scratch],
        compiler_params=pltpu.CompilerParams(vmem_limit_bytes=VMEM_BYTES),
        name=name,
    )(*operands)


def solution(mesh):
    tiles_x, tiles_y = mesh.shape["gx"], mesh.shape["gy"]
    grid = (32 * tiles_x, 128 * tiles_y)
    big = [array(NZ, ROWS[level], LANES) for level in range(4)]

    def on_device(source, rho):
        index = jnp.stack([lax.axis_index("gx"), lax.axis_index("gy")]).astype(jnp.int32)

        lows = jnp.concatenate([source[:, :16], rho[:, :16]], axis=0)
        highs = jnp.concatenate([source[:, 16:], rho[:, 16:]], axis=0)
        up = ring(highs, "gx", 1)
        dn = ring(lows, "gx", -1)
        strip = array(4, ROWS[0], LANES)
        lefts, rights = call(edges_kernel, "edges", [strip, strip], [], None, source, rho, up, dn)
        from_left_strip = ring(rights, "gy", 1)
        from_right_strip = ring(lefts, "gy", -1)

        s0, s1, s2, s3 = [x.shape for x in big]
        fine = call(
            lambda *refs: fine_kernel(grid, *refs),
            "fine",
            [array(8, 8, LANES)] + [big[0]] * 14 + [big[1]] * 7,
            [s0] * 6 + [s1] * 4,
            index, source, rho, up, dn, from_left_strip, from_right_strip,
        )
        tile = fine[0]
        pieces = [ring(tile, "gx", 2), ring(tile, "gx", 1), tile, ring(tile, "gx", -1), ring(tile, "gx", -2)]
        column = jnp.concatenate(pieces, axis=1)
        from_left_column = ring(column, "gy", 1)
        from_right_column = ring(column, "gy", -1)
        coarser = call(
            lambda *refs: coarser_kernel(grid, *refs),
            "coarser",
            [array(4, LANES)] + [big[2]] * 7 + [big[3]] * 7,
            [s2] * 4 + [s3] * 4,
            index, column, from_left_column, from_right_column,
        )
        devices = tiles_x * tiles_y
        blocks = jnp.broadcast_to(coarser[0][None], (devices, 4, LANES))
        gathered = lax.all_to_all(blocks, ("gx", "gy"), 0, 0).reshape(devices * 4, LANES)

        s4 = (NZ, 16 + 2 * tiles_x, LANES)
        (pressure,) = call(
            lambda *refs: top_kernel(grid, (tiles_x, tiles_y), *refs),
            "top",
            [array(NZ, 32, LANES)],
            [s4] * 10 + [s3] * 2 + [s2] * 2 + [s1] * 2 + [s0] * 4,
            index, gathered, *fine[1:], *coarser[1:],
        )
        return pressure

    return jax.shard_map(
        on_device,
        mesh=mesh,
        in_specs=(P(None, "gx", "gy"), P(None, "gx", "gy")),
        out_specs=P(None, "gx", "gy"),
        check_vma=False,
    )
```

profile of v0, /device:TPU:1, one launch (start us, length us, event | category | flops | bytes accessed | tf_op | source)
XLA Modules:
  0.0 103.1 jit_solution(9883526466241602533)
XLA Ops:
  0.0 1.1 %fusion = (f32[16,16,128]{2,1,0:T(8,128)S(1)}, f32[16,16,128]{2,1,0:T(8,128)S(1)}, f32[16,16,128]{2,1,0:T(8,128)S(1)}, f32[16,16,128]{2,1,0:T(8,128)S(1)}) fusion(f32[16,32,128]{2,1,0:T(8,128)} %refs_1_.1, f32[16,32,128]{2,1,0:T(8,128)} %refs_2_.1), kind=kLoop, calls=%fused_computation.8 | loop fusion | bytes 1048576 | tf_op jit(solution)/shard_map/slice | solution.py:619
  1.2 2.1 %collective-permute-start = (f32[32,16,128]{2,1,0:T(8,128)S(1)}, f32[32,16,128]{2,1,0:T(8,128)S(1)}, u32[]{:S(2)}, u32[]{:S(2)}) collective-permute-start(f32[32,16,128]{2,1,0:T(8,128)S(1)} %pad_maximum_fusion), channel_id=1, source_target_pairs={{0,16},{16,32},{32,48},{48,64},{64,80},{80,96},{96,112},{112,128},... | collective-permute-start | bytes 786440 | tf_op jit(solution)/shard_map/ppermute | solution.py:588
  3.3 0.0 copy-start
  3.3 0.0 copy-start.1
  3.3 3.8 %collective-permute-start.1 = (f32[32,16,128]{2,1,0:T(8,128)S(1)}, f32[32,16,128]{2,1,0:T(8,128)S(1)}, u32[]{:S(2)}, u32[]{:S(2)}) collective-permute-start(f32[32,16,128]{2,1,0:T(8,128)S(1)} %pad_maximum_fusion.1), channel_id=1, source_target_pairs={{0,240},{16,0},{32,16},{48,32},{64,48},{80,64},{96,80},{112,96},{1... | collective-permute-start | bytes 786440 | tf_op jit(solution)/shard_map/ppermute | solution.py:588
  7.1 3.9 %collective-permute-done.up_ref.refs_3_ = f32[32,16,128]{2,1,0:T(8,128)S(1)} collective-permute-done((f32[32,16,128]{2,1,0:T(8,128)S(1)}, f32[32,16,128]{2,1,0:T(8,128)S(1)}, u32[]{:S(2)}, u32[]{:S(2)}) %collective-permute-start) | collective-permute-done | bytes 262176 | tf_op jit(solution)/shard_map/ppermute | solution.py:588
  11.1 0.0 collective-permute-done.1.dn_ref.refs_4_
  11.1 0.0 copy-done
  11.1 0.0 copy-done.1
  11.1 0.5 edges.1
  11.6 4.7 %collective-permute-start.2 = (f32[4,64,128]{2,1,0:T(8,128)S(1)}, f32[4,64,128]{2,1,0:T(8,128)S(1)}, u32[]{:S(2)}, u32[]{:S(2)}) collective-permute-start(f32[4,64,128]{2,1,0:T(8,128)S(1)} %get-tuple-element.44), channel_id=1, source_target_pairs={{0,1},{1,2},{2,3},{3,4},{4,5},{5,6},{6,7},{7,8},{8,9},{9,10},{10,1... | collective-permute-start | bytes 393224 | tf_op jit(solution)/shard_map/ppermute | solution.py:588
  16.4 0.0 collective-permute-start.3
  16.4 0.1 pad_add_fusion.refs_0_
  16.4 1.9 %collective-permute-done.2.refs_5_ = f32[4,64,128]{2,1,0:T(8,128)S(1)} collective-permute-done((f32[4,64,128]{2,1,0:T(8,128)S(1)}, f32[4,64,128]{2,1,0:T(8,128)S(1)}, u32[]{:S(2)}, u32[]{:S(2)}) %collective-permute-start.2) | collective-permute-done | bytes 131104 | tf_op jit(solution)/shard_map/ppermute | solution.py:588
  18.3 2.7 %collective-permute-done.3.refs_6_ = f32[4,64,128]{2,1,0:T(8,128)S(1)} collective-permute-done((f32[4,64,128]{2,1,0:T(8,128)S(1)}, f32[4,64,128]{2,1,0:T(8,128)S(1)}, u32[]{:S(2)}, u32[]{:S(2)}) %collective-permute-start.3) | collective-permute-done | bytes 131104 | tf_op jit(solution)/shard_map/ppermute | solution.py:588
  21.0 9.8 %fine.1 = (f32[8,8,128]{2,1,0:T(8,128)S(1)}, f32[16,64,128]{2,1,0:T(8,128)S(1)}, f32[16,64,128]{2,1,0:T(8,128)S(1)}, f32[16,64,128]{2,1,0:T(8,128)S(1)}, f32[16,...) custom-call(s32[2]{0:T(128)S(1)} %pad_add_fusion.refs_0_, ...), custom_call_target="tpu_custom_call" | custom-call | tf_op jit(solution)/shard_map/fine/pallas_call | solution.py:600
  30.8 0.0 copy-start.2
  30.8 0.8 copy-done.2
  31.6 0.0 copy-start.3
  31.6 0.8 copy-done.3
  32.5 0.0 copy-start.4
  32.5 0.8 copy-done.4
  33.3 0.0 copy-start.5
  33.3 0.8 copy-done.5
  34.1 0.0 copy-start.6
  34.1 0.8 copy-done.6
  34.9 0.3 collective-permute-start.4
  35.1 4.8 %collective-permute-start.7 = (f32[8,8,128]{2,1,0:T(8,128)S(1)}, f32[8,8,128]{2,1,0:T(8,128)S(1)}, u32[]{:S(2)}, u32[]{:S(2)}) collective-permute-start(f32[8,8,128]{2,1,0:T(8,128)S(1)} %get-tuple-element.46), channel_id=1, source_target_pairs={{0,224},{16,240},{32,0},{48,16},{64,32},{80,48},{96,64},{112,80},{... | collective-permute-start | bytes 98312 | tf_op jit(solution)/shard_map/ppermute | solution.py:588
  39.9 2.8 %collective-permute-start.6 = (f32[8,8,128]{2,1,0:T(8,128)S(1)}, f32[8,8,128]{2,1,0:T(8,128)S(1)}, u32[]{:S(2)}, u32[]{:S(2)}) collective-permute-start(f32[8,8,128]{2,1,0:T(8,128)S(1)} %get-tuple-element.46), channel_id=1, source_target_pairs={{0,240},{16,0},{32,16},{48,32},{64,48},{80,64},{96,80},{112,96},{1... | collective-permute-start | bytes 98312 | tf_op jit(solution)/shard_map/ppermute | solution.py:588
  42.7 0.0 collective-permute-start.5
  42.8 0.0 collective-permute-done.4
  42.8 6.1 %collective-permute-done.5 = f32[8,8,128]{2,1,0:T(8,128)S(1)} collective-permute-done((f32[8,8,128]{2,1,0:T(8,128)S(1)}, f32[8,8,128]{2,1,0:T(8,128)S(1)}, u32[]{:S(2)}, u32[]{:S(2)}) %collective-permute-start.5) | collective-permute-done | bytes 32800 | tf_op jit(solution)/shard_map/ppermute | solution.py:588
  48.8 0.0 collective-permute-done.6
  48.9 0.0 collective-permute-done.7
  48.9 2.8 %collective-permute-start.9 = (f32[8,40,128]{2,1,0:T(8,128)S(1)}, f32[8,40,128]{2,1,0:T(8,128)S(1)}, u32[]{:S(2)}, u32[]{:S(2)}) collective-permute-start(f32[8,40,128]{2,1,0:T(8,128)S(1)} %constant_dynamic-update-slice_fusion.refs_1_), channel_id=1, source_target_pairs={{0,15},{1,0},{2,1},{3,2},{4,3},{5,4},{6,5},{7,6},{8,7},{9,8},{10,9... | collective-permute-start | bytes 491528 | tf_op jit(solution)/shard_map/ppermute | solution.py:588
  51.6 0.0 collective-permute-start.8
  51.6 2.1 %collective-permute-done.9.refs_3_ = f32[8,40,128]{2,1,0:T(8,128)S(1)} collective-permute-done((f32[8,40,128]{2,1,0:T(8,128)S(1)}, f32[8,40,128]{2,1,0:T(8,128)S(1)}, u32[]{:S(2)}, u32[]{:S(2)}) %collective-permute-start.9) | collective-permute-done | bytes 163872 | tf_op jit(solution)/shard_map/ppermute | solution.py:588
  53.7 0.2 collective-permute-done.8.refs_2_
  53.9 4.9 %coarser.1 = (f32[4,128]{1,0:T(4,128)S(1)}, f32[16,40,128]{2,1,0:T(8,128)S(1)}, f32[16,40,128]{2,1,0:T(8,128)S(1)}, f32[16,40,128]{2,1,0:T(8,128)S(1)}, f32[16,4...) custom-call(s32[2]{0:T(128)S(1)} %pad_add_fusion.refs_0_, ...), custom_call_target="tpu_custom_call" | custom-call | tf_op jit(solution)/shard_map/coarser/pallas_call | solution.py:600
  58.9 0.1 broadcast_in_dim.2
  58.9 33.6 %all_to_all.5 = f32[256,4,128]{2,1,0:T(4,128)S(1)} all-to-all(f32[256,4,128]{2,1,0:T(4,128)S(1)} %broadcast_in_dim.2), channel_id=1, replica_groups=mesh['gx'=16,'gy'=16] {'gx','gy'}, dimensions={0} | all-to-all | bytes 1048576 | tf_op jit(solution)/shard_map/all_to_all | solution.py:650
  92.5 10.6 %top.1 = f32[16,32,128]{2,1,0:T(8,128)} custom-call(s32[2]{0:T(128)S(1)} %pad_add_fusion.refs_0_, f32[1024,128]{1,0:T(8,128)S(1)} %bitcast.3, f32[16,64,128]{2,1,0:T(8,128)} %copy-done.2, f32[16,64,128]{2,1,0:T(8,128)} %copy-done.3, f32[16,64,128]{2,1,0:T(8,128)} %copy-done.4, f32[16,64,128]{2,1,0:T(8,128)} %copy-done.5, f32[16,64,128]{2,1,0:T(8,128)} %copy-done.6, ...), custom_call_target="tpu_custom_call" | custom-call | tf_op jit(solution)/shard_map/top/pallas_call | solution.py:600
  (7 shorter events, 0.1 us)
Async XLA Ops:
  1.2 9.9 %collective-permute-start = (f32[32,16,128]{2,1,0:T(8,128)S(1)}, f32[32,16,128]{2,1,0:T(8,128)S(1)}, u32[]{:S(2)}, u32[]{:S(2)}) collective-permute-start(f32[32,16,128]{2,1,0:T(8,128)S(1)} %pad_maximum_fusion), channel_id=1, source_target_pairs={{0,16},{16,32},{32,48},{48,64},{64,80},{80,96},{96,112},{112,128},... | collective-permute-start | bytes 786440 | tf_op jit(solution)/shard_map/ppermute | solution.py:588
  3.3 7.8 %copy-start = (f32[16,32,128]{2,1,0:T(8,128)S(1)}, f32[16,32,128]{2,1,0:T(8,128)}, u32[]{:S(2)}) copy-start(f32[16,32,128]{2,1,0:T(8,128)} %refs_1_.1) | copy-start | bytes 786436
  3.3 7.8 %copy-start.1 = (f32[16,32,128]{2,1,0:T(8,128)S(1)}, f32[16,32,128]{2,1,0:T(8,128)}, u32[]{:S(2)}) copy-start(f32[16,32,128]{2,1,0:T(8,128)} %refs_2_.1) | copy-start | bytes 786436
  3.3 7.8 %collective-permute-start.1 = (f32[32,16,128]{2,1,0:T(8,128)S(1)}, f32[32,16,128]{2,1,0:T(8,128)S(1)}, u32[]{:S(2)}, u32[]{:S(2)}) collective-permute-start(f32[32,16,128]{2,1,0:T(8,128)S(1)} %pad_maximum_fusion.1), channel_id=1, source_target_pairs={{0,240},{16,0},{32,16},{48,32},{64,48},{80,64},{96,80},{112,96},{1... | collective-permute-start | bytes 786440 | tf_op jit(solution)/shard_map/ppermute | solution.py:588
  11.6 6.7 %collective-permute-start.2 = (f32[4,64,128]{2,1,0:T(8,128)S(1)}, f32[4,64,128]{2,1,0:T(8,128)S(1)}, u32[]{:S(2)}, u32[]{:S(2)}) collective-permute-start(f32[4,64,128]{2,1,0:T(8,128)S(1)} %get-tuple-element.44), channel_id=1, source_target_pairs={{0,1},{1,2},{2,3},{3,4},{4,5},{5,6},{6,7},{7,8},{8,9},{9,10},{10,1... | collective-permute-start | bytes 393224 | tf_op jit(solution)/shard_map/ppermute | solution.py:588
  16.4 4.7 %collective-permute-start.3 = (f32[4,64,128]{2,1,0:T(8,128)S(1)}, f32[4,64,128]{2,1,0:T(8,128)S(1)}, u32[]{:S(2)}, u32[]{:S(2)}) collective-permute-start(f32[4,64,128]{2,1,0:T(8,128)S(1)} %get-tuple-element.45), channel_id=1, source_target_pairs={{0,15},{1,0},{2,1},{3,2},{4,3},{5,4},{6,5},{7,6},{8,7},{9,8},{10,9... | collective-permute-start | bytes 393224 | tf_op jit(solution)/shard_map/ppermute | solution.py:588
  30.8 0.8 copy-start.2
  31.6 0.8 copy-start.3
  32.5 0.8 copy-start.4
  33.3 0.8 copy-start.5
  34.1 0.8 copy-start.6
  34.9 7.9 %collective-permute-start.4 = (f32[8,8,128]{2,1,0:T(8,128)S(1)}, f32[8,8,128]{2,1,0:T(8,128)S(1)}, u32[]{:S(2)}, u32[]{:S(2)}) collective-permute-start(f32[8,8,128]{2,1,0:T(8,128)S(1)} %get-tuple-element.46), channel_id=1, source_target_pairs={{0,32},{16,48},{32,64},{48,80},{64,96},{80,112},{96,128},{112,144}... | collective-permute-start | bytes 98312 | tf_op jit(solution)/shard_map/ppermute | solution.py:588
  35.1 13.7 %collective-permute-start.7 = (f32[8,8,128]{2,1,0:T(8,128)S(1)}, f32[8,8,128]{2,1,0:T(8,128)S(1)}, u32[]{:S(2)}, u32[]{:S(2)}) collective-permute-start(f32[8,8,128]{2,1,0:T(8,128)S(1)} %get-tuple-element.46), channel_id=1, source_target_pairs={{0,224},{16,240},{32,0},{48,16},{64,32},{80,48},{96,64},{112,80},{... | collective-permute-start | bytes 98312 | tf_op jit(solution)/shard_map/ppermute | solution.py:588
  39.9 8.9 %collective-permute-start.6 = (f32[8,8,128]{2,1,0:T(8,128)S(1)}, f32[8,8,128]{2,1,0:T(8,128)S(1)}, u32[]{:S(2)}, u32[]{:S(2)}) collective-permute-start(f32[8,8,128]{2,1,0:T(8,128)S(1)} %get-tuple-element.46), channel_id=1, source_target_pairs={{0,240},{16,0},{32,16},{48,32},{64,48},{80,64},{96,80},{112,96},{1... | collective-permute-start | bytes 98312 | tf_op jit(solution)/shard_map/ppermute | solution.py:588
  42.7 6.1 %collective-permute-start.5 = (f32[8,8,128]{2,1,0:T(8,128)S(1)}, f32[8,8,128]{2,1,0:T(8,128)S(1)}, u32[]{:S(2)}, u32[]{:S(2)}) collective-permute-start(f32[8,8,128]{2,1,0:T(8,128)S(1)} %get-tuple-element.46), channel_id=1, source_target_pairs={{0,16},{16,32},{32,48},{48,64},{64,80},{80,96},{96,112},{112,128},... | collective-permute-start | bytes 98312 | tf_op jit(solution)/shard_map/ppermute | solution.py:588
  48.9 4.8 %collective-permute-start.9 = (f32[8,40,128]{2,1,0:T(8,128)S(1)}, f32[8,40,128]{2,1,0:T(8,128)S(1)}, u32[]{:S(2)}, u32[]{:S(2)}) collective-permute-start(f32[8,40,128]{2,1,0:T(8,128)S(1)} %constant_dynamic-update-slice_fusion.refs_1_), channel_id=1, source_target_pairs={{0,15},{1,0},{2,1},{3,2},{4,3},{5,4},{6,5},{7,6},{8,7},{9,8},{10,9... | collective-permute-start | bytes 491528 | tf_op jit(solution)/shard_map/ppermute | solution.py:588
  51.6 2.3 %collective-permute-start.8 = (f32[8,40,128]{2,1,0:T(8,128)S(1)}, f32[8,40,128]{2,1,0:T(8,128)S(1)}, u32[]{:S(2)}, u32[]{:S(2)}) collective-permute-start(f32[8,40,128]{2,1,0:T(8,128)S(1)} %constant_dynamic-update-slice_fusion.refs_1_), channel_id=1, source_target_pairs={{0,1},{1,2},{2,3},{3,4},{4,5},{5,6},{6,7},{7,8},{8,9},{9,10},{10,1... | collective-permute-start | bytes 491528 | tf_op jit(solution)/shard_map/ppermute | solution.py:588
where the time goes:
time: 103 us
  blocking collectives  33.6 us (33%)
  Pallas kernels  25.9 us (25%)
  starting transfers between devices  21.3 us (21%)
  waiting for transfers between devices  16.9 us (16%)
  local copies, waits for them, and re-layouts  5.24 us (5%)
    all_to_all x1, blocking collectives, on_device(): lax.all_to_all(blocks, ('gx', 'gy'), 0, 0).reshape(devices * 4, LANES)  33.6 us
    pallas_call x4, Pallas kernels, call(): pl.pallas_call(kernel, out_shape=outs, in_specs=ins, out_specs=[vmem] * l...  25.9 us
    ppermute x10, starting transfers between devices, ring(): return lax.ppermute(x, axis, [(i, (i + step) % size) for i in range(size)])  21.3 us
    ppermute x10, waiting for transfers between devices, ring(): return lax.ppermute(x, axis, [(i, (i + step) % size) for i in range(size)])  16.9 us
    unnamed x18, local copies, waits for them, and re-layouts  4.04 us
  transfers between devices with their start and end apart: 10, of which 6 were waited for; matrix products, arithmetic and copies ran while one was open for 0% of the time, Pallas kernels for 0%

commit v1 on v0

v1 whole, which is shorter than its diff:
```python
import jax
import jax.numpy as jnp
from jax import lax
from jax.experimental import pallas as pl
from jax.experimental.pallas import tpu as pltpu
from jax.sharding import PartitionSpec as P

NZ = 16
LANES = 128
SWEEPS = 6
VERTICAL = 0.015625
TINY = 2.0**-20
VMEM_BYTES = 24 * 1024 * 1024

ROW0 = (16, 8, 16, 8)
ROWS = (64, 32, 40, 24)
LANE0 = (0, 32, 16, 8)


def spacing(level):
    return 2.0 * 0.25**level


def lanes_of(shape=(8, LANES)):
    return lax.broadcasted_iota(jnp.int32, shape, 1)


def rows_of(shape=(8, LANES)):
    return lax.broadcasted_iota(jnp.int32, shape, 0)


def rcp(x):
    guess = pl.reciprocal(x, approx=True)
    return guess * (2.0 - x * guess)


def from_left(xs):
    rolled = [pltpu.roll(x, 1, 1) for x in xs]
    if len(xs) == 1:
        return rolled
    edge = lanes_of(xs[0].shape) == 0
    return [jnp.where(edge, rolled[1], rolled[0]), jnp.where(edge, rolled[0], rolled[1])]


def from_right(xs):
    rolled = [pltpu.roll(x, LANES - 1, 1) for x in xs]
    if len(xs) == 1:
        return rolled
    edge = lanes_of(xs[0].shape) == LANES - 1
    return [jnp.where(edge, rolled[1], rolled[0]), jnp.where(edge, rolled[0], rolled[1])]


def split_dot(x, matrix, pieces=2):
    total = None
    for piece in range(pieces):
        part = x.astype(jnp.bfloat16)
        product = jnp.dot(part, matrix, preferred_element_type=jnp.float32)
        total = product if total is None else total + product
        if piece + 1 < pieces:
            x = x - part.astype(jnp.float32)
    return total


def one_hot(rows, test, value, lanes=LANES):
    shape = (rows, lanes)
    source, target = lax.broadcasted_iota(jnp.int32, shape, 0), lax.broadcasted_iota(jnp.int32, shape, 1)
    return jnp.where(test(source, target), value, 0.0).astype(jnp.bfloat16)


def run_blocks(blocks, body):
    for block in blocks:
        if len(block) == 2:
            body(*block)
        else:
            first, height, count = block

            def step(index, carry):
                body(first + height * index, height)
                return carry

            lax.fori_loop(0, count, step, 0)


class Level:
    def __init__(self, level, rho, ax, ay, d, e, g):
        self.level, self.rho, self.ax, self.ay, self.d, self.e, self.g = level, rho, ax, ay, d, e, g
        self.parts = range(len(ax))

    def faces(self, blocks):
        scale = spacing(self.level)

        def body(r, h):
            for k in range(NZ):
                here = [ref[k, pl.ds(r, h), :] for ref in self.rho]
                above = [ref[k, pl.ds(r - 1, h), :] for ref in self.rho]
                left = from_left(here)
                for p in self.parts:
                    self.ax[p][k, pl.ds(r, h), :] = scale * rcp(jnp.maximum(here[p] + above[p], TINY))
                    self.ay[p][k, pl.ds(r, h), :] = scale * rcp(jnp.maximum(here[p] + left[p], TINY))

        run_blocks(blocks, body)

    def factor_and_first(self, blocks, inside, f, v):
        def body(r, h):
            masks = [inside(r, h, p) for p in self.parts]
            ratio = [None for p in self.parts]
            partial = [[] for p in self.parts]
            upper = [None for p in self.parts]
            rho = [ref[0, pl.ds(r, h), :] for ref in self.rho]
            for p in self.parts:
                upper[p] = (2.0 * VERTICAL) * rcp(jnp.maximum(rho[p], TINY))
            for k in range(NZ):
                if k + 1 < NZ:
                    below = [ref[k + 1, pl.ds(r, h), :] for ref in self.rho]
                    lower = [
                        (2.0 * VERTICAL) * rcp(jnp.maximum(rho[p] + below[p], TINY)) for p in self.parts
                    ]
                ay = [ref[k, pl.ds(r, h), :] for ref in self.ay]
                right = from_right(ay)
                for p in self.parts:
                    center = (
                        self.ax[p][k, pl.ds(r, h), :]
                        + self.ax[p][k, pl.ds(r + 1, h), :]
                        + ay[p]
                        + right[p]
                        + upper[p]
                    )
                    if k + 1 < NZ:
                        center = center + lower[p]
                    pivot = center if k == 0 else center - upper[p] * ratio[p]
                    inverse = jnp.where(masks[p], rcp(pivot), 0.0)
                    scaled = 0.8 * inverse
                    self.d[p][k, pl.ds(r, h), :] = scaled
                    value = scaled * f[p][k, pl.ds(r, h), :]
                    if k > 0:
                        weight = upper[p] * inverse
                        self.e[p][k, pl.ds(r, h), :] = weight
                        value = value + weight * partial[p][-1]
                    partial[p].append(value)
                    if k + 1 < NZ:
                        ratio[p] = lower[p] * inverse
                        self.g[p][k, pl.ds(r, h), :] = ratio[p]
                if k + 1 < NZ:
                    rho, upper = below, lower
            for p in self.parts:
                w = partial[p][-1]
                v[p][NZ - 1, pl.ds(r, h), :] = w
                for k in range(NZ - 2, -1, -1):
                    w = partial[p][k] + self.g[p][k, pl.ds(r, h), :] * w
                    v[p][k, pl.ds(r, h), :] = w

        run_blocks(blocks, body)

    def pull(self, v, k, r, h, wanted):
        here = [ref[k, pl.ds(r, h), :] for ref in v]
        ay = [ref[k, pl.ds(r, h), :] for ref in self.ay]
        left = from_left(here)
        right = from_right([a * x for a, x in zip(ay, here)])
        return [
            self.ax[p][k, pl.ds(r, h), :] * v[p][k, pl.ds(r - 1, h), :]
            + self.ax[p][k, pl.ds(r + 1, h), :] * v[p][k, pl.ds(r + 1, h), :]
            + ay[p] * left[p]
            + right[p]
            for p in wanted
        ]

    def relax(self, blocks, f, v, out, u=None, wanted=None, shift=0):
        wanted = self.parts if wanted is None else wanted

        def body(r, h):
            partial = [[] for p in wanted]
            for k in range(NZ):
                pulls = self.pull(v, k, r, h, wanted)
                for n, p in enumerate(wanted):
                    value = self.d[p][k, pl.ds(r, h), :] * (f[p][k, pl.ds(r, h), :] + pulls[n])
                    if k > 0:
                        value = value + self.e[p][k, pl.ds(r, h), :] * partial[n][-1]
                    partial[n].append(value)
            for n, p in enumerate(wanted):
                w = None
                for k in range(NZ - 1, -1, -1):
                    w = partial[n][k] if w is None else partial[n][k] + self.g[p][k, pl.ds(r, h), :] * w
                    old = v[p][k, pl.ds(r, h), :]
                    out[p][k, pl.ds(r - shift, h), :] = 0.2 * old + w
                    if u is not None:
                        u[p][k, pl.ds(r, h), :] = w - 0.6 * old

        run_blocks(blocks, body)

    def residual(self, blocks, f, u, out):
        def body(r, h):
            for k in range(NZ):
                pulls = self.pull(u, k, r, h, self.parts)
                for p in self.parts:
                    out[p][k, pl.ds(r, h), :] = 0.04 * f[p][k, pl.ds(r, h), :] + pulls[p]

        run_blocks(blocks, body)


def inside_of(level, ix, iy, shape):
    grid_rows, grid_lanes, tile_rows, tile_lanes = shape

    def inside(r, h, part):
        row, lane = rows_of((h, LANES)) + (r + ix * tile_rows - ROW0[level]), lanes_of((h, LANES))
        good = jnp.logical_and(row >= 0, row < grid_rows)
        if level == 0 and part == 0:
            return good
        if level == 0:
            right = jnp.logical_and(lane < 64, iy * tile_lanes + tile_lanes < grid_lanes)
            side = jnp.logical_or(right, jnp.logical_and(lane >= 64, iy > 0))
        else:
            column = iy * tile_lanes + lane - LANE0[level]
            side = jnp.logical_and(column >= 0, column < grid_lanes)
        return jnp.logical_and(good, side)

    return inside


def pair_rows(ref, k, start, count):
    layer = ref.at[k]
    return layer[pl.ds(start, count, stride=2), :] + layer[pl.ds(start + 1, count, stride=2), :]


def stack_rows(blocks):
    return jnp.concatenate(blocks, axis=0)


def edges_kernel(f_ref, rho_ref, up_ref, dn_ref, left_ref, right_ref):
    lane = lanes_of()
    slot = lane // 16
    for field, own in enumerate((f_ref, rho_ref)):
        for block in range(8):
            for half in range(2):
                lefts, rights = None, None
                for q in range(8):
                    k = half * 8 + q
                    if block < 2:
                        x = up_ref[field * NZ + k, pl.ds(block * 8, 8), :]
                    elif block < 6:
                        x = own[k, pl.ds(block * 8 - 16, 8), :]
                    else:
                        x = dn_ref[field * NZ + k, pl.ds(block * 8 - 48, 8), :]
                    a = x if q == 0 else pltpu.roll(x, 16 * q, 1)
                    b = pltpu.roll(x, 16 * q + 16, 1) if q < 7 else x
                    lefts = a if q == 0 else jnp.where(slot == q, a, lefts)
                    rights = b if q == 0 else jnp.where(slot == q, b, rights)
                left_ref[field * 2 + half, pl.ds(block * 8, 8), :] = lefts
                right_ref[field * 2 + half, pl.ds(block * 8, 8), :] = rights


def fine_kernel(
    grid, index_ref, f_ref, rho_ref, up_ref, dn_ref, from_left_ref, from_right_ref,
    pack_ref, fm, fh, vm, vh, axm, axh, aym, ayh, dm, dh, em, eh, gm, gh, f1, v1, ax1, ay1, d1, e1, g1,
    rm, rh, firstm, firsth, um, uh, rho1, first1, u1, res1,
):
    ix, iy = index_ref[0], index_ref[1]
    grid_rows, grid_lanes = grid
    inside = inside_of(0, ix, iy, (grid_rows, grid_lanes, 32, 128))

    unpack = one_hot(
        2 * LANES,
        lambda s, t: jnp.logical_or(
            jnp.logical_and(s < LANES, (t // LANES) * 16 == s - t % LANES) & (t % LANES < 16),
            jnp.logical_and(s >= LANES, (t // LANES) * 16 == s - t % LANES - 16) & (t % LANES >= 112),
        ),
        1.0,
        8 * LANES,
    )
    for field, (own, main, side) in enumerate(((f_ref, fm, fh), (rho_ref, rm, rh))):
        for k in range(NZ):
            for first, count, source, shift in (
                (0, 16, up_ref, 0),
                (16, 32, own, -16),
                (48, 16, dn_ref, -48),
            ):
                layer = k if source is own else field * NZ + k
                x = source[layer, pl.ds(first + shift, count), :]
                if field == 1 and source is not own:
                    x = jnp.where(inside(first, count, 0), x, 0.0)
                main[k, pl.ds(first, count), :] = x
        for half in range(2):
            strips = jnp.concatenate([from_right_ref[field * 2 + half], from_left_ref[field * 2 + half]], axis=1)
            wide = split_dot(strips, unpack, 3)
            for q in range(8):
                y = wide[:, q * LANES : (q + 1) * LANES]
                if field == 1:
                    y = jnp.where(inside(0, 64, 1), y, 0.0)
                side[half * 8 + q, :, :] = y

    fine = Level(0, [rm, rh], [axm, axh], [aym, ayh], [dm, dh], [em, eh], [gm, gh])
    fine.faces([(6, 16, 3), (51, 8)])
    fine.factor_and_first([(6, 16, 3), (50, 8)], inside, [fm, fh], [firstm, firsth])
    fine.relax([(7, 16, 3), (49, 8)], [fm, fh], [firstm, firsth], [vm, vh], u=[um, uh])
    fine.residual([(8, 16, 3)], [fm, fh], [um, uh], [firstm, firsth])

    main_matrix = one_hot(LANES, lambda s, t: s // 2 + 32 == t, 0.25)
    side_matrix = one_hot(
        LANES,
        lambda s, t: jnp.logical_or(
            jnp.logical_and(s < 64, s // 2 + 96 == t), jnp.logical_and(s >= 64, s // 2 - 32 == t)
        ),
        0.25,
    )
    for first in range(0, NZ, 4):
        ks = range(first, first + 4)
        total = split_dot(stack_rows([pair_rows(firstm, k, 8, 24) for k in ks]), main_matrix)
        total = total + split_dot(stack_rows([pair_rows(firsth, k, 8, 24) for k in ks]), side_matrix)
        for n, k in enumerate(ks):
            f1[k, pl.ds(4, 24), :] = total[n * 24 : (n + 1) * 24]
        total = split_dot(stack_rows([pair_rows(rm, k, 0, 32) for k in ks]), main_matrix)
        total = total + split_dot(stack_rows([pair_rows(rh, k, 0, 32) for k in ks]), side_matrix)
        for n, k in enumerate(ks):
            rho1[k, :, :] = total[n * 32 : (n + 1) * 32]

    middle = Level(1, [rho1], [ax1], [ay1], [d1], [e1], [g1])
    inside = inside_of(1, ix, iy, (grid_rows // 2, grid_lanes // 2, 16, 64))
    middle.faces([(4, 24), (21, 8)])
    middle.factor_and_first([(4, 24)], inside, [f1], [first1])
    middle.relax([(4, 24)], [f1], [first1], [v1], u=[u1])
    middle.residual([(8, 16)], [f1], [u1], [res1])

    pack_matrix = one_hot(
        4 * LANES,
        lambda s, t: jnp.logical_and(
            (s % LANES) // 2 - 16 + 32 * (s // LANES) == t,
            jnp.logical_and(s % LANES >= 32, s % LANES < 96),
        ),
        0.25,
    )
    blocks = []
    for ref in (res1, rho1):
        for group in range(4):
            blocks.append(jnp.concatenate([pair_rows(ref, 4 * group + q, 8, 8) for q in range(4)], axis=1))
    packed = split_dot(stack_rows(blocks), pack_matrix)
    for n in range(8):
        pack_ref[n, :, :] = packed[n * 8 : (n + 1) * 8]


def coarser_kernel(
    grid, index_ref, own_ref, from_left_ref, from_right_ref,
    pack_ref, f2, v2, ax2, ay2, d2, e2, g2, f3, v3, ax3, ay3, d3, e3, g3,
    rho2, first2, u2, res2, rho3, first3, u3, res3,
):
    ix, iy = index_ref[0], index_ref[1]
    grid_rows, grid_lanes = grid
    lane = lanes_of()
    inside = inside_of(2, ix, iy, (grid_rows // 4, grid_lanes // 4, 8, 32))

    unpack = [
        one_hot(
            LANES,
            lambda s, t: jnp.logical_and(t % LANES < 64, (t % LANES + 64 * (t // LANES) + odd * 32) % LANES == s),
            1.0,
            2 * LANES,
        )
        for odd in range(2)
    ]
    good = inside(0, 40, 0)
    for field, target in enumerate((f2, rho2)):
        for group in range(4):
            own = pltpu.roll(own_ref[field * 4 + group], 16, 1)
            left = pltpu.roll(from_left_ref[field * 4 + group], LANES - 16, 1)
            right = pltpu.roll(from_right_ref[field * 4 + group], 48, 1)
            for odd in range(2):
                place = (lanes_of((40, LANES)) + 32 * odd) % 64
                merged = jnp.where(place < 16, left, jnp.where(place < 48, own, right))
                wide = split_dot(merged, unpack[odd], 3)
                for n in range(2):
                    y = wide[:, n * LANES : (n + 1) * LANES]
                    if field == 1:
                        y = jnp.where(good, y, 0.0)
                    target[4 * group + 2 * n + odd, :, :] = y

    level2 = Level(2, [rho2], [ax2], [ay2], [d2], [e2], [g2])
    level2.faces([(4, 16, 2), (29, 8)])
    level2.factor_and_first([(4, 16, 2)], inside, [f2], [first2])
    level2.relax([(4, 16, 2)], [f2], [first2], [v2], u=[u2])
    level2.residual([(4, 16, 2)], [f2], [u2], [res2])

    halve = one_hot(LANES, lambda s, t: s // 2 == t, 0.25)
    for ref, target, first, count in ((res2, f3, 4, 16), (rho2, rho3, 4, 16)):
        total = split_dot(stack_rows([pair_rows(ref, k, first, count) for k in range(NZ)]), halve)
        for k in range(NZ):
            target[k, pl.ds(first // 2, count), :] = total[k * count : (k + 1) * count]

    level3 = Level(3, [rho3], [ax3], [ay3], [d3], [e3], [g3])
    inside = inside_of(3, ix, iy, (grid_rows // 8, grid_lanes // 8, 4, 16))
    level3.faces([(2, 16)])
    level3.factor_and_first([(2, 16)], inside, [f3], [first3])
    level3.relax([(2, 16)], [f3], [first3], [v3], u=[u3])
    level3.residual([(6, 8)], [f3], [u3], [res3])

    spread = one_hot(
        LANES,
        lambda s, t: jnp.logical_and(s // 2 - 4 == t % 8, jnp.logical_and(s >= 8, s < 24)),
        0.25,
    )
    for field, ref in enumerate((res3, rho3)):
        total = split_dot(stack_rows([pair_rows(ref, k, 8, 8) for k in range(NZ)]), spread)
        merged = total[0:8]
        for k in range(1, NZ):
            merged = jnp.where(lane // 8 == k, total[k * 8 : (k + 1) * 8], merged)
        pack_ref[pl.ds(2 * field, 2), :] = merged[0:2]


def prolong(coarse, first_row, count, ref, old, target, target_row, matrix):
    rows = stack_rows([coarse(k) for k in range(NZ)])
    for part in range(len(target)):
        fine = split_dot(rows, matrix[part])
        for k in range(NZ):
            x = fine[k * count : (k + 1) * count]
            for odd in range(2):
                where = pl.ds(target_row + odd, count, stride=2)
                target[part].at[k][where, :] = old[part].at[k][where, :] + x


def top_kernel(
    grid, tiles, index_ref, gathered, fm, fh, vm, vh, axm, axh, aym, ayh, dm, dh, em, eh, gm, gh,
    f1, v1, ax1, ay1, d1, e1, g1, f2, v2, ax2, ay2, d2, e2, g2, f3, v3, ax3, ay3, d3, e3, g3,
    out_ref,
    rho4, f4, ax4, ay4, d4, e4, g4, c4, a4, va4, vb4, va3, vb3, va2, vb2, va1, vb1, vam, vah, vbm, vbh,
):
    ix, iy = index_ref[0], index_ref[1]
    grid_rows, grid_lanes = grid
    lane = lanes_of()
    rows4 = grid_rows // 16
    tiles_x, tiles_y = tiles

    zero = jnp.zeros((8, LANES), jnp.float32)
    for ref in (rho4, va4, vb4):
        for k in range(NZ):
            ref[k, pl.ds(0, 8), :] = zero
            ref[k, pl.ds(8 + rows4, 8), :] = zero

    count = min(8, tiles_x)
    for field, target in enumerate((f4, rho4)):
        for r in range(2):
            for base in range(0, tiles_x, count):
                xs = [
                    gathered[pl.ds((base * tiles_y + t) * 4 + field * 2 + r, count, stride=4 * tiles_y), :]
                    for t in range(16)
                ]
                column = lax.broadcasted_iota(jnp.int32, (count, LANES), 1) // 8
                for bit in (1, 2, 4, 8):
                    high = (column & bit) != 0
                    for i in range(16):
                        if i & bit:
                            continue
                        a, b = xs[i], xs[i | bit]
                        xs[i] = jnp.where(high, pltpu.roll(b, 8 * bit, 1), a)
                        xs[i | bit] = jnp.where(high, b, pltpu.roll(a, LANES - 8 * bit, 1))
                for k in range(NZ):
                    target.at[k][pl.ds(8 + 2 * base + r, count, stride=2), :] = xs[k]

    scale = spacing(4)
    h = min(16, rows4)
    first_lane, last_lane = lanes_of((h, LANES)) == 0, lanes_of((h, LANES)) == LANES - 1
    starts = list(range(8, 8 + rows4, h))

    def faces_x(r, h):
        for k in range(NZ):
            total = rho4[k, pl.ds(r, h), :] + rho4[k, pl.ds(r - 1, h), :]
            ax4[k, pl.ds(r, h), :] = scale * rcp(jnp.maximum(total, TINY))

    for r in starts:
        faces_x(r, h)
    faces_x(rows4 + 1, 8)

    def first_sweep(r):
        rho = rho4[0, pl.ds(r, h), :]
        upper = (2.0 * VERTICAL) * rcp(rho)
        partial, ratio = [], None
        for k in range(NZ):
            here = rho4[k, pl.ds(r, h), :]
            left = jnp.where(first_lane, 0.0, pltpu.roll(here, 1, 1))
            ay = scale * rcp(here + left)
            right = jnp.where(last_lane, scale * rcp(here), pltpu.roll(ay, LANES - 1, 1))
            ay4[k, pl.ds(r, h), :] = jnp.where(first_lane, 0.0, ay)
            center = ax4[k, pl.ds(r, h), :] + ax4[k, pl.ds(r + 1, h), :] + ay + right + upper
            if k + 1 < NZ:
                lower = (2.0 * VERTICAL) * rcp(here + rho4[k + 1, pl.ds(r, h), :])
                center = center + lower
            c4[k, pl.ds(r, h), :] = center
            a4[k, pl.ds(r, h), :] = upper
            pivot = center if k == 0 else center - upper * ratio
            inverse = rcp(pivot)
            scaled = 0.8 * inverse
            d4[k, pl.ds(r, h), :] = scaled
            value = scaled * f4[k, pl.ds(r, h), :]
            if k > 0:
                weight = upper * inverse
                e4[k, pl.ds(r, h), :] = weight
                value = value + weight * partial[-1]
            partial.append(value)
            if k + 1 < NZ:
                ratio = lower * inverse
                g4[k, pl.ds(r, h), :] = ratio
                upper = lower
        w = partial[-1]
        va4[NZ - 1, pl.ds(r, h), :] = w
        for k in range(NZ - 2, -1, -1):
            w = partial[k] + g4[k, pl.ds(r, h), :] * w
            va4[k, pl.ds(r, h), :] = w

    for r in starts:
        first_sweep(r)

    def pulled4(v, k, r):
        here = v[k, pl.ds(r, h), :]
        ay = ay4[k, pl.ds(r, h), :]
        return (
            f4[k, pl.ds(r, h), :]
            + ax4[k, pl.ds(r, h), :] * v[k, pl.ds(r - 1, h), :]
            + ax4[k, pl.ds(r + 1, h), :] * v[k, pl.ds(r + 1, h), :]
            + ay * pltpu.roll(here, 1, 1)
            + pltpu.roll(ay * here, LANES - 1, 1)
        )

    def sweep(v, out):
        for r in starts:
            partial = []
            for k in range(NZ):
                value = d4[k, pl.ds(r, h), :] * pulled4(v, k, r)
                if k > 0:
                    value = value + e4[k, pl.ds(r, h), :] * partial[-1]
                partial.append(value)
            w = None
            for k in range(NZ - 1, -1, -1):
                w = partial[k] if w is None else partial[k] + g4[k, pl.ds(r, h), :] * w
                out[k, pl.ds(r, h), :] = 0.2 * v[k, pl.ds(r, h), :] + w

    ends = [va4, vb4]
    for number in range(SWEEPS - 1):
        sweep(ends[number % 2], ends[(number + 1) % 2])
    final = ends[(SWEEPS - 1) % 2]
    shifts = []
    for k in range(NZ):
        left_over, weights = None, None
        for r in starts:
            center = c4[k, pl.ds(r, h), :]
            part = pulled4(final, k, r) - center * final[k, pl.ds(r, h), :]
            if k > 0:
                part = part + a4[k, pl.ds(r, h), :] * final[k - 1, pl.ds(r, h), :]
            if k + 1 < NZ:
                part = part + a4[k + 1, pl.ds(r, h), :] * final[k + 1, pl.ds(r, h), :]
            left_over = part if left_over is None else left_over + part
            weights = center if weights is None else weights + center
        raised = jnp.sum(left_over, axis=(0, 1), keepdims=True)
        shifts.append(raised / jnp.sum(weights, axis=(0, 1), keepdims=True))

    row = rows_of() + (ix * 2 - 4)
    column = lane + (iy * 8 - 4)
    good = jnp.logical_and(
        jnp.logical_and(row >= 0, row < rows4),
        jnp.logical_and(jnp.logical_and(column >= 0, column < grid_lanes // 16), lane < 16),
    )
    amount = lax.rem(132 - iy * 8, LANES)

    def coarsest(k):
        x = final[k, pl.ds(4 + 2 * ix, 8), :] + shifts[k]
        return jnp.where(good, pltpu.roll(x, amount, 1), 0.0)

    repeat = one_hot(LANES, lambda s, t: s == t // 2, 1.0)
    prolong(coarsest, 0, 8, None, [v3], [va3], 0, [repeat])
    level3 = Level(3, None, [ax3], [ay3], [d3], [e3], [g3])
    level3.relax([(2, 16)], [f3], [va3], [vb3])
    level3.relax([(6, 8)], [f3], [vb3], [va3])

    prolong(lambda k: va3[k, pl.ds(6, 8), :], 0, 8, None, [v2], [va2], 12, [repeat])
    level2 = Level(2, None, [ax2], [ay2], [d2], [e2], [g2])
    level2.relax([(12, 16)], [f2], [va2], [vb2])
    level2.relax([(12, 16)], [f2], [vb2], [va2])

    prolong(lambda k: va2[k, pl.ds(12, 16), :], 0, 16, None, [v1], [va1], 0, [repeat])
    level1 = Level(1, None, [ax1], [ay1], [d1], [e1], [g1])
    level1.relax([(4, 24)], [f1], [va1], [vb1])
    level1.relax([(4, 24)], [f1], [vb1], [va1])

    to_main = one_hot(LANES, lambda s, t: s == t // 2 + 32, 1.0)
    to_side = one_hot(
        LANES,
        lambda s, t: jnp.logical_or(
            jnp.logical_and(t < 64, s == t // 2 + 96), jnp.logical_and(t >= 64, s == t // 2 - 32)
        ),
        1.0,
    )
    prolong(lambda k: va1[k, pl.ds(4, 24), :], 0, 24, None, [vm, vh], [vam, vah], 8, [to_main, to_side])
    fine = Level(0, None, [axm, axh], [aym, ayh], [dm, dh], [em, eh], [gm, gh])
    fine.relax([(15, 16, 2), (41, 8)], [fm, fh], [vam, vah], [vbm, vbh])
    fine.relax([(16, 16, 2)], [fm, fh], [vbm, vbh], [out_ref], wanted=[0], shift=16)


def ring(x, axis, step):
    size = lax.axis_size(axis)
    return lax.ppermute(x, axis, [(i, (i + step) % size) for i in range(size)])


def gather(x, axis):
    size = lax.axis_size(axis)
    blocks = jnp.broadcast_to(x[None], (size,) + x.shape)
    return lax.all_to_all(blocks, axis, 0, 0).reshape(size * x.shape[0], LANES)


def array(*shape):
    return jax.ShapeDtypeStruct(shape, jnp.float32)


def call(kernel, name, outs, scratch, index, *operands):
    vmem = pl.BlockSpec(memory_space=pltpu.VMEM)
    ins = [vmem] * len(operands)
    if index is not None:
        ins, operands = [pl.BlockSpec(memory_space=pltpu.SMEM)] + ins, (index,) + operands
    return pl.pallas_call(
        kernel,
        out_shape=outs,
        in_specs=ins,
        out_specs=[vmem] * len(outs),
        scratch_shapes=[pltpu.VMEM(shape, jnp.float32) for shape in scratch],
        compiler_params=pltpu.CompilerParams(vmem_limit_bytes=VMEM_BYTES),
        name=name,
    )(*operands)


def solution(mesh):
    tiles_x, tiles_y = mesh.shape["gx"], mesh.shape["gy"]
    grid = (32 * tiles_x, 128 * tiles_y)
    big = [array(NZ, ROWS[level], LANES) for level in range(4)]

    def on_device(source, rho):
        index = jnp.stack([lax.axis_index("gx"), lax.axis_index("gy")]).astype(jnp.int32)

        lows = jnp.concatenate([source[:, :16], rho[:, :16]], axis=0)
        highs = jnp.concatenate([source[:, 16:], rho[:, 16:]], axis=0)
        up = ring(highs, "gx", 1)
        dn = ring(lows, "gx", -1)
        strip = array(4, ROWS[0], LANES)
        lefts, rights = call(edges_kernel, "edges", [strip, strip], [], None, source, rho, up, dn)
        from_left_strip = ring(rights, "gy", 1)
        from_right_strip = ring(lefts, "gy", -1)

        s0, s1, s2, s3 = [x.shape for x in big]
        fine = call(
            lambda *refs: fine_kernel(grid, *refs),
            "fine",
            [array(8, 8, LANES)] + [big[0]] * 14 + [big[1]] * 7,
            [s0] * 6 + [s1] * 4,
            index, source, rho, up, dn, from_left_strip, from_right_strip,
        )
        tile = fine[0]
        pieces = [ring(tile, "gx", 2), ring(tile, "gx", 1), tile, ring(tile, "gx", -1), ring(tile, "gx", -2)]
        column = jnp.concatenate(pieces, axis=1)
        from_left_column = ring(column, "gy", 1)
        from_right_column = ring(column, "gy", -1)
        coarser = call(
            lambda *refs: coarser_kernel(grid, *refs),
            "coarser",
            [array(4, LANES)] + [big[2]] * 7 + [big[3]] * 7,
            [s2] * 4 + [s3] * 4,
            index, column, from_left_column, from_right_column,
        )
        gathered = gather(gather(coarser[0], "gy"), "gx")

        s4 = (NZ, 16 + 2 * tiles_x, LANES)
        (pressure,) = call(
            lambda *refs: top_kernel(grid, (tiles_x, tiles_y), *refs),
            "top",
            [array(NZ, 32, LANES)],
            [s4] * 11 + [s3] * 2 + [s2] * 2 + [s1] * 2 + [s0] * 4,
            index, gathered, *fine[1:], *coarser[1:],
        )
        return pressure

    return jax.shard_map(
        on_device,
        mesh=mesh,
        in_specs=(P(None, "gx", "gy"), P(None, "gx", "gy")),
        out_specs=P(None, "gx", "gy"),
        check_vma=False,
    )
```

time: 103 us -> 91.1 us (0.88)
  Pallas kernels: 25.9 us -> 18.7 us
  local copies, waits for them, and re-layouts: 5.24 us -> 1.21 us
  blocking collectives: 33.6 us -> 32.5 us
    pallas_call x4, Pallas kernels: 25.9 us -> 18.7 us  [call(): pl.pallas_call(kernel, out_shape=outs, in_specs=ins, out_specs=[vmem] * l...]
    unnamed x18 -> x8, local copies, waits for them, and re-layouts: 4.04 us -> 0.02 us
    all_to_all x1 -> x2, blocking collectives: 33.6 us -> 32.5 us  [gather(): return lax.all_to_all(blocks, axis, 0, 0).reshape(size * x.shape[0], LANES)]
where the time goes in v1:
time: 91.1 us; the launch traced here: 90.9 us
  blocking collectives  32.5 us (36%)
  starting transfers between devices  21.4 us (23%)
  Pallas kernels  18.7 us (21%)
  waiting for transfers between devices  16.9 us (19%)
  local copies, waits for them, and re-layouts  1.21 us (1%)
    all_to_all x2, blocking collectives, gather(): return lax.all_to_all(blocks, axis, 0, 0).reshape(size * x.shape[0], LANES)  32.5 us
    ppermute x10, starting transfers between devices, ring(): return lax.ppermute(x, axis, [(i, (i + step) % size) for i in range(size)])  21.4 us
    pallas_call x4, Pallas kernels, call(): pl.pallas_call(kernel, out_shape=outs, in_specs=ins, out_specs=[vmem] * l...  18.7 us
    ppermute x10, waiting for transfers between devices, ring(): return lax.ppermute(x, axis, [(i, (i + step) % size) for i in range(size)])  16.9 us
  transfers between devices with their start and end apart: 10, of which 6 were waited for; matrix products, arithmetic and copies ran while one was open for 0% of the time, Pallas kernels for 0%

profile of v1, /device:TPU:1, one launch (start us, length us, event | category | flops | bytes accessed | tf_op | source)
XLA Modules:
  0.0 90.9 jit_solution(16086800306750995267)
XLA Ops:
  0.0 1.1 %fusion = (f32[16,16,128]{2,1,0:T(8,128)S(1)}, f32[16,16,128]{2,1,0:T(8,128)S(1)}, f32[16,16,128]{2,1,0:T(8,128)S(1)}, f32[16,16,128]{2,1,0:T(8,128)S(1)}) fusion(f32[16,32,128]{2,1,0:T(8,128)} %refs_1_.1, f32[16,32,128]{2,1,0:T(8,128)} %refs_2_.1), kind=kLoop, calls=%fused_computation.8 | loop fusion | bytes 1048576 | tf_op jit(solution)/shard_map/slice | solution.py:632
  1.2 2.1 %collective-permute-start = (f32[32,16,128]{2,1,0:T(8,128)S(1)}, f32[32,16,128]{2,1,0:T(8,128)S(1)}, u32[]{:S(2)}, u32[]{:S(2)}) collective-permute-start(f32[32,16,128]{2,1,0:T(8,128)S(1)} %pad_maximum_fusion), channel_id=1, source_target_pairs={{0,16},{16,32},{32,48},{48,64},{64,80},{80,96},{96,112},{112,128},... | collective-permute-start | bytes 786440 | tf_op jit(solution)/shard_map/ppermute | solution.py:595
  3.3 0.0 copy-start
  3.3 0.0 copy-start.1
  3.3 3.8 %collective-permute-start.1 = (f32[32,16,128]{2,1,0:T(8,128)S(1)}, f32[32,16,128]{2,1,0:T(8,128)S(1)}, u32[]{:S(2)}, u32[]{:S(2)}) collective-permute-start(f32[32,16,128]{2,1,0:T(8,128)S(1)} %pad_maximum_fusion.1), channel_id=1, source_target_pairs={{0,240},{16,0},{32,16},{48,32},{64,48},{80,64},{96,80},{112,96},{1... | collective-permute-start | bytes 786440 | tf_op jit(solution)/shard_map/ppermute | solution.py:595
  7.1 3.9 %collective-permute-done.up_ref.refs_3_ = f32[32,16,128]{2,1,0:T(8,128)S(1)} collective-permute-done((f32[32,16,128]{2,1,0:T(8,128)S(1)}, f32[32,16,128]{2,1,0:T(8,128)S(1)}, u32[]{:S(2)}, u32[]{:S(2)}) %collective-permute-start) | collective-permute-done | bytes 262176 | tf_op jit(solution)/shard_map/ppermute | solution.py:595
  11.1 0.0 collective-permute-done.1.dn_ref.refs_4_
  11.1 0.0 copy-done
  11.1 0.0 copy-done.1
  11.1 0.5 edges.1
  11.6 4.7 %collective-permute-start.2 = (f32[4,64,128]{2,1,0:T(8,128)S(1)}, f32[4,64,128]{2,1,0:T(8,128)S(1)}, u32[]{:S(2)}, u32[]{:S(2)}) collective-permute-start(f32[4,64,128]{2,1,0:T(8,128)S(1)} %get-tuple-element.44), channel_id=1, source_target_pairs={{0,1},{1,2},{2,3},{3,4},{4,5},{5,6},{6,7},{7,8},{8,9},{9,10},{10,1... | collective-permute-start | bytes 393224 | tf_op jit(solution)/shard_map/ppermute | solution.py:595
  16.4 0.0 collective-permute-start.3
  16.4 0.1 pad_add_fusion.refs_0_
  16.4 1.9 %collective-permute-done.2.refs_5_ = f32[4,64,128]{2,1,0:T(8,128)S(1)} collective-permute-done((f32[4,64,128]{2,1,0:T(8,128)S(1)}, f32[4,64,128]{2,1,0:T(8,128)S(1)}, u32[]{:S(2)}, u32[]{:S(2)}) %collective-permute-start.2) | collective-permute-done | bytes 131104 | tf_op jit(solution)/shard_map/ppermute | solution.py:595
  18.3 2.7 %collective-permute-done.3.refs_6_ = f32[4,64,128]{2,1,0:T(8,128)S(1)} collective-permute-done((f32[4,64,128]{2,1,0:T(8,128)S(1)}, f32[4,64,128]{2,1,0:T(8,128)S(1)}, u32[]{:S(2)}, u32[]{:S(2)}) %collective-permute-start.3) | collective-permute-done | bytes 131104 | tf_op jit(solution)/shard_map/ppermute | solution.py:595
  21.0 7.1 %fine.1 = (f32[8,8,128]{2,1,0:T(8,128)S(1)}, f32[16,64,128]{2,1,0:T(8,128)S(1)}, f32[16,64,128]{2,1,0:T(8,128)S(1)}, f32[16,64,128]{2,1,0:T(8,128)S(1)}, f32[16,...) custom-call(s32[2]{0:T(128)S(1)} %pad_add_fusion.refs_0_, ...), custom_call_target="tpu_custom_call" | custom-call | tf_op jit(solution)/shard_map/fine/pallas_call | solution.py:613
  28.2 0.4 collective-permute-start.4
  28.5 4.8 %collective-permute-start.7 = (f32[8,8,128]{2,1,0:T(8,128)S(1)}, f32[8,8,128]{2,1,0:T(8,128)S(1)}, u32[]{:S(2)}, u32[]{:S(2)}) collective-permute-start(f32[8,8,128]{2,1,0:T(8,128)S(1)} %get-tuple-element.46), channel_id=1, source_target_pairs={{0,224},{16,240},{32,0},{48,16},{64,32},{80,48},{96,64},{112,80},{... | collective-permute-start | bytes 98312 | tf_op jit(solution)/shard_map/ppermute | solution.py:595
  33.3 2.8 %collective-permute-start.6 = (f32[8,8,128]{2,1,0:T(8,128)S(1)}, f32[8,8,128]{2,1,0:T(8,128)S(1)}, u32[]{:S(2)}, u32[]{:S(2)}) collective-permute-start(f32[8,8,128]{2,1,0:T(8,128)S(1)} %get-tuple-element.46), channel_id=1, source_target_pairs={{0,240},{16,0},{32,16},{48,32},{64,48},{80,64},{96,80},{112,96},{1... | collective-permute-start | bytes 98312 | tf_op jit(solution)/shard_map/ppermute | solution.py:595
  36.1 0.0 collective-permute-start.5
  36.1 0.0 collective-permute-done.4
  36.1 6.1 %collective-permute-done.5 = f32[8,8,128]{2,1,0:T(8,128)S(1)} collective-permute-done((f32[8,8,128]{2,1,0:T(8,128)S(1)}, f32[8,8,128]{2,1,0:T(8,128)S(1)}, u32[]{:S(2)}, u32[]{:S(2)}) %collective-permute-start.5) | collective-permute-done | bytes 32800 | tf_op jit(solution)/shard_map/ppermute | solution.py:595
  42.2 0.0 collective-permute-done.6
  42.2 0.0 collective-permute-done.7
  42.3 2.8 %collective-permute-start.9 = (f32[8,40,128]{2,1,0:T(8,128)S(1)}, f32[8,40,128]{2,1,0:T(8,128)S(1)}, u32[]{:S(2)}, u32[]{:S(2)}) collective-permute-start(f32[8,40,128]{2,1,0:T(8,128)S(1)} %constant_dynamic-update-slice_fusion.refs_1_), channel_id=1, source_target_pairs={{0,15},{1,0},{2,1},{3,2},{4,3},{5,4},{6,5},{7,6},{8,7},{9,8},{10,9... | collective-permute-start | bytes 491528 | tf_op jit(solution)/shard_map/ppermute | solution.py:595
  45.0 0.0 collective-permute-start.8
  45.0 2.1 %collective-permute-done.9.refs_3_ = f32[8,40,128]{2,1,0:T(8,128)S(1)} collective-permute-done((f32[8,40,128]{2,1,0:T(8,128)S(1)}, f32[8,40,128]{2,1,0:T(8,128)S(1)}, u32[]{:S(2)}, u32[]{:S(2)}) %collective-permute-start.9) | collective-permute-done | bytes 163872 | tf_op jit(solution)/shard_map/ppermute | solution.py:595
  47.1 0.2 collective-permute-done.8.refs_2_
  47.3 3.7 %coarser.1 = (f32[4,128]{1,0:T(4,128)S(1)}, f32[16,40,128]{2,1,0:T(8,128)S(1)}, f32[16,40,128]{2,1,0:T(8,128)S(1)}, f32[16,40,128]{2,1,0:T(8,128)S(1)}, f32[16,4...) custom-call(s32[2]{0:T(128)S(1)} %pad_add_fusion.refs_0_, ...), custom_call_target="tpu_custom_call" | custom-call | tf_op jit(solution)/shard_map/coarser/pallas_call | solution.py:613
  51.0 19.0 %all_to_all.10 = f32[16,4,128]{2,1,0:T(4,128)S(1)} all-to-all(f32[16,4,128]{2,1,0:T(4,128)S(1)} %broadcast_in_dim.6), channel_id=1, replica_groups=mesh['gx'=16,'gy'=16] {'gy'}, dimensions={0} | all-to-all | bytes 65536 | tf_op jit(solution)/shard_map/all_to_all | solution.py:601
  70.0 13.6 %all_to_all.11 = f32[16,64,128]{2,1,0:T(8,128)S(1)} all-to-all(f32[16,64,128]{2,1,0:T(8,128)S(1)} %broadcast_in_dim.15), channel_id=1, replica_groups=mesh['gx'=16,'gy'=16] {'gx'}, dimensions={0} | all-to-all | bytes 1048576 | tf_op jit(solution)/shard_map/all_to_all | solution.py:601
  83.6 7.3 %top.1 = f32[16,32,128]{2,1,0:T(8,128)} custom-call(s32[2]{0:T(128)S(1)} %pad_add_fusion.refs_0_, f32[1024,128]{1,0:T(8,128)S(1)} %bitcast.4, f32[16,64,128]{2,1,0:T(8,128)S(1)} %get-tuple-element.48.refs_2_, f32[16,64,128]{2,1,0:T(8,128)S(1)} %get-tuple-element.49.refs_3_, f32[16,64,128]{2,1,0:T(8,128)S(1)} %get-tuple-element.50.refs_4_, ...), custom_call_target="tpu_custom_call" | custom-call | tf_op jit(solution)/shard_map/top/pallas_call | solution.py:613
  (9 shorter events, 0.1 us)
Async XLA Ops:
  1.2 9.9 %collective-permute-start = (f32[32,16,128]{2,1,0:T(8,128)S(1)}, f32[32,16,128]{2,1,0:T(8,128)S(1)}, u32[]{:S(2)}, u32[]{:S(2)}) collective-permute-start(f32[32,16,128]{2,1,0:T(8,128)S(1)} %pad_maximum_fusion), channel_id=1, source_target_pairs={{0,16},{16,32},{32,48},{48,64},{64,80},{80,96},{96,112},{112,128},... | collective-permute-start | bytes 786440 | tf_op jit(solution)/shard_map/ppermute | solution.py:595
  3.3 7.8 %copy-start = (f32[16,32,128]{2,1,0:T(8,128)S(1)}, f32[16,32,128]{2,1,0:T(8,128)}, u32[]{:S(2)}) copy-start(f32[16,32,128]{2,1,0:T(8,128)} %refs_1_.1) | copy-start | bytes 786436
  3.3 7.8 %copy-start.1 = (f32[16,32,128]{2,1,0:T(8,128)S(1)}, f32[16,32,128]{2,1,0:T(8,128)}, u32[]{:S(2)}) copy-start(f32[16,32,128]{2,1,0:T(8,128)} %refs_2_.1) | copy-start | bytes 786436
  3.3 7.8 %collective-permute-start.1 = (f32[32,16,128]{2,1,0:T(8,128)S(1)}, f32[32,16,128]{2,1,0:T(8,128)S(1)}, u32[]{:S(2)}, u32[]{:S(2)}) collective-permute-start(f32[32,16,128]{2,1,0:T(8,128)S(1)} %pad_maximum_fusion.1), channel_id=1, source_target_pairs={{0,240},{16,0},{32,16},{48,32},{64,48},{80,64},{96,80},{112,96},{1... | collective-permute-start | bytes 786440 | tf_op jit(solution)/shard_map/ppermute | solution.py:595
  11.6 6.7 %collective-permute-start.2 = (f32[4,64,128]{2,1,0:T(8,128)S(1)}, f32[4,64,128]{2,1,0:T(8,128)S(1)}, u32[]{:S(2)}, u32[]{:S(2)}) collective-permute-start(f32[4,64,128]{2,1,0:T(8,128)S(1)} %get-tuple-element.44), channel_id=1, source_target_pairs={{0,1},{1,2},{2,3},{3,4},{4,5},{5,6},{6,7},{7,8},{8,9},{9,10},{10,1... | collective-permute-start | bytes 393224 | tf_op jit(solution)/shard_map/ppermute | solution.py:595
  16.4 4.7 %collective-permute-start.3 = (f32[4,64,128]{2,1,0:T(8,128)S(1)}, f32[4,64,128]{2,1,0:T(8,128)S(1)}, u32[]{:S(2)}, u32[]{:S(2)}) collective-permute-start(f32[4,64,128]{2,1,0:T(8,128)S(1)} %get-tuple-element.45), channel_id=1, source_target_pairs={{0,15},{1,0},{2,1},{3,2},{4,3},{5,4},{6,5},{7,6},{8,7},{9,8},{10,9... | collective-permute-start | bytes 393224 | tf_op jit(solution)/shard_map/ppermute | solution.py:595
  28.2 8.0 %collective-permute-start.4 = (f32[8,8,128]{2,1,0:T(8,128)S(1)}, f32[8,8,128]{2,1,0:T(8,128)S(1)}, u32[]{:S(2)}, u32[]{:S(2)}) collective-permute-start(f32[8,8,128]{2,1,0:T(8,128)S(1)} %get-tuple-element.46), channel_id=1, source_target_pairs={{0,32},{16,48},{32,64},{48,80},{64,96},{80,112},{96,128},{112,144}... | collective-permute-start | bytes 98312 | tf_op jit(solution)/shard_map/ppermute | solution.py:595
  28.5 13.7 %collective-permute-start.7 = (f32[8,8,128]{2,1,0:T(8,128)S(1)}, f32[8,8,128]{2,1,0:T(8,128)S(1)}, u32[]{:S(2)}, u32[]{:S(2)}) collective-permute-start(f32[8,8,128]{2,1,0:T(8,128)S(1)} %get-tuple-element.46), channel_id=1, source_target_pairs={{0,224},{16,240},{32,0},{48,16},{64,32},{80,48},{96,64},{112,80},{... | collective-permute-start | bytes 98312 | tf_op jit(solution)/shard_map/ppermute | solution.py:595
  33.3 8.9 %collective-permute-start.6 = (f32[8,8,128]{2,1,0:T(8,128)S(1)}, f32[8,8,128]{2,1,0:T(8,128)S(1)}, u32[]{:S(2)}, u32[]{:S(2)}) collective-permute-start(f32[8,8,128]{2,1,0:T(8,128)S(1)} %get-tuple-element.46), channel_id=1, source_target_pairs={{0,240},{16,0},{32,16},{48,32},{64,48},{80,64},{96,80},{112,96},{1... | collective-permute-start | bytes 98312 | tf_op jit(solution)/shard_map/ppermute | solution.py:595
  36.1 6.1 %collective-permute-start.5 = (f32[8,8,128]{2,1,0:T(8,128)S(1)}, f32[8,8,128]{2,1,0:T(8,128)S(1)}, u32[]{:S(2)}, u32[]{:S(2)}) collective-permute-start(f32[8,8,128]{2,1,0:T(8,128)S(1)} %get-tuple-element.46), channel_id=1, source_target_pairs={{0,16},{16,32},{32,48},{48,64},{64,80},{80,96},{96,112},{112,128},... | collective-permute-start | bytes 98312 | tf_op jit(solution)/shard_map/ppermute | solution.py:595
  42.3 4.8 %collective-permute-start.9 = (f32[8,40,128]{2,1,0:T(8,128)S(1)}, f32[8,40,128]{2,1,0:T(8,128)S(1)}, u32[]{:S(2)}, u32[]{:S(2)}) collective-permute-start(f32[8,40,128]{2,1,0:T(8,128)S(1)} %constant_dynamic-update-slice_fusion.refs_1_), channel_id=1, source_target_pairs={{0,15},{1,0},{2,1},{3,2},{4,3},{5,4},{6,5},{7,6},{8,7},{9,8},{10,9... | collective-permute-start | bytes 491528 | tf_op jit(solution)/shard_map/ppermute | solution.py:595
  45.0 2.3 %collective-permute-start.8 = (f32[8,40,128]{2,1,0:T(8,128)S(1)}, f32[8,40,128]{2,1,0:T(8,128)S(1)}, u32[]{:S(2)}, u32[]{:S(2)}) collective-permute-start(f32[8,40,128]{2,1,0:T(8,128)S(1)} %constant_dynamic-update-slice_fusion.refs_1_), channel_id=1, source_target_pairs={{0,1},{1,2},{2,3},{3,4},{4,5},{5,6},{6,7},{7,8},{8,9},{9,10},{10,1... | collective-permute-start | bytes 491528 | tf_op jit(solution)/shard_map/ppermute | solution.py:595

commit v2 on v1

--- a/solution.py
+++ b/solution.py
@@ -225,27 +225,33 @@
     return jnp.concatenate(blocks, axis=0)
 
 
+PIECES = ((5, 8, "up", 0), (8, 8, "up", 3), (16, 32, "own", 0), (48, 8, "down", 0), (51, 8, "down", 3))
+REACH = 11
+
+
+def piece_of(piece, field, k, own, up, down):
+    first, count, source, start = piece
+    if source == "own":
+        return own[k, :, :]
+    ref = up if source == "up" else down
+    return ref[pl.ds(start * 2 * NZ + field * NZ + k, count, stride=2 * NZ), :]
+
+
 def edges_kernel(f_ref, rho_ref, up_ref, dn_ref, left_ref, right_ref):
-    lane = lanes_of()
-    slot = lane // 16
     for field, own in enumerate((f_ref, rho_ref)):
-        for block in range(8):
+        for piece in PIECES:
+            first, count = piece[:2]
+            slot = lanes_of((count, LANES)) // 16
             for half in range(2):
                 lefts, rights = None, None
                 for q in range(8):
-                    k = half * 8 + q
-                    if block < 2:
-                        x = up_ref[field * NZ + k, pl.ds(block * 8, 8), :]
-                    elif block < 6:
-                        x = own[k, pl.ds(block * 8 - 16, 8), :]
-                    else:
-                        x = dn_ref[field * NZ + k, pl.ds(block * 8 - 48, 8), :]
+                    x = piece_of(piece, field, half * 8 + q, own, up_ref, dn_ref)
                     a = x if q == 0 else pltpu.roll(x, 16 * q, 1)
                     b = pltpu.roll(x, 16 * q + 16, 1) if q < 7 else x
                     lefts = a if q == 0 else jnp.where(slot == q, a, lefts)
                     rights = b if q == 0 else jnp.where(slot == q, b, rights)
-                left_ref[field * 2 + half, pl.ds(block * 8, 8), :] = lefts
-                right_ref[field * 2 + half, pl.ds(block * 8, 8), :] = rights
+                left_ref[field * 2 + half, pl.ds(first, count), :] = lefts
+                right_ref[field * 2 + half, pl.ds(first, count), :] = rights
 
 
 def fine_kernel(
@@ -257,35 +263,27 @@
     grid_rows, grid_lanes = grid
     inside = inside_of(0, ix, iy, (grid_rows, grid_lanes, 32, 128))
 
-    unpack = one_hot(
-        2 * LANES,
-        lambda s, t: jnp.logical_or(
-            jnp.logical_and(s < LANES, (t // LANES) * 16 == s - t % LANES) & (t % LANES < 16),
-            jnp.logical_and(s >= LANES, (t // LANES) * 16 == s - t % LANES - 16) & (t % LANES >= 112),
-        ),
-        1.0,
-        8 * LANES,
-    )
     for field, (own, main, side) in enumerate(((f_ref, fm, fh), (rho_ref, rm, rh))):
         for k in range(NZ):
-            for first, count, source, shift in (
-                (0, 16, up_ref, 0),
-                (16, 32, own, -16),
-                (48, 16, dn_ref, -48),
-            ):
-                layer = k if source is own else field * NZ + k
-                x = source[layer, pl.ds(first + shift, count), :]
-                if field == 1 and source is not own:
+            for piece in PIECES:
+                first, count, source, _ = piece
+                x = piece_of(piece, field, k, own, up_ref, dn_ref)
+                if field == 1 and source != "own":
                     x = jnp.where(inside(first, count, 0), x, 0.0)
                 main[k, pl.ds(first, count), :] = x
-        for half in range(2):
-            strips = jnp.concatenate([from_right_ref[field * 2 + half], from_left_ref[field * 2 + half]], axis=1)
-            wide = split_dot(strips, unpack, 3)
-            for q in range(8):
-                y = wide[:, q * LANES : (q + 1) * LANES]
-                if field == 1:
-                    y = jnp.where(inside(0, 64, 1), y, 0.0)
-                side[half * 8 + q, :, :] = y
+        for first in (5, 16, 32, 43):
+            slot = lanes_of((16, LANES)) // 16
+            good = inside(first, 16, 1)
+            for half in range(2):
+                right = from_right_ref[field * 2 + half, pl.ds(first, 16), :]
+                left = pltpu.roll(from_left_ref[field * 2 + half, pl.ds(first, 16), :], LANES - 16, 1)
+                merged = [jnp.where(slot % 2 == odd, right, left) for odd in range(2)]
+                for q in range(8):
+                    y = merged[q % 2]
+                    y = y if q == 0 else pltpu.roll(y, LANES - 16 * q, 1)
+                    if field == 1:
+                        y = jnp.where(good, y, 0.0)
+                    side[half * 8 + q, pl.ds(first, 16), :] = y
 
     fine = Level(0, [rm, rh], [axm, axh], [aym, ayh], [dm, dh], [em, eh], [gm, gh])
     fine.faces([(6, 16, 3), (51, 8)])
@@ -320,24 +318,28 @@
     middle.residual([(8, 16)], [f1], [u1], [res1])
 
     pack_matrix = one_hot(
-        4 * LANES,
+        LANES,
         lambda s, t: jnp.logical_and(
-            (s % LANES) // 2 - 16 + 32 * (s // LANES) == t,
-            jnp.logical_and(s % LANES >= 32, s % LANES < 96),
+            s // 2 - 16 == (t // LANES) * 16 + t % 16, jnp.logical_and(s >= 32, s < 96)
         ),
         0.25,
+        2 * LANES,
     )
-    blocks = []
-    for ref in (res1, rho1):
-        for group in range(4):
-            blocks.append(jnp.concatenate([pair_rows(ref, 4 * group + q, 8, 8) for q in range(4)], axis=1))
-    packed = split_dot(stack_rows(blocks), pack_matrix)
-    for n in range(8):
-        pack_ref[n, :, :] = packed[n * 8 : (n + 1) * 8]
+    slot = lanes_of() // 16
+    for field, ref in enumerate((res1, rho1)):
+        wide = split_dot(stack_rows([pair_rows(ref, k, 8, 8) for k in range(NZ)]), pack_matrix)
+        for side in range(2):
+            for half in range(2):
+                packed = None
+                for q in range(8):
+                    k = half * 8 + q
+                    x = wide[k * 8 : (k + 1) * 8, side * LANES : (side + 1) * LANES]
+                    packed = x if q == 0 else jnp.where(slot == q, x, packed)
+                pack_ref[side * 4 + field * 2 + half, :, :] = packed
 
 
 def coarser_kernel(
-    grid, index_ref, own_ref, from_left_ref, from_right_ref,
+    grid, index_ref, own_left_ref, own_right_ref, from_left_ref, from_right_ref,
     pack_ref, f2, v2, ax2, ay2, d2, e2, g2, f3, v3, ax3, ay3, d3, e3, g3,
     rho2, first2, u2, res2, rho3, first3, u3, res3,
 ):
@@ -346,30 +348,29 @@
     lane = lanes_of()
     inside = inside_of(2, ix, iy, (grid_rows // 4, grid_lanes // 4, 8, 32))
 
-    unpack = [
-        one_hot(
-            LANES,
-            lambda s, t: jnp.logical_and(t % LANES < 64, (t % LANES + 64 * (t // LANES) + odd * 32) % LANES == s),
-            1.0,
-            2 * LANES,
-        )
-        for odd in range(2)
-    ]
+    lane40 = lanes_of((40, LANES))
     good = inside(0, 40, 0)
     for field, target in enumerate((f2, rho2)):
-        for group in range(4):
-            own = pltpu.roll(own_ref[field * 4 + group], 16, 1)
-            left = pltpu.roll(from_left_ref[field * 4 + group], LANES - 16, 1)
-            right = pltpu.roll(from_right_ref[field * 4 + group], 48, 1)
-            for odd in range(2):
-                place = (lanes_of((40, LANES)) + 32 * odd) % 64
-                merged = jnp.where(place < 16, left, jnp.where(place < 48, own, right))
-                wide = split_dot(merged, unpack[odd], 3)
-                for n in range(2):
-                    y = wide[:, n * LANES : (n + 1) * LANES]
+        for half in range(2):
+            g = field * 2 + half
+            tiles = [
+                from_left_ref[g],
+                pltpu.roll(own_left_ref[g], 16, 1),
+                pltpu.roll(own_right_ref[g], 32, 1),
+                pltpu.roll(from_right_ref[g], 48, 1),
+            ]
+            for m in range(4):
+                place = (lane40 - 16 * m) % 64
+                merged = jnp.where(
+                    place < 32,
+                    jnp.where(place < 16, tiles[0], tiles[1]),
+                    jnp.where(place < 48, tiles[2], tiles[3]),
+                )
+                for q in (m, m + 4):
+                    y = merged if q == 0 else pltpu.roll(merged, LANES - 16 * q, 1)
                     if field == 1:
                         y = jnp.where(good, y, 0.0)
-                    target[4 * group + 2 * n + odd, :, :] = y
+                    target[half * 8 + q, :, :] = y
 
     level2 = Level(2, [rho2], [ax2], [ay2], [d2], [e2], [g2])
     level2.faces([(4, 16, 2), (29, 8)])
@@ -400,7 +401,7 @@
         merged = total[0:8]
         for k in range(1, NZ):
             merged = jnp.where(lane // 8 == k, total[k * 8 : (k + 1) * 8], merged)
-        pack_ref[pl.ds(2 * field, 2), :] = merged[0:2]
+        pack_ref[pl.ds(2 * field, 2), :] = pltpu.roll(merged, 8 * iy, 1)[0:2]
 
 
 def prolong(coarse, first_row, count, ref, old, target, target_row, matrix):
@@ -440,17 +441,14 @@
                     gathered[pl.ds((base * tiles_y + t) * 4 + field * 2 + r, count, stride=4 * tiles_y), :]
                     for t in range(16)
                 ]
-                column = lax.broadcasted_iota(jnp.int32, (count, LANES), 1) // 8
+                block = lanes_of((count, LANES)) // 8
                 for bit in (1, 2, 4, 8):
-                    high = (column & bit) != 0
-                    for i in range(16):
-                        if i & bit:
-                            continue
-                        a, b = xs[i], xs[i | bit]
-                        xs[i] = jnp.where(high, pltpu.roll(b, 8 * bit, 1), a)
-                        xs[i | bit] = jnp.where(high, b, pltpu.roll(a, LANES - 8 * bit, 1))
+                    moved = (block & bit) != 0
+                    xs = [jnp.where(moved, xs[(i + bit) % 16], xs[i]) for i in range(16)]
                 for k in range(NZ):
-                    target.at[k][pl.ds(8 + 2 * base + r, count, stride=2), :] = xs[k]
+                    x = xs[-k % 16]
+                    x = x if k == 0 else pltpu.roll(x, LANES - 8 * k, 1)
+                    target.at[k][pl.ds(8 + 2 * base + r, count, stride=2), :] = x
 
     scale = spacing(4)
     h = min(16, rows4)
@@ -629,8 +627,9 @@
     def on_device(source, rho):
         index = jnp.stack([lax.axis_index("gx"), lax.axis_index("gy")]).astype(jnp.int32)
 
-        lows = jnp.concatenate([source[:, :16], rho[:, :16]], axis=0)
-        highs = jnp.concatenate([source[:, 16:], rho[:, 16:]], axis=0)
+        both = jnp.concatenate([source, rho], axis=0).transpose(1, 0, 2)
+        lows = both[:REACH].reshape(REACH * 2 * NZ, LANES)
+        highs = both[-REACH:].reshape(REACH * 2 * NZ, LANES)
         up = ring(highs, "gx", 1)
         dn = ring(lows, "gx", -1)
         strip = array(4, ROWS[0], LANES)
@@ -648,15 +647,16 @@
         )
         tile = fine[0]
         pieces = [ring(tile, "gx", 2), ring(tile, "gx", 1), tile, ring(tile, "gx", -1), ring(tile, "gx", -2)]
-        column = jnp.concatenate(pieces, axis=1)
-        from_left_column = ring(column, "gy", 1)
-        from_right_column = ring(column, "gy", -1)
+        own_left = jnp.concatenate([piece[:4] for piece in pieces], axis=1)
+        own_right = jnp.concatenate([piece[4:] for piece in pieces], axis=1)
+        from_left_column = ring(own_right, "gy", 1)
+        from_right_column = ring(own_left, "gy", -1)
         coarser = call(
             lambda *refs: coarser_kernel(grid, *refs),
             "coarser",
             [array(4, LANES)] + [big[2]] * 7 + [big[3]] * 7,
             [s2] * 4 + [s3] * 4,
-            index, column, from_left_column, from_right_column,
+            index, own_left, own_right, from_left_column, from_right_column,
         )
         gathered = gather(gather(coarser[0], "gy"), "gx")
 

time: 91.1 us -> 87.3 us (0.958)
  blocking collectives: 32.5 us -> 30.3 us
  other arithmetic: 0.11 us -> 1.14 us
  local copies, waits for them, and re-layouts: 1.21 us -> 0.25 us
    all_to_all x2, blocking collectives: 32.5 us -> 30.3 us  [gather(): return lax.all_to_all(blocks, axis, 0, 0).reshape(size * x.shape[0], LANES)]
    transpose x0 -> x1, other arithmetic: none -> 1.06 us  [on_device(): both = jnp.concatenate([source, rho], axis=0).transpose(1, 0, 2)]
    slice x1 -> x3, local copies, waits for them, and re-layouts: 1.13 us -> 0.16 us  [the longest x2 0.1 us: on_device(): lows = both[:REACH].reshape(REACH * 2 * NZ, LANES)]
where the time goes in v2:
time: 87.3 us; the launch traced here: 87.1 us
  blocking collectives  30.3 us (35%)
  starting transfers between devices  20.8 us (24%)
  Pallas kernels  18.1 us (21%)
  waiting for transfers between devices  16.4 us (19%)
  other arithmetic  1.14 us (1%)
    all_to_all x2, blocking collectives, gather(): return lax.all_to_all(blocks, axis, 0, 0).reshape(size * x.shape[0], LANES)  30.3 us
    ppermute x10, starting transfers between devices, ring(): return lax.ppermute(x, axis, [(i, (i + step) % size) for i in range(size)])  20.8 us
    pallas_call x4, Pallas kernels, call(): pl.pallas_call(kernel, out_shape=outs, in_specs=ins, out_specs=[vmem] * l...  18.1 us
    ppermute x10, waiting for transfers between devices, ring(): return lax.ppermute(x, axis, [(i, (i + step) % size) for i in range(size)])  16.4 us
  transfers between devices with their start and end apart: 10, of which 6 were waited for; matrix products, arithmetic and copies ran while one was open for 0% of the time, Pallas kernels for 0%

profile of v2, /device:TPU:1, one launch (start us, length us, event | category | flops | bytes accessed | tf_op | source)
XLA Modules:
  0.0 87.1 jit_solution(7210606403735394711)
XLA Ops:
  0.0 1.1 %maximum_bitcast_fusion = f32[32,32,128]{2,0,1:T(8,128)S(1)} fusion(f32[16,32,128]{2,1,0:T(8,128)} %refs_2_.1, f32[16,32,128]{2,1,0:T(8,128)} %refs_1_.1), kind=kLoop, calls=%fused_computation | loop fusion | flops 131072 | bytes 1048576 | tf_op jit(solution)/shard_map/transpose | solution.py:630
  1.1 0.0 copy-start.1
  1.1 0.1 copy.3
  1.2 0.0 copy-start
  1.2 2.1 %collective-permute-start = (f32[352,128]{1,0:T(8,128)S(1)}, f32[352,128]{1,0:T(8,128)S(1)}, u32[]{:S(2)}, u32[]{:S(2)}) collective-permute-start(f32[352,128]{1,0:T(8,128)S(1)} %bitcast.9), channel_id=1, source_target_pairs={{0,16},{16,32},{32,48},{48,64},{64,80},{80,96},{96,112},{112,128},... | collective-permute-start | bytes 540680 | tf_op jit(solution)/shard_map/ppermute | solution.py:593
  3.3 0.1 copy.4
  3.4 3.8 %collective-permute-start.1 = (f32[352,128]{1,0:T(8,128)S(1)}, f32[352,128]{1,0:T(8,128)S(1)}, u32[]{:S(2)}, u32[]{:S(2)}) collective-permute-start(f32[352,128]{1,0:T(8,128)S(1)} %bitcast.10), channel_id=1, source_target_pairs={{0,240},{16,0},{32,16},{48,32},{64,48},{80,64},{96,80},{112,96},{1... | collective-permute-start | bytes 540680 | tf_op jit(solution)/shard_map/ppermute | solution.py:593
  7.2 2.7 %collective-permute-done.up_ref.refs_3_ = f32[352,128]{1,0:T(8,128)S(1)} collective-permute-done((f32[352,128]{1,0:T(8,128)S(1)}, f32[352,128]{1,0:T(8,128)S(1)}, u32[]{:S(2)}, u32[]{:S(2)}) %collective-permute-start) | collective-permute-done | bytes 180256 | tf_op jit(solution)/shard_map/ppermute | solution.py:593
  9.9 0.0 collective-permute-done.1.dn_ref.refs_4_
  9.9 0.0 copy-done.1
  9.9 0.0 copy-done
  9.9 0.6 edges.1
  10.5 4.2 %collective-permute-start.2 = (f32[4,64,128]{2,1,0:T(8,128)S(1)}, f32[4,64,128]{2,1,0:T(8,128)S(1)}, u32[]{:S(2)}, u32[]{:S(2)}) collective-permute-start(f32[4,64,128]{2,1,0:T(8,128)S(1)} %get-tuple-element.44), channel_id=1, source_target_pairs={{0,1},{1,2},{2,3},{3,4},{4,5},{5,6},{6,7},{7,8},{8,9},{9,10},{10,1... | collective-permute-start | bytes 393224 | tf_op jit(solution)/shard_map/ppermute | solution.py:593
  14.7 0.0 collective-permute-start.3
  14.7 0.1 pad_add_fusion.refs_0_
  14.8 1.9 %collective-permute-done.2.refs_5_ = f32[4,64,128]{2,1,0:T(8,128)S(1)} collective-permute-done((f32[4,64,128]{2,1,0:T(8,128)S(1)}, f32[4,64,128]{2,1,0:T(8,128)S(1)}, u32[]{:S(2)}, u32[]{:S(2)}) %collective-permute-start.2) | collective-permute-done | bytes 131104 | tf_op jit(solution)/shard_map/ppermute | solution.py:593
  16.6 2.7 %collective-permute-done.3.refs_6_ = f32[4,64,128]{2,1,0:T(8,128)S(1)} collective-permute-done((f32[4,64,128]{2,1,0:T(8,128)S(1)}, f32[4,64,128]{2,1,0:T(8,128)S(1)}, u32[]{:S(2)}, u32[]{:S(2)}) %collective-permute-start.3) | collective-permute-done | bytes 131104 | tf_op jit(solution)/shard_map/ppermute | solution.py:593
  19.4 6.8 %fine.1 = (f32[8,8,128]{2,1,0:T(8,128)S(1)}, f32[16,64,128]{2,1,0:T(8,128)S(1)}, f32[16,64,128]{2,1,0:T(8,128)S(1)}, f32[16,64,128]{2,1,0:T(8,128)S(1)}, f32[16,...) custom-call(s32[2]{0:T(128)S(1)} %pad_add_fusion.refs_0_, ...), custom_call_target="tpu_custom_call" | custom-call | tf_op jit(solution)/shard_map/fine/pallas_call | solution.py:611
  26.2 0.4 collective-permute-start.4
  26.6 4.8 %collective-permute-start.7 = (f32[8,8,128]{2,1,0:T(8,128)S(1)}, f32[8,8,128]{2,1,0:T(8,128)S(1)}, u32[]{:S(2)}, u32[]{:S(2)}) collective-permute-start(f32[8,8,128]{2,1,0:T(8,128)S(1)} %get-tuple-element.46), channel_id=1, source_target_pairs={{0,224},{16,240},{32,0},{48,16},{64,32},{80,48},{96,64},{112,80},{... | collective-permute-start | bytes 98312 | tf_op jit(solution)/shard_map/ppermute | solution.py:593
  31.4 2.8 %collective-permute-start.6 = (f32[8,8,128]{2,1,0:T(8,128)S(1)}, f32[8,8,128]{2,1,0:T(8,128)S(1)}, u32[]{:S(2)}, u32[]{:S(2)}) collective-permute-start(f32[8,8,128]{2,1,0:T(8,128)S(1)} %get-tuple-element.46), channel_id=1, source_target_pairs={{0,240},{16,0},{32,16},{48,32},{64,48},{80,64},{96,80},{112,96},{1... | collective-permute-start | bytes 98312 | tf_op jit(solution)/shard_map/ppermute | solution.py:593
  34.2 0.0 collective-permute-start.5
  34.2 0.0 collective-permute-done.4
  34.2 6.1 %collective-permute-done.5 = f32[8,8,128]{2,1,0:T(8,128)S(1)} collective-permute-done((f32[8,8,128]{2,1,0:T(8,128)S(1)}, f32[8,8,128]{2,1,0:T(8,128)S(1)}, u32[]{:S(2)}, u32[]{:S(2)}) %collective-permute-start.5) | collective-permute-done | bytes 32800 | tf_op jit(solution)/shard_map/ppermute | solution.py:593
  40.3 0.0 collective-permute-done.6
  40.3 0.0 collective-permute-done.7
  40.3 1.8 %collective-permute-start.8 = (f32[4,40,128]{2,1,0:T(8,128)S(1)}, f32[4,40,128]{2,1,0:T(8,128)S(1)}, u32[]{:S(2)}, u32[]{:S(2)}) collective-permute-start(f32[4,40,128]{2,1,0:T(8,128)S(1)} %get-tuple-element.85.refs_2_), channel_id=1, source_target_pairs={{0,1},{1,2},{2,3},{3,4},{4,5},{5,6},{6,7},{7,8},{8,9},{9,10},{10,1... | collective-permute-start | bytes 245768 | tf_op jit(solution)/shard_map/ppermute | solution.py:593
  42.2 0.9 %collective-permute-start.9 = (f32[4,40,128]{2,1,0:T(8,128)S(1)}, f32[4,40,128]{2,1,0:T(8,128)S(1)}, u32[]{:S(2)}, u32[]{:S(2)}) collective-permute-start(f32[4,40,128]{2,1,0:T(8,128)S(1)} %get-tuple-element.86.refs_1_), channel_id=1, source_target_pairs={{0,15},{1,0},{2,1},{3,2},{4,3},{5,4},{6,5},{7,6},{8,7},{9,8},{10,9... | collective-permute-start | bytes 245768 | tf_op jit(solution)/shard_map/ppermute | solution.py:593
  43.1 0.7 collective-permute-done.8.refs_3_
  43.8 2.2 %collective-permute-done.9.refs_4_ = f32[4,40,128]{2,1,0:T(8,128)S(1)} collective-permute-done((f32[4,40,128]{2,1,0:T(8,128)S(1)}, f32[4,40,128]{2,1,0:T(8,128)S(1)}, u32[]{:S(2)}, u32[]{:S(2)}) %collective-permute-start.9) | collective-permute-done | bytes 81952 | tf_op jit(solution)/shard_map/ppermute | solution.py:593
  46.0 3.6 %coarser.1 = (f32[4,128]{1,0:T(4,128)S(1)}, f32[16,40,128]{2,1,0:T(8,128)S(1)}, f32[16,40,128]{2,1,0:T(8,128)S(1)}, f32[16,40,128]{2,1,0:T(8,128)S(1)}, f32[16,4...) custom-call(s32[2]{0:T(128)S(1)} %pad_add_fusion.refs_0_, ...), custom_call_target="tpu_custom_call" | custom-call | tf_op jit(solution)/shard_map/coarser/pallas_call | solution.py:611
  49.7 16.7 %all_to_all.10 = f32[16,4,128]{2,1,0:T(4,128)S(1)} all-to-all(f32[16,4,128]{2,1,0:T(4,128)S(1)} %broadcast_in_dim.6), channel_id=1, replica_groups=mesh['gx'=16,'gy'=16] {'gy'}, dimensions={0} | all-to-all | bytes 65536 | tf_op jit(solution)/shard_map/all_to_all | solution.py:599
  66.4 13.6 %all_to_all.11 = f32[16,64,128]{2,1,0:T(8,128)S(1)} all-to-all(f32[16,64,128]{2,1,0:T(8,128)S(1)} %broadcast_in_dim.15), channel_id=1, replica_groups=mesh['gx'=16,'gy'=16] {'gx'}, dimensions={0} | all-to-all | bytes 1048576 | tf_op jit(solution)/shard_map/all_to_all | solution.py:599
  80.0 7.1 %top.1 = f32[16,32,128]{2,1,0:T(8,128)} custom-call(s32[2]{0:T(128)S(1)} %pad_add_fusion.refs_0_, f32[1024,128]{1,0:T(8,128)S(1)} %bitcast.8, f32[16,64,128]{2,1,0:T(8,128)S(1)} %get-tuple-element.48.refs_2_, f32[16,64,128]{2,1,0:T(8,128)S(1)} %get-tuple-element.49.refs_3_, f32[16,64,128]{2,1,0:T(8,128)S(1)} %get-tuple-element.50.refs_4_, ...), custom_call_target="tpu_custom_call" | custom-call | tf_op jit(solution)/shard_map/top/pallas_call | solution.py:611
  (8 shorter events, 0.1 us)
Async XLA Ops:
  1.1 8.8 %copy-start.1 = (f32[16,32,128]{2,1,0:T(8,128)S(1)}, f32[16,32,128]{2,1,0:T(8,128)}, u32[]{:S(2)}) copy-start(f32[16,32,128]{2,1,0:T(8,128)} %refs_2_.1) | copy-start | bytes 786436
  1.2 8.7 %copy-start = (f32[16,32,128]{2,1,0:T(8,128)S(1)}, f32[16,32,128]{2,1,0:T(8,128)}, u32[]{:S(2)}) copy-start(f32[16,32,128]{2,1,0:T(8,128)} %refs_1_.1) | copy-start | bytes 786436
  1.2 8.7 %collective-permute-start = (f32[352,128]{1,0:T(8,128)S(1)}, f32[352,128]{1,0:T(8,128)S(1)}, u32[]{:S(2)}, u32[]{:S(2)}) collective-permute-start(f32[352,128]{1,0:T(8,128)S(1)} %bitcast.9), channel_id=1, source_target_pairs={{0,16},{16,32},{32,48},{48,64},{64,80},{80,96},{96,112},{112,128},... | collective-permute-start | bytes 540680 | tf_op jit(solution)/shard_map/ppermute | solution.py:593
  3.4 6.5 %collective-permute-start.1 = (f32[352,128]{1,0:T(8,128)S(1)}, f32[352,128]{1,0:T(8,128)S(1)}, u32[]{:S(2)}, u32[]{:S(2)}) collective-permute-start(f32[352,128]{1,0:T(8,128)S(1)} %bitcast.10), channel_id=1, source_target_pairs={{0,240},{16,0},{32,16},{48,32},{64,48},{80,64},{96,80},{112,96},{1... | collective-permute-start | bytes 540680 | tf_op jit(solution)/shard_map/ppermute | solution.py:593
  10.5 6.1 %collective-permute-start.2 = (f32[4,64,128]{2,1,0:T(8,128)S(1)}, f32[4,64,128]{2,1,0:T(8,128)S(1)}, u32[]{:S(2)}, u32[]{:S(2)}) collective-permute-start(f32[4,64,128]{2,1,0:T(8,128)S(1)} %get-tuple-element.44), channel_id=1, source_target_pairs={{0,1},{1,2},{2,3},{3,4},{4,5},{5,6},{6,7},{7,8},{8,9},{9,10},{10,1... | collective-permute-start | bytes 393224 | tf_op jit(solution)/shard_map/ppermute | solution.py:593
  14.7 4.7 %collective-permute-start.3 = (f32[4,64,128]{2,1,0:T(8,128)S(1)}, f32[4,64,128]{2,1,0:T(8,128)S(1)}, u32[]{:S(2)}, u32[]{:S(2)}) collective-permute-start(f32[4,64,128]{2,1,0:T(8,128)S(1)} %get-tuple-element.45), channel_id=1, source_target_pairs={{0,15},{1,0},{2,1},{3,2},{4,3},{5,4},{6,5},{7,6},{8,7},{9,8},{10,9... | collective-permute-start | bytes 393224 | tf_op jit(solution)/shard_map/ppermute | solution.py:593
  26.2 8.0 %collective-permute-start.4 = (f32[8,8,128]{2,1,0:T(8,128)S(1)}, f32[8,8,128]{2,1,0:T(8,128)S(1)}, u32[]{:S(2)}, u32[]{:S(2)}) collective-permute-start(f32[8,8,128]{2,1,0:T(8,128)S(1)} %get-tuple-element.46), channel_id=1, source_target_pairs={{0,32},{16,48},{32,64},{48,80},{64,96},{80,112},{96,128},{112,144}... | collective-permute-start | bytes 98312 | tf_op jit(solution)/shard_map/ppermute | solution.py:593
  26.6 13.7 %collective-permute-start.7 = (f32[8,8,128]{2,1,0:T(8,128)S(1)}, f32[8,8,128]{2,1,0:T(8,128)S(1)}, u32[]{:S(2)}, u32[]{:S(2)}) collective-permute-start(f32[8,8,128]{2,1,0:T(8,128)S(1)} %get-tuple-element.46), channel_id=1, source_target_pairs={{0,224},{16,240},{32,0},{48,16},{64,32},{80,48},{96,64},{112,80},{... | collective-permute-start | bytes 98312 | tf_op jit(solution)/shard_map/ppermute | solution.py:593
  31.4 8.9 %collective-permute-start.6 = (f32[8,8,128]{2,1,0:T(8,128)S(1)}, f32[8,8,128]{2,1,0:T(8,128)S(1)}, u32[]{:S(2)}, u32[]{:S(2)}) collective-permute-start(f32[8,8,128]{2,1,0:T(8,128)S(1)} %get-tuple-element.46), channel_id=1, source_target_pairs={{0,240},{16,0},{32,16},{48,32},{64,48},{80,64},{96,80},{112,96},{1... | collective-permute-start | bytes 98312 | tf_op jit(solution)/shard_map/ppermute | solution.py:593
  34.2 6.1 %collective-permute-start.5 = (f32[8,8,128]{2,1,0:T(8,128)S(1)}, f32[8,8,128]{2,1,0:T(8,128)S(1)}, u32[]{:S(2)}, u32[]{:S(2)}) collective-permute-start(f32[8,8,128]{2,1,0:T(8,128)S(1)} %get-tuple-element.46), channel_id=1, source_target_pairs={{0,16},{16,32},{32,48},{48,64},{64,80},{80,96},{96,112},{112,128},... | collective-permute-start | bytes 98312 | tf_op jit(solution)/shard_map/ppermute | solution.py:593
  40.3 3.5 %collective-permute-start.8 = (f32[4,40,128]{2,1,0:T(8,128)S(1)}, f32[4,40,128]{2,1,0:T(8,128)S(1)}, u32[]{:S(2)}, u32[]{:S(2)}) collective-permute-start(f32[4,40,128]{2,1,0:T(8,128)S(1)} %get-tuple-element.85.refs_2_), channel_id=1, source_target_pairs={{0,1},{1,2},{2,3},{3,4},{4,5},{5,6},{6,7},{7,8},{8,9},{9,10},{10,1... | collective-permute-start | bytes 245768 | tf_op jit(solution)/shard_map/ppermute | solution.py:593
  42.2 3.9 %collective-permute-start.9 = (f32[4,40,128]{2,1,0:T(8,128)S(1)}, f32[4,40,128]{2,1,0:T(8,128)S(1)}, u32[]{:S(2)}, u32[]{:S(2)}) collective-permute-start(f32[4,40,128]{2,1,0:T(8,128)S(1)} %get-tuple-element.86.refs_1_), channel_id=1, source_target_pairs={{0,15},{1,0},{2,1},{3,2},{4,3},{5,4},{6,5},{7,6},{8,7},{9,8},{10,9... | collective-permute-start | bytes 245768 | tf_op jit(solution)/shard_map/ppermute | solution.py:593

commit v3 on v2

--- a/solution.py
+++ b/solution.py
@@ -10,8 +10,10 @@
 SWEEPS = 6
 VERTICAL = 0.015625
 TINY = 2.0**-20
-VMEM_BYTES = 24 * 1024 * 1024
-
+VMEM_BYTES = 16 * 1024 * 1024
+
+SPLIT = 24
+SIDE_ROWS = 40
 ROW0 = (16, 8, 16, 8)
 ROWS = (64, 32, 40, 24)
 LANE0 = (0, 32, 16, 8)
@@ -102,7 +104,7 @@
 
     def factor_and_first(self, blocks, inside, f, v):
         def body(r, h):
-            masks = [inside(r, h, p) for p in self.parts]
+            masks = None if inside is None else [inside(r, h) for p in self.parts]
             ratio = [None for p in self.parts]
             partial = [[] for p in self.parts]
             upper = [None for p in self.parts]
@@ -128,7 +130,7 @@
                     if k + 1 < NZ:
                         center = center + lower[p]
                     pivot = center if k == 0 else center - upper[p] * ratio[p]
-                    inverse = jnp.where(masks[p], rcp(pivot), 0.0)
+                    inverse = rcp(pivot) if masks is None else jnp.where(masks[p], rcp(pivot), 0.0)
                     scaled = 0.8 * inverse
                     self.d[p][k, pl.ds(r, h), :] = scaled
                     value = scaled * f[p][k, pl.ds(r, h), :]
@@ -197,17 +199,20 @@
         run_blocks(blocks, body)
 
 
-def inside_of(level, ix, iy, shape):
+def inside_of(level, ix, iy, shape, part=0):
     grid_rows, grid_lanes, tile_rows, tile_lanes = shape
 
-    def inside(r, h, part):
+    def inside(r, h):
         row, lane = rows_of((h, LANES)) + (r + ix * tile_rows - ROW0[level]), lanes_of((h, LANES))
+        if level == 0 and part == 1:
+            row = row + jnp.where(lane < 64, 0, SPLIT)
+            lane = lane % 64
         good = jnp.logical_and(row >= 0, row < grid_rows)
         if level == 0 and part == 0:
             return good
         if level == 0:
-            right = jnp.logical_and(lane < 64, iy * tile_lanes + tile_lanes < grid_lanes)
-            side = jnp.logical_or(right, jnp.logical_and(lane >= 64, iy > 0))
+            column = iy * tile_lanes + jnp.where(lane < 32, lane - 16, lane + 80)
+            side = jnp.logical_and(column >= 0, column < grid_lanes)
         else:
             column = iy * tile_lanes + lane - LANE0[level]
             side = jnp.logical_and(column >= 0, column < grid_lanes)
@@ -254,61 +259,110 @@
                 right_ref[field * 2 + half, pl.ds(first, count), :] = rights
 
 
+def inner_kernel(f_ref, rho_ref, fm, vm, axm, aym, dm, em, gm, rm, firstm, um, resm):
+    for k in range(NZ):
+        fm[k, pl.ds(16, 32), :] = f_ref[k, :, :]
+        rm[k, pl.ds(16, 32), :] = rho_ref[k, :, :]
+    main = Level(0, [rm], [axm], [aym], [dm], [em], [gm])
+    main.faces([(17, 16), (32, 16)])
+    main.factor_and_first([(17, 16), (31, 16)], None, [fm], [firstm])
+    main.relax([(18, 16), (30, 16)], [fm], [firstm], [vm], u=[um])
+    main.residual([(19, 16), (29, 16)], [fm], [um], [resm])
+
+
+def outer_kernel(grid, index_ref, near_ref, far_ref, *refs):
+    fm, vm, axm, aym, dm, em, gm, rm, firstm, um, resm = refs[11:]
+    ix, iy = index_ref[0], index_ref[1]
+    inside = inside_of(0, ix, iy, grid + (32, 128))
+    for k in range(NZ):
+        for piece in PIECES:
+            if piece[2] == "own":
+                continue
+            first, count = piece[:2]
+            fm[k, pl.ds(first, count), :] = piece_of(piece, 0, k, None, near_ref, far_ref)
+            x = piece_of(piece, 1, k, None, near_ref, far_ref)
+            rm[k, pl.ds(first, count), :] = jnp.where(inside(first, count), x, 0.0)
+    main = Level(0, [rm], [axm], [aym], [dm], [em], [gm])
+    main.faces([(1, 16), (48, 16)])
+    main.factor_and_first([(1, 16), (47, 16)], inside, [fm], [firstm])
+    main.relax([(2, 16), (46, 16)], [fm], [firstm], [vm], u=[um])
+    main.residual([(3, 16), (45, 16)], [fm], [um], [resm])
+
+
 def fine_kernel(
-    grid, index_ref, f_ref, rho_ref, up_ref, dn_ref, from_left_ref, from_right_ref,
-    pack_ref, fm, fh, vm, vh, axm, axh, aym, ayh, dm, dh, em, eh, gm, gh, f1, v1, ax1, ay1, d1, e1, g1,
-    rm, rh, firstm, firsth, um, uh, rho1, first1, u1, res1,
+    grid, index_ref, rm, resm, own_left, own_right, from_left_ref, from_right_ref,
+    pack_ref, fh, vh, axh, ayh, dh, eh, gh, f1, v1, ax1, ay1, d1, e1, g1,
+    rh, firsth, uh, rho1, first1, u1, res1,
 ):
     ix, iy = index_ref[0], index_ref[1]
     grid_rows, grid_lanes = grid
-    inside = inside_of(0, ix, iy, (grid_rows, grid_lanes, 32, 128))
-
-    for field, (own, main, side) in enumerate(((f_ref, fm, fh), (rho_ref, rm, rh))):
-        for k in range(NZ):
-            for piece in PIECES:
-                first, count, source, _ = piece
-                x = piece_of(piece, field, k, own, up_ref, dn_ref)
-                if field == 1 and source != "own":
-                    x = jnp.where(inside(first, count, 0), x, 0.0)
-                main[k, pl.ds(first, count), :] = x
-        for first in (5, 16, 32, 43):
-            slot = lanes_of((16, LANES)) // 16
-            good = inside(first, 16, 1)
+    inside = inside_of(0, ix, iy, grid + (32, 128), part=1)
+
+    lane = lanes_of((16, LANES))
+    for field, side in enumerate((fh, rh)):
+        for first in (4, 20):
+            good = inside(first, 16)
             for half in range(2):
-                right = from_right_ref[field * 2 + half, pl.ds(first, 16), :]
-                left = pltpu.roll(from_left_ref[field * 2 + half, pl.ds(first, 16), :], LANES - 16, 1)
-                merged = [jnp.where(slot % 2 == odd, right, left) for odd in range(2)]
-                for q in range(8):
-                    y = merged[q % 2]
-                    y = y if q == 0 else pltpu.roll(y, LANES - 16 * q, 1)
-                    if field == 1:
-                        y = jnp.where(good, y, 0.0)
-                    side[half * 8 + q, pl.ds(first, 16), :] = y
-
-    fine = Level(0, [rm, rh], [axm, axh], [aym, ayh], [dm, dh], [em, eh], [gm, gh])
-    fine.faces([(6, 16, 3), (51, 8)])
-    fine.factor_and_first([(6, 16, 3), (50, 8)], inside, [fm, fh], [firstm, firsth])
-    fine.relax([(7, 16, 3), (49, 8)], [fm, fh], [firstm, firsth], [vm, vh], u=[um, uh])
-    fine.residual([(8, 16, 3)], [fm, fh], [um, uh], [firstm, firsth])
-
-    main_matrix = one_hot(LANES, lambda s, t: s // 2 + 32 == t, 0.25)
-    side_matrix = one_hot(
-        LANES,
-        lambda s, t: jnp.logical_or(
-            jnp.logical_and(s < 64, s // 2 + 96 == t), jnp.logical_and(s >= 64, s // 2 - 32 == t)
-        ),
-        0.25,
-    )
+                g = field * 2 + half
+                tiles = []
+                for start in (first, first + SPLIT):
+                    rows = pl.ds(start, 16)
+                    tiles.append(
+                        [
+                            from_left_ref[g, rows, :],
+                            pltpu.roll(own_left[g, rows, :], 16, 1),
+                            pltpu.roll(own_right[g, rows, :], 32, 1),
+                            pltpu.roll(from_right_ref[g, rows, :], 48, 1),
+                        ]
+                    )
+                for m in range(4):
+                    place = (lane - 16 * m) % 128
+                    spot = place % 64
+                    upper, lower = [
+                        jnp.where(
+                            spot < 32, jnp.where(spot < 16, t[0], t[1]), jnp.where(spot < 48, t[2], t[3])
+                        )
+                        for t in tiles
+                    ]
+                    straight = jnp.where(place < 64, upper, lower)
+                    crossed = jnp.where(place < 64, lower, upper)
+                    if m > 0:
+                        straight = pltpu.roll(straight, LANES - 16 * m, 1)
+                        crossed = pltpu.roll(crossed, LANES - 16 * m, 1)
+                    crossed = pltpu.roll(crossed, 64, 1)
+                    for layer, y in (
+                        (m, jnp.where(lane < 64, straight, crossed)),
+                        (m + 4, jnp.where(lane < 64, crossed, straight)),
+                    ):
+                        if field == 1:
+                            y = jnp.where(good, y, 0.0)
+                        side[half * 8 + layer, pl.ds(first, 16), :] = y
+
+    sides = Level(0, [rh], [axh], [ayh], [dh], [eh], [gh])
+    sides.faces([(4, 16), (20, 16)])
+    sides.factor_and_first([(5, 16), (19, 16)], inside, [fh], [firsth])
+    sides.relax([(6, 16), (18, 16)], [fh], [firsth], [vh], u=[uh])
+    sides.residual([(8, 24)], [fh], [uh], [firsth])
+
+    main_matrix = one_hot(LANES, lambda s, t: (s // 2 + 32 == t) & (s >= 4) & (s < 124), 0.25)
+    upper_matrix, lower_matrix = [
+        one_hot(
+            LANES,
+            lambda s, t: ((s // 2 - base // 2 + 24 == t) & (s >= base + 6) & (s < base + 20))
+            | ((s // 2 - base // 2 + 72 == t) & (s >= base + 44) & (s < base + 58)),
+            0.25,
+        )
+        for base in (0, 64)
+    ]
     for first in range(0, NZ, 4):
         ks = range(first, first + 4)
-        total = split_dot(stack_rows([pair_rows(firstm, k, 8, 24) for k in ks]), main_matrix)
-        total = total + split_dot(stack_rows([pair_rows(firsth, k, 8, 24) for k in ks]), side_matrix)
-        for n, k in enumerate(ks):
-            f1[k, pl.ds(4, 24), :] = total[n * 24 : (n + 1) * 24]
-        total = split_dot(stack_rows([pair_rows(rm, k, 0, 32) for k in ks]), main_matrix)
-        total = total + split_dot(stack_rows([pair_rows(rh, k, 0, 32) for k in ks]), side_matrix)
-        for n, k in enumerate(ks):
-            rho1[k, :, :] = total[n * 32 : (n + 1) * 32]
+        for target, main, side in ((f1, resm, firsth), (rho1, rm, rh)):
+            total = split_dot(stack_rows([pair_rows(main, k, 0, 32) for k in ks]), main_matrix)
+            upper = split_dot(stack_rows([pair_rows(side, k, 0, 16) for k in ks]), upper_matrix)
+            lower = split_dot(stack_rows([pair_rows(side, k, 8, 16) for k in ks]), lower_matrix)
+            for n, k in enumerate(ks):
+                target[k, pl.ds(0, 16), :] = total[n * 32 : n * 32 + 16] + upper[n * 16 : n * 16 + 16]
+                target[k, pl.ds(16, 16), :] = total[n * 32 + 16 : n * 32 + 32] + lower[n * 16 : n * 16 + 16]
 
     middle = Level(1, [rho1], [ax1], [ay1], [d1], [e1], [g1])
     inside = inside_of(1, ix, iy, (grid_rows // 2, grid_lanes // 2, 16, 64))
@@ -349,7 +403,7 @@
     inside = inside_of(2, ix, iy, (grid_rows // 4, grid_lanes // 4, 8, 32))
 
     lane40 = lanes_of((40, LANES))
-    good = inside(0, 40, 0)
+    good = inside(0, 40)
     for field, target in enumerate((f2, rho2)):
         for half in range(2):
             g = field * 2 + half
@@ -416,7 +470,7 @@
 
 
 def top_kernel(
-    grid, tiles, index_ref, gathered, fm, fh, vm, vh, axm, axh, aym, ayh, dm, dh, em, eh, gm, gh,
+    grid, tiles, index_ref, gathered, fm, vm, axm, aym, dm, em, gm, fh, vh, axh, ayh, dh, eh, gh,
     f1, v1, ax1, ay1, d1, e1, g1, f2, v2, ax2, ay2, d2, e2, g2, f3, v3, ax3, ay3, d3, e3, g3,
     out_ref,
     rho4, f4, ax4, ay4, d4, e4, g4, c4, a4, va4, vb4, va3, vb3, va2, vb2, va1, vb1, vam, vah, vbm, vbh,
@@ -575,17 +629,36 @@
     level1.relax([(4, 24)], [f1], [vb1], [va1])
 
     to_main = one_hot(LANES, lambda s, t: s == t // 2 + 32, 1.0)
-    to_side = one_hot(
-        LANES,
-        lambda s, t: jnp.logical_or(
-            jnp.logical_and(t < 64, s == t // 2 + 96), jnp.logical_and(t >= 64, s == t // 2 - 32)
-        ),
-        1.0,
-    )
-    prolong(lambda k: va1[k, pl.ds(4, 24), :], 0, 24, None, [vm, vh], [vam, vah], 8, [to_main, to_side])
-    fine = Level(0, None, [axm, axh], [aym, ayh], [dm, dh], [em, eh], [gm, gh])
-    fine.relax([(15, 16, 2), (41, 8)], [fm, fh], [vam, vah], [vbm, vbh])
-    fine.relax([(16, 16, 2)], [fm, fh], [vbm, vbh], [out_ref], wanted=[0], shift=16)
+    prolong(lambda k: va1[k, pl.ds(4, 24), :], 0, 24, None, [vm], [vam], 8, [to_main])
+    lane = lanes_of((16, LANES))
+    to_upper, to_lower = [
+        one_hot(
+            LANES,
+            lambda s, t: ((t < base + 32) & (t >= base) & (s == (t - base) // 2 + 24))
+            | ((t >= base + 32) & (t < base + 64) & (s == (t - base) // 2 + 72)),
+            1.0,
+        )
+        for base in (0, 64)
+    ]
+    upper = split_dot(stack_rows([va1[k, pl.ds(2, 16), :] for k in range(NZ)]), to_upper)
+    lower = split_dot(stack_rows([va1[k, pl.ds(2 + SPLIT // 2, 16), :] for k in range(NZ)]), to_lower)
+    for k in range(NZ):
+        x = jnp.where(lane < 64, upper[k * 16 : k * 16 + 16], lower[k * 16 : k * 16 + 16])
+        for odd in range(2):
+            where = pl.ds(4 + odd, 16, stride=2)
+            vah.at[k][where, :] = vh.at[k][where, :] + x
+    sides = Level(0, None, [axh], [ayh], [dh], [eh], [gh])
+    sides.relax([(7, 16), (17, 16)], [fh], [vah], [vbh])
+    sides.relax([(8, 24)], [fh], [vbh], [vah])
+    main = Level(0, None, [axm], [aym], [dm], [em], [gm])
+    main.relax([(15, 16, 2), (41, 8)], [fm], [vam], [vbm])
+    main.relax([(16, 16, 2)], [fm], [vbm], [vam])
+    for k in range(NZ):
+        for row, start, low, high in ((0, 16, 112, 80), (16, 16 - SPLIT + 16, 48, 16)):
+            side = vah[k, pl.ds(start, 16), :]
+            side = jnp.where(lane < 64, pltpu.roll(side, low, 1), pltpu.roll(side, high, 1))
+            x = vam[k, pl.ds(16 + row, 16), :]
+            out_ref[k, pl.ds(row, 16), :] = jnp.where(jnp.logical_or(lane < 4, lane >= 124), side, x)
 
 
 def ring(x, axis, step):
@@ -603,7 +676,7 @@
     return jax.ShapeDtypeStruct(shape, jnp.float32)
 
 
-def call(kernel, name, outs, scratch, index, *operands):
+def call(kernel, name, outs, scratch, index, *operands, aliases=None, cost=4000000):
     vmem = pl.BlockSpec(memory_space=pltpu.VMEM)
     ins = [vmem] * len(operands)
     if index is not None:
@@ -615,6 +688,8 @@
         out_specs=[vmem] * len(outs),
         scratch_shapes=[pltpu.VMEM(shape, jnp.float32) for shape in scratch],
         compiler_params=pltpu.CompilerParams(vmem_limit_bytes=VMEM_BYTES),
+        input_output_aliases=aliases or {},
+        cost_estimate=pl.CostEstimate(flops=cost, bytes_accessed=cost, transcendentals=0),
         name=name,
     )(*operands)
 
@@ -632,18 +707,24 @@
         highs = both[-REACH:].reshape(REACH * 2 * NZ, LANES)
         up = ring(highs, "gx", 1)
         dn = ring(lows, "gx", -1)
+        s0, s1, s2, s3 = [x.shape for x in big]
+        sh = (NZ, SIDE_ROWS, LANES)
+        inner = call(inner_kernel, "inner", [big[0]] * 11, [], None, source, rho)
         strip = array(4, ROWS[0], LANES)
         lefts, rights = call(edges_kernel, "edges", [strip, strip], [], None, source, rho, up, dn)
         from_left_strip = ring(rights, "gy", 1)
         from_right_strip = ring(lefts, "gy", -1)
-
-        s0, s1, s2, s3 = [x.shape for x in big]
+        main = call(
+            lambda *refs: outer_kernel(grid, *refs), "outer", [big[0]] * 11, [], index, up, dn, *inner,
+            aliases={3 + n: n for n in range(11)},
+        )
+        main_state, rho_main, residual_main = main[:7], main[7], main[10]
         fine = call(
             lambda *refs: fine_kernel(grid, *refs),
             "fine",
-            [array(8, 8, LANES)] + [big[0]] * 14 + [big[1]] * 7,
-            [s0] * 6 + [s1] * 4,
-            index, source, rho, up, dn, from_left_strip, from_right_strip,
+            [array(8, 8, LANES)] + [array(*sh)] * 7 + [big[1]] * 7,
+            [sh] * 3 + [s1] * 4,
+            index, rho_main, residual_main, lefts, rights, from_left_strip, from_right_strip,
         )
         tile = fine[0]
         pieces = [ring(tile, "gx", 2), ring(tile, "gx", 1), tile, ring(tile, "gx", -1), ring(tile, "gx", -2)]
@@ -665,8 +746,8 @@
             lambda *refs: top_kernel(grid, (tiles_x, tiles_y), *refs),
             "top",
             [array(NZ, 32, LANES)],
-            [s4] * 11 + [s3] * 2 + [s2] * 2 + [s1] * 2 + [s0] * 4,
-            index, gathered, *fine[1:], *coarser[1:],
+            [s4] * 11 + [s3] * 2 + [s2] * 2 + [s1] * 2 + [s0, sh] * 2,
+            index, gathered, *main_state, *fine[1:], *coarser[1:],
         )
         return pressure
 

time: 87.3 us -> 84.2 us (0.964)
  waiting for transfers between devices: 16.4 us -> 10.5 us
  starting transfers between devices: 20.8 us -> 24.6 us
  blocking collectives: 30.3 us -> 29.4 us
    ppermute x10, waiting for transfers between devices: 16.4 us -> 10.5 us  [ring(): return lax.ppermute(x, axis, [(i, (i + step) % size) for i in range(size)])]
    ppermute x10, starting transfers between devices: 20.8 us -> 24.6 us  [ring(): return lax.ppermute(x, axis, [(i, (i + step) % size) for i in range(size)])]
    all_to_all x2, blocking collectives: 30.3 us -> 29.4 us  [gather(): return lax.all_to_all(blocks, axis, 0, 0).reshape(size * x.shape[0], LANES)]
    pallas_call x4 -> x6, Pallas kernels: 18.1 us -> 18.1 us  [call(): pl.pallas_call(kernel, out_shape=outs, in_specs=ins, out_specs=[vmem] * l...]
  transfers between devices with their start and end apart: 10 -> 10, of which waited for: 6 -> 5; matrix products, arithmetic and copies ran while one was open for 0% -> 0% of each run, Pallas kernels for 0% -> 4%
where the time goes in v3:
time: 84.2 us; the launch traced here: 84 us
  blocking collectives  29.4 us (35%)
  starting transfers between devices  24.6 us (29%)
  Pallas kernels  18.1 us (21%)
  waiting for transfers between devices  10.5 us (12%)
  other arithmetic  1.14 us (1%)
    all_to_all x2, blocking collectives, gather(): return lax.all_to_all(blocks, axis, 0, 0).reshape(size * x.shape[0], LANES)  29.4 us
    ppermute x10, starting transfers between devices, ring(): return lax.ppermute(x, axis, [(i, (i + step) % size) for i in range(size)])  24.6 us
    pallas_call x6, Pallas kernels, call(): pl.pallas_call(kernel, out_shape=outs, in_specs=ins, out_specs=[vmem] * l...  18.1 us
    ppermute x10, waiting for transfers between devices, ring(): return lax.ppermute(x, axis, [(i, (i + step) % size) for i in range(size)])  10.5 us
  transfers between devices with their start and end apart: 10, of which 5 were waited for; matrix products, arithmetic and copies ran while one was open for 0% of the time, Pallas kernels for 4%

profile of v3, /device:TPU:1, one launch (start us, length us, event | category | flops | bytes accessed | tf_op | source)
XLA Modules:
  0.0 84.0 jit_solution(7675770788347724872)
XLA Ops:
  0.0 1.1 %maximum_bitcast_fusion = f32[32,32,128]{2,0,1:T(8,128)S(1)} fusion(f32[16,32,128]{2,1,0:T(8,128)} %rho_ref.3, f32[16,32,128]{2,1,0:T(8,128)} %f_ref.3), kind=kLoop, calls=%fused_computation | loop fusion | flops 131072 | bytes 1048576 | tf_op jit(solution)/shard_map/transpose | solution.py:705
  1.1 0.0 copy-start.1
  1.1 0.1 copy.14
  1.2 0.0 copy-start
  1.2 2.1 %collective-permute-start = (f32[352,128]{1,0:T(8,128)S(1)}, f32[352,128]{1,0:T(8,128)S(1)}, u32[]{:S(2)}, u32[]{:S(2)}) collective-permute-start(f32[352,128]{1,0:T(8,128)S(1)} %bitcast.9), channel_id=1, source_target_pairs={{0,16},{16,32},{32,48},{48,64},{64,80},{80,96},{96,112},{112,128},... | collective-permute-start | bytes 540680 | tf_op jit(solution)/shard_map/ppermute | solution.py:666
  3.3 0.1 copy.15
  3.4 3.8 %collective-permute-start.1 = (f32[352,128]{1,0:T(8,128)S(1)}, f32[352,128]{1,0:T(8,128)S(1)}, u32[]{:S(2)}, u32[]{:S(2)}) collective-permute-start(f32[352,128]{1,0:T(8,128)S(1)} %bitcast.10), channel_id=1, source_target_pairs={{0,240},{16,0},{32,16},{48,32},{64,48},{80,64},{96,80},{112,96},{1... | collective-permute-start | bytes 540680 | tf_op jit(solution)/shard_map/ppermute | solution.py:666
  7.2 2.7 %collective-permute-done.refs_1_.up_ref = f32[352,128]{1,0:T(8,128)S(1)} collective-permute-done((f32[352,128]{1,0:T(8,128)S(1)}, f32[352,128]{1,0:T(8,128)S(1)}, u32[]{:S(2)}, u32[]{:S(2)}) %collective-permute-start) | collective-permute-done | bytes 180256 | tf_op jit(solution)/shard_map/ppermute | solution.py:666
  9.9 0.0 collective-permute-done.1.refs_2_.dn_ref
  9.9 0.0 copy-done.1
  9.9 0.0 copy-done
  9.9 0.6 edges.1
  10.5 3.4 %collective-permute-start.3 = (f32[4,64,128]{2,1,0:T(8,128)S(1)}, f32[4,64,128]{2,1,0:T(8,128)S(1)}, u32[]{:S(2)}, u32[]{:S(2)}) collective-permute-start(f32[4,64,128]{2,1,0:T(8,128)S(1)} %get-tuple-element.70.refs_3_), channel_id=1, source_target_pairs={{0,15},{1,0},{2,1},{3,2},{4,3},{5,4},{6,5},{7,6},{8,7},{9,8},{10,9... | collective-permute-start | bytes 393224 | tf_op jit(solution)/shard_map/ppermute | solution.py:666
  13.9 0.8 collective-permute-start.2
  14.7 1.2 %inner.1 = (f32[16,64,128]{2,1,0:T(8,128)S(1)}, f32[16,64,128]{2,1,0:T(8,128)S(1)}, f32[16,64,128]{2,1,0:T(8,128)S(1)}, f32[16,64,128]{2,1,0:T(8,128)S(1)}, f32[...) custom-call(f32[16,32,128]{2,1,0:T(8,128)S(1)} %copy-done.1, ...), custom_call_target="tpu_custom_call" | custom-call | flops 4000000 | bytes 4000000 | tf_op jit(solution)/shard_map/inner/pallas_call | solution.py:684
  15.9 0.1 pad_add_fusion.refs_0_
  16.0 1.9 %outer.1 = (f32[16,64,128]{2,1,0:T(8,128)S(1)}, f32[16,64,128]{2,1,0:T(8,128)S(1)}, f32[16,64,128]{2,1,0:T(8,128)S(1)}, f32[16,64,128]{2,1,0:T(8,128)S(1)}, f32[...) custom-call(s32[2]{0:T(128)S(1)} %pad_add_fusion.refs_0_, ...), custom_call_target="tpu_custom_call", output_to_operand_aliasing={{0}: (3, {}), {1}: (4, {}), {2}: (5, {}), {3}: (6, {}), {4}... | custom-call | flops 4000000 | bytes 4000000 | tf_op jit(solution)/shard_map/outer/pallas_call | solution.py:684
  17.8 0.0 collective-permute-done.3.refs_6_
  17.9 0.7 collective-permute-done.2.refs_5_
  18.6 3.2 %fine.1 = (f32[8,8,128]{2,1,0:T(8,128)S(1)}, f32[16,40,128]{2,1,0:T(8,128)S(1)}, f32[16,40,128]{2,1,0:T(8,128)S(1)}, f32[16,40,128]{2,1,0:T(8,128)S(1)}, f32[16,...) custom-call(s32[2]{0:T(128)S(1)} %pad_add_fusion.refs_0_, ...), custom_call_target="tpu_custom_call" | custom-call | flops 4000000 | bytes 4000000 | tf_op jit(solution)/shard_map/fine/pallas_call | solution.py:684
  21.8 0.1 collective-permute-start.4
  21.9 5.1 %collective-permute-start.7 = (f32[8,8,128]{2,1,0:T(8,128)S(1)}, f32[8,8,128]{2,1,0:T(8,128)S(1)}, u32[]{:S(2)}, u32[]{:S(2)}) collective-permute-start(f32[8,8,128]{2,1,0:T(8,128)S(1)} %get-tuple-element.72), channel_id=1, source_target_pairs={{0,224},{16,240},{32,0},{48,16},{64,32},{80,48},{96,64},{112,80},{... | collective-permute-start | bytes 98312 | tf_op jit(solution)/shard_map/ppermute | solution.py:666
  27.0 2.5 %collective-permute-start.6 = (f32[8,8,128]{2,1,0:T(8,128)S(1)}, f32[8,8,128]{2,1,0:T(8,128)S(1)}, u32[]{:S(2)}, u32[]{:S(2)}) collective-permute-start(f32[8,8,128]{2,1,0:T(8,128)S(1)} %get-tuple-element.72), channel_id=1, source_target_pairs={{0,240},{16,0},{32,16},{48,32},{64,48},{80,64},{96,80},{112,96},{1... | collective-permute-start | bytes 98312 | tf_op jit(solution)/shard_map/ppermute | solution.py:666
  29.5 0.0 collective-permute-start.5
  29.5 0.0 collective-permute-done.4
  29.5 6.1 %collective-permute-done.5 = f32[8,8,128]{2,1,0:T(8,128)S(1)} collective-permute-done((f32[8,8,128]{2,1,0:T(8,128)S(1)}, f32[8,8,128]{2,1,0:T(8,128)S(1)}, u32[]{:S(2)}, u32[]{:S(2)}) %collective-permute-start.5) | collective-permute-done | bytes 32800 | tf_op jit(solution)/shard_map/ppermute | solution.py:666
  35.6 0.0 collective-permute-done.6
  35.6 0.0 collective-permute-done.7
  35.7 2.8 %collective-permute-start.8 = (f32[4,40,128]{2,1,0:T(8,128)S(1)}, f32[4,40,128]{2,1,0:T(8,128)S(1)}, u32[]{:S(2)}, u32[]{:S(2)}) collective-permute-start(f32[4,40,128]{2,1,0:T(8,128)S(1)} %get-tuple-element.111.refs_2_), channel_id=1, source_target_pairs={{0,1},{1,2},{2,3},{3,4},{4,5},{5,6},{6,7},{7,8},{8,9},{9,10},{10,1... | collective-permute-start | bytes 245768 | tf_op jit(solution)/shard_map/ppermute | solution.py:666
  38.5 4.0 %collective-permute-start.9 = (f32[4,40,128]{2,1,0:T(8,128)S(1)}, f32[4,40,128]{2,1,0:T(8,128)S(1)}, u32[]{:S(2)}, u32[]{:S(2)}) collective-permute-start(f32[4,40,128]{2,1,0:T(8,128)S(1)} %get-tuple-element.112.refs_1_), channel_id=1, source_target_pairs={{0,15},{1,0},{2,1},{3,2},{4,3},{5,4},{6,5},{7,6},{8,7},{9,8},{10,9... | collective-permute-start | bytes 245768 | tf_op jit(solution)/shard_map/ppermute | solution.py:666
  42.5 0.7 collective-permute-done.8.refs_3_
  43.2 0.2 collective-permute-done.9.refs_4_
  43.4 3.7 %coarser.1 = (f32[4,128]{1,0:T(4,128)S(1)}, f32[16,40,128]{2,1,0:T(8,128)S(1)}, f32[16,40,128]{2,1,0:T(8,128)S(1)}, f32[16,40,128]{2,1,0:T(8,128)S(1)}, f32[16,4...) custom-call(s32[2]{0:T(128)S(1)} %pad_add_fusion.refs_0_, ...), custom_call_target="tpu_custom_call" | custom-call | flops 4000000 | bytes 4000000 | tf_op jit(solution)/shard_map/coarser/pallas_call | solution.py:684
  47.0 15.8 %all_to_all.10 = f32[16,4,128]{2,1,0:T(4,128)S(1)} all-to-all(f32[16,4,128]{2,1,0:T(4,128)S(1)} %broadcast_in_dim.6), channel_id=1, replica_groups=mesh['gx'=16,'gy'=16] {'gy'}, dimensions={0} | all-to-all | bytes 65536 | tf_op jit(solution)/shard_map/all_to_all | solution.py:672
  62.9 13.6 %all_to_all.11 = f32[16,64,128]{2,1,0:T(8,128)S(1)} all-to-all(f32[16,64,128]{2,1,0:T(8,128)S(1)} %broadcast_in_dim.15), channel_id=1, replica_groups=mesh['gx'=16,'gy'=16] {'gx'}, dimensions={0} | all-to-all | bytes 1048576 | tf_op jit(solution)/shard_map/all_to_all | solution.py:672
  76.5 7.5 %top.1 = f32[16,32,128]{2,1,0:T(8,128)} custom-call(s32[2]{0:T(128)S(1)} %pad_add_fusion.refs_0_, f32[1024,128]{1,0:T(8,128)S(1)} %bitcast.8, f32[16,64,128]{2,1,0:T(8,128)S(1)} %get-tuple-element.74.refs_2_, f32[16,64,128]{2,1,0:T(8,128)S(1)} %get-tuple-element.75.refs_3_, f32[16,64,128]{2,1,0:T(8,128)S(1)} %get-tuple-element.76.refs_4_, ...), custom_call_target="tpu_custom_call" | custom-call | flops 4000000 | bytes 4000000 | tf_op jit(solution)/shard_map/top/pallas_call | solution.py:684
  (8 shorter events, 0.1 us)
Async XLA Ops:
  1.1 8.8 %copy-start.1 = (f32[16,32,128]{2,1,0:T(8,128)S(1)}, f32[16,32,128]{2,1,0:T(8,128)}, u32[]{:S(2)}) copy-start(f32[16,32,128]{2,1,0:T(8,128)} %f_ref.3) | copy-start | bytes 786436
  1.2 8.7 %copy-start = (f32[16,32,128]{2,1,0:T(8,128)S(1)}, f32[16,32,128]{2,1,0:T(8,128)}, u32[]{:S(2)}) copy-start(f32[16,32,128]{2,1,0:T(8,128)} %rho_ref.3) | copy-start | bytes 786436
  1.2 8.7 %collective-permute-start = (f32[352,128]{1,0:T(8,128)S(1)}, f32[352,128]{1,0:T(8,128)S(1)}, u32[]{:S(2)}, u32[]{:S(2)}) collective-permute-start(f32[352,128]{1,0:T(8,128)S(1)} %bitcast.9), channel_id=1, source_target_pairs={{0,16},{16,32},{32,48},{48,64},{64,80},{80,96},{96,112},{112,128},... | collective-permute-start | bytes 540680 | tf_op jit(solution)/shard_map/ppermute | solution.py:666
  3.4 6.5 %collective-permute-start.1 = (f32[352,128]{1,0:T(8,128)S(1)}, f32[352,128]{1,0:T(8,128)S(1)}, u32[]{:S(2)}, u32[]{:S(2)}) collective-permute-start(f32[352,128]{1,0:T(8,128)S(1)} %bitcast.10), channel_id=1, source_target_pairs={{0,240},{16,0},{32,16},{48,32},{64,48},{80,64},{96,80},{112,96},{1... | collective-permute-start | bytes 540680 | tf_op jit(solution)/shard_map/ppermute | solution.py:666
  10.5 7.3 %collective-permute-start.3 = (f32[4,64,128]{2,1,0:T(8,128)S(1)}, f32[4,64,128]{2,1,0:T(8,128)S(1)}, u32[]{:S(2)}, u32[]{:S(2)}) collective-permute-start(f32[4,64,128]{2,1,0:T(8,128)S(1)} %get-tuple-element.70.refs_3_), channel_id=1, source_target_pairs={{0,15},{1,0},{2,1},{3,2},{4,3},{5,4},{6,5},{7,6},{8,7},{9,8},{10,9... | collective-permute-start | bytes 393224 | tf_op jit(solution)/shard_map/ppermute | solution.py:666
  13.9 4.6 %collective-permute-start.2 = (f32[4,64,128]{2,1,0:T(8,128)S(1)}, f32[4,64,128]{2,1,0:T(8,128)S(1)}, u32[]{:S(2)}, u32[]{:S(2)}) collective-permute-start(f32[4,64,128]{2,1,0:T(8,128)S(1)} %get-tuple-element.71.refs_4_), channel_id=1, source_target_pairs={{0,1},{1,2},{2,3},{3,4},{4,5},{5,6},{6,7},{7,8},{8,9},{9,10},{10,1... | collective-permute-start | bytes 393224 | tf_op jit(solution)/shard_map/ppermute | solution.py:666
  21.8 7.7 %collective-permute-start.4 = (f32[8,8,128]{2,1,0:T(8,128)S(1)}, f32[8,8,128]{2,1,0:T(8,128)S(1)}, u32[]{:S(2)}, u32[]{:S(2)}) collective-permute-start(f32[8,8,128]{2,1,0:T(8,128)S(1)} %get-tuple-element.72), channel_id=1, source_target_pairs={{0,32},{16,48},{32,64},{48,80},{64,96},{80,112},{96,128},{112,144}... | collective-permute-start | bytes 98312 | tf_op jit(solution)/shard_map/ppermute | solution.py:666
  21.9 13.7 %collective-permute-start.7 = (f32[8,8,128]{2,1,0:T(8,128)S(1)}, f32[8,8,128]{2,1,0:T(8,128)S(1)}, u32[]{:S(2)}, u32[]{:S(2)}) collective-permute-start(f32[8,8,128]{2,1,0:T(8,128)S(1)} %get-tuple-element.72), channel_id=1, source_target_pairs={{0,224},{16,240},{32,0},{48,16},{64,32},{80,48},{96,64},{112,80},{... | collective-permute-start | bytes 98312 | tf_op jit(solution)/shard_map/ppermute | solution.py:666
  27.0 8.6 %collective-permute-start.6 = (f32[8,8,128]{2,1,0:T(8,128)S(1)}, f32[8,8,128]{2,1,0:T(8,128)S(1)}, u32[]{:S(2)}, u32[]{:S(2)}) collective-permute-start(f32[8,8,128]{2,1,0:T(8,128)S(1)} %get-tuple-element.72), channel_id=1, source_target_pairs={{0,240},{16,0},{32,16},{48,32},{64,48},{80,64},{96,80},{112,96},{1... | collective-permute-start | bytes 98312 | tf_op jit(solution)/shard_map/ppermute | solution.py:666
  29.5 6.1 %collective-permute-start.5 = (f32[8,8,128]{2,1,0:T(8,128)S(1)}, f32[8,8,128]{2,1,0:T(8,128)S(1)}, u32[]{:S(2)}, u32[]{:S(2)}) collective-permute-start(f32[8,8,128]{2,1,0:T(8,128)S(1)} %get-tuple-element.72), channel_id=1, source_target_pairs={{0,16},{16,32},{32,48},{48,64},{64,80},{80,96},{96,112},{112,128},... | collective-permute-start | bytes 98312 | tf_op jit(solution)/shard_map/ppermute | solution.py:666
  35.7 7.5 %collective-permute-start.8 = (f32[4,40,128]{2,1,0:T(8,128)S(1)}, f32[4,40,128]{2,1,0:T(8,128)S(1)}, u32[]{:S(2)}, u32[]{:S(2)}) collective-permute-start(f32[4,40,128]{2,1,0:T(8,128)S(1)} %get-tuple-element.111.refs_2_), channel_id=1, source_target_pairs={{0,1},{1,2},{2,3},{3,4},{4,5},{5,6},{6,7},{7,8},{8,9},{9,10},{10,1... | collective-permute-start | bytes 245768 | tf_op jit(solution)/shard_map/ppermute | solution.py:666
  38.5 4.9 %collective-permute-start.9 = (f32[4,40,128]{2,1,0:T(8,128)S(1)}, f32[4,40,128]{2,1,0:T(8,128)S(1)}, u32[]{:S(2)}, u32[]{:S(2)}) collective-permute-start(f32[4,40,128]{2,1,0:T(8,128)S(1)} %get-tuple-element.112.refs_1_), channel_id=1, source_target_pairs={{0,15},{1,0},{2,1},{3,2},{4,3},{5,4},{6,5},{7,6},{8,7},{9,8},{10,9... | collective-permute-start | bytes 245768 | tf_op jit(solution)/shard_map/ppermute | solution.py:666

commit v4 on v3

--- a/solution.py
+++ b/solution.py
@@ -83,10 +83,16 @@
             lax.fori_loop(0, count, step, 0)
 
 
+TWISTED = (0, 2, 3)
+
+
 class Level:
     def __init__(self, level, rho, ax, ay, d, e, g):
         self.level, self.rho, self.ax, self.ay, self.d, self.e, self.g = level, rho, ax, ay, d, e, g
         self.parts = range(len(ax))
+        self.twist = level in TWISTED
+        ends = [n if side == 0 else NZ - 1 - n for n in range(NZ // 2) for side in range(2)]
+        self.order = ends if self.twist else list(range(NZ))
 
     def faces(self, blocks):
         scale = spacing(self.level)
@@ -102,54 +108,87 @@
 
         run_blocks(blocks, body)
 
+    def before(self, k):
+        if self.twist and k >= 8:
+            return k + 1 if k + 1 < NZ else None
+        return k - 1 if k > 0 else None
+
+    def substitute(self, p, r, h, partial, emit):
+        def weight(k):
+            return self.g[p][k, pl.ds(r, h), :]
+
+        if not self.twist:
+            w = partial[NZ - 1]
+            emit(NZ - 1, w)
+            for k in range(NZ - 2, -1, -1):
+                w = partial[k] + weight(k) * w
+                emit(k, w)
+            return
+        w = self.e[p][0, pl.ds(r, h), :] * (partial[7] + weight(7) * partial[8])
+        emit(7, w)
+        x = partial[8] + weight(8) * w
+        emit(8, x)
+        for k in range(6, -1, -1):
+            w = partial[k] + weight(k) * w
+            emit(k, w)
+            x = partial[15 - k] + weight(15 - k) * x
+            emit(15 - k, x)
+
     def factor_and_first(self, blocks, inside, f, v):
         def body(r, h):
             masks = None if inside is None else [inside(r, h) for p in self.parts]
-            ratio = [None for p in self.parts]
-            partial = [[] for p in self.parts]
-            upper = [None for p in self.parts]
-            rho = [ref[0, pl.ds(r, h), :] for ref in self.rho]
-            for p in self.parts:
-                upper[p] = (2.0 * VERTICAL) * rcp(jnp.maximum(rho[p], TINY))
-            for k in range(NZ):
-                if k + 1 < NZ:
-                    below = [ref[k + 1, pl.ds(r, h), :] for ref in self.rho]
-                    lower = [
-                        (2.0 * VERTICAL) * rcp(jnp.maximum(rho[p] + below[p], TINY)) for p in self.parts
-                    ]
+            upper = {}
+
+            def upper_at(k):
+                if k not in upper:
+                    total = [ref[k, pl.ds(r, h), :] for ref in self.rho]
+                    if k > 0:
+                        total = [x + ref[k - 1, pl.ds(r, h), :] for x, ref in zip(total, self.rho)]
+                    upper[k] = [(2.0 * VERTICAL) * rcp(jnp.maximum(x, TINY)) for x in total]
+                return upper[k]
+
+            partial = [[None] * NZ for p in self.parts]
+            back = {}
+            for k in self.order:
+                above = upper_at(k)
+                below = upper_at(k + 1) if k + 1 < NZ else None
                 ay = [ref[k, pl.ds(r, h), :] for ref in self.ay]
                 right = from_right(ay)
+                upwards = self.twist and k >= 8
+                before = self.before(k)
                 for p in self.parts:
                     center = (
                         self.ax[p][k, pl.ds(r, h), :]
                         + self.ax[p][k, pl.ds(r + 1, h), :]
                         + ay[p]
                         + right[p]
-                        + upper[p]
+                        + above[p]
                     )
                     if k + 1 < NZ:
-                        center = center + lower[p]
-                    pivot = center if k == 0 else center - upper[p] * ratio[p]
+                        center = center + below[p]
+                    toward, away = (below, above) if upwards else (above, below)
+                    pivot = center if before is None else center - toward[p] * back[before, p]
                     inverse = rcp(pivot) if masks is None else jnp.where(masks[p], rcp(pivot), 0.0)
                     scaled = 0.8 * inverse
                     self.d[p][k, pl.ds(r, h), :] = scaled
                     value = scaled * f[p][k, pl.ds(r, h), :]
-                    if k > 0:
-                        weight = upper[p] * inverse
+                    if before is not None:
+                        weight = toward[p] * inverse
                         self.e[p][k, pl.ds(r, h), :] = weight
-                        value = value + weight * partial[p][-1]
-                    partial[p].append(value)
-                    if k + 1 < NZ:
-                        ratio[p] = lower[p] * inverse
-                        self.g[p][k, pl.ds(r, h), :] = ratio[p]
-                if k + 1 < NZ:
-                    rho, upper = below, lower
+                        value = value + weight * partial[p][before]
+                    partial[p][k] = value
+                    if away is not None:
+                        back[k, p] = away[p] * inverse
+                        self.g[p][k, pl.ds(r, h), :] = back[k, p]
+
             for p in self.parts:
-                w = partial[p][-1]
-                v[p][NZ - 1, pl.ds(r, h), :] = w
-                for k in range(NZ - 2, -1, -1):
-                    w = partial[p][k] + self.g[p][k, pl.ds(r, h), :] * w
+                if self.twist:
+                    self.e[p][0, pl.ds(r, h), :] = rcp(1.0 - back[7, p] * back[8, p])
+
+                def emit(k, w):
                     v[p][k, pl.ds(r, h), :] = w
+
+                self.substitute(p, r, h, partial[p], emit)
 
         run_blocks(blocks, body)
 
@@ -166,26 +205,27 @@
             for p in wanted
         ]
 
-    def relax(self, blocks, f, v, out, u=None, wanted=None, shift=0):
-        wanted = self.parts if wanted is None else wanted
-
+    def relax(self, blocks, f, v, out, u=None):
         def body(r, h):
-            partial = [[] for p in wanted]
-            for k in range(NZ):
-                pulls = self.pull(v, k, r, h, wanted)
-                for n, p in enumerate(wanted):
-                    value = self.d[p][k, pl.ds(r, h), :] * (f[p][k, pl.ds(r, h), :] + pulls[n])
-                    if k > 0:
-                        value = value + self.e[p][k, pl.ds(r, h), :] * partial[n][-1]
-                    partial[n].append(value)
-            for n, p in enumerate(wanted):
-                w = None
-                for k in range(NZ - 1, -1, -1):
-                    w = partial[n][k] if w is None else partial[n][k] + self.g[p][k, pl.ds(r, h), :] * w
+            partial = [[None] * NZ for p in self.parts]
+            for k in self.order:
+                pulls = self.pull(v, k, r, h, self.parts)
+                before = self.before(k)
+                for p in self.parts:
+                    value = self.d[p][k, pl.ds(r, h), :] * (f[p][k, pl.ds(r, h), :] + pulls[p])
+                    if before is not None:
+                        value = value + self.e[p][k, pl.ds(r, h), :] * partial[p][before]
+                    partial[p][k] = value
+
+            for p in self.parts:
+
+                def emit(k, w):
                     old = v[p][k, pl.ds(r, h), :]
-                    out[p][k, pl.ds(r - shift, h), :] = 0.2 * old + w
+                    out[p][k, pl.ds(r, h), :] = 0.2 * old + w
                     if u is not None:
                         u[p][k, pl.ds(r, h), :] = w - 0.6 * old
+
+                self.substitute(p, r, h, partial[p], emit)
 
         run_blocks(blocks, body)
 
@@ -242,21 +282,30 @@
     return ref[pl.ds(start * 2 * NZ + field * NZ + k, count, stride=2 * NZ), :]
 
 
-def edges_kernel(f_ref, rho_ref, up_ref, dn_ref, left_ref, right_ref):
-    for field, own in enumerate((f_ref, rho_ref)):
-        for piece in PIECES:
-            first, count = piece[:2]
-            slot = lanes_of((count, LANES)) // 16
-            for half in range(2):
-                lefts, rights = None, None
-                for q in range(8):
-                    x = piece_of(piece, field, half * 8 + q, own, up_ref, dn_ref)
-                    a = x if q == 0 else pltpu.roll(x, 16 * q, 1)
-                    b = pltpu.roll(x, 16 * q + 16, 1) if q < 7 else x
-                    lefts = a if q == 0 else jnp.where(slot == q, a, lefts)
-                    rights = b if q == 0 else jnp.where(slot == q, b, rights)
-                left_ref[field * 2 + half, pl.ds(first, count), :] = lefts
-                right_ref[field * 2 + half, pl.ds(first, count), :] = rights
+def pack_rows(piece, sources, left_ref, right_ref):
+    first, count = piece[:2]
+    slot = lanes_of((count, LANES)) // 16
+    for field in range(2):
+        for half in range(2):
+            lefts, rights = None, None
+            for q in range(8):
+                x = piece_of(piece, field, half * 8 + q, sources[field], *sources[2:])
+                a = x if q == 0 else pltpu.roll(x, 16 * q, 1)
+                b = pltpu.roll(x, 16 * q + 16, 1) if q < 7 else x
+                lefts = a if q == 0 else jnp.where(slot == q, a, lefts)
+                rights = b if q == 0 else jnp.where(slot == q, b, rights)
+            left_ref[field * 2 + half, pl.ds(first, count), :] = lefts
+            right_ref[field * 2 + half, pl.ds(first, count), :] = rights
+
+
+def own_edges_kernel(f_ref, rho_ref, left_ref, right_ref):
+    pack_rows(PIECES[2], (f_ref, rho_ref, None, None), left_ref, right_ref)
+
+
+def edges_kernel(up_ref, dn_ref, _, __, left_ref, right_ref):
+    for piece in PIECES:
+        if piece[2] != "own":
+            pack_rows(piece, (None, None, up_ref, dn_ref), left_ref, right_ref)
 
 
 def inner_kernel(f_ref, rho_ref, fm, vm, axm, aym, dm, em, gm, rm, firstm, um, resm):
@@ -473,7 +522,7 @@
     grid, tiles, index_ref, gathered, fm, vm, axm, aym, dm, em, gm, fh, vh, axh, ayh, dh, eh, gh,
     f1, v1, ax1, ay1, d1, e1, g1, f2, v2, ax2, ay2, d2, e2, g2, f3, v3, ax3, ay3, d3, e3, g3,
     out_ref,
-    rho4, f4, ax4, ay4, d4, e4, g4, c4, a4, va4, vb4, va3, vb3, va2, vb2, va1, vb1, vam, vah, vbm, vbh,
+    rho4, f4, ax4, ay4, d4, e4, g4, c4, a4, b4, v4, va3, vb3, va2, vb2, va1, vb1, vam, vah, vbm, vbh,
 ):
     ix, iy = index_ref[0], index_ref[1]
     grid_rows, grid_lanes = grid
@@ -482,7 +531,7 @@
     tiles_x, tiles_y = tiles
 
     zero = jnp.zeros((8, LANES), jnp.float32)
-    for ref in (rho4, va4, vb4):
+    for ref in (rho4, v4.at[0], v4.at[1]):
         for k in range(NZ):
             ref[k, pl.ds(0, 8), :] = zero
             ref[k, pl.ds(8 + rows4, 8), :] = zero
@@ -505,7 +554,7 @@
                     target.at[k][pl.ds(8 + 2 * base + r, count, stride=2), :] = x
 
     scale = spacing(4)
-    h = min(16, rows4)
+    h = min(32, rows4)
     first_lane, last_lane = lanes_of((h, LANES)) == 0, lanes_of((h, LANES)) == LANES - 1
     starts = list(range(8, 8 + rows4, h))
 
@@ -521,6 +570,7 @@
     def first_sweep(r):
         rho = rho4[0, pl.ds(r, h), :]
         upper = (2.0 * VERTICAL) * rcp(rho)
+        row = rows_of((h, LANES)) + r
         partial, ratio = [], None
         for k in range(NZ):
             here = rho4[k, pl.ds(r, h), :]
@@ -528,7 +578,11 @@
             ay = scale * rcp(here + left)
             right = jnp.where(last_lane, scale * rcp(here), pltpu.roll(ay, LANES - 1, 1))
             ay4[k, pl.ds(r, h), :] = jnp.where(first_lane, 0.0, ay)
-            center = ax4[k, pl.ds(r, h), :] + ax4[k, pl.ds(r + 1, h), :] + ay + right + upper
+            up, down = ax4[k, pl.ds(r, h), :], ax4[k, pl.ds(r + 1, h), :]
+            center = up + down + ay + right + upper
+            across = jnp.where(first_lane, ay, 0.0) + jnp.where(last_lane, right, 0.0)
+            along = jnp.where(row == 8, up, 0.0) + jnp.where(row == 7 + rows4, down, 0.0)
+            b4[k, pl.ds(r, h), :] = across + along
             if k + 1 < NZ:
                 lower = (2.0 * VERTICAL) * rcp(here + rho4[k + 1, pl.ds(r, h), :])
                 center = center + lower
@@ -549,10 +603,10 @@
                 g4[k, pl.ds(r, h), :] = ratio
                 upper = lower
         w = partial[-1]
-        va4[NZ - 1, pl.ds(r, h), :] = w
+        v4[0, NZ - 1, pl.ds(r, h), :] = w
         for k in range(NZ - 2, -1, -1):
             w = partial[k] + g4[k, pl.ds(r, h), :] * w
-            va4[k, pl.ds(r, h), :] = w
+            v4[0, k, pl.ds(r, h), :] = w
 
     for r in starts:
         first_sweep(r)
@@ -581,20 +635,24 @@
                 w = partial[k] if w is None else partial[k] + g4[k, pl.ds(r, h), :] * w
                 out[k, pl.ds(r, h), :] = 0.2 * v[k, pl.ds(r, h), :] + w
 
-    ends = [va4, vb4]
-    for number in range(SWEEPS - 1):
-        sweep(ends[number % 2], ends[(number + 1) % 2])
-    final = ends[(SWEEPS - 1) % 2]
-    shifts = []
+    def one_sweep(number, carry):
+        sweep(v4.at[number % 2], v4.at[1 - number % 2])
+        return carry
+
+    lax.fori_loop(0, SWEEPS - 1, one_sweep, 0)
+    final = v4.at[(SWEEPS - 1) % 2]
+
+    shifts, flux = [], [None] * len(starts)
     for k in range(NZ):
         left_over, weights = None, None
-        for r in starts:
+        for n, r in enumerate(starts):
+            v = final[k, pl.ds(r, h), :]
+            part = f4[k, pl.ds(r, h), :] - b4[k, pl.ds(r, h), :] * v
+            part = part - (a4[0, pl.ds(r, h), :] * v if k == 0 else flux[n])
+            if k + 1 < NZ:
+                flux[n] = a4[k + 1, pl.ds(r, h), :] * (final[k + 1, pl.ds(r, h), :] - v)
+                part = part + flux[n]
             center = c4[k, pl.ds(r, h), :]
-            part = pulled4(final, k, r) - center * final[k, pl.ds(r, h), :]
-            if k > 0:
-                part = part + a4[k, pl.ds(r, h), :] * final[k - 1, pl.ds(r, h), :]
-            if k + 1 < NZ:
-                part = part + a4[k + 1, pl.ds(r, h), :] * final[k + 1, pl.ds(r, h), :]
             left_over = part if left_over is None else left_over + part
             weights = center if weights is None else weights + center
         raised = jnp.sum(left_over, axis=(0, 1), keepdims=True)
@@ -711,7 +769,10 @@
         sh = (NZ, SIDE_ROWS, LANES)
         inner = call(inner_kernel, "inner", [big[0]] * 11, [], None, source, rho)
         strip = array(4, ROWS[0], LANES)
-        lefts, rights = call(edges_kernel, "edges", [strip, strip], [], None, source, rho, up, dn)
+        own_strips = call(own_edges_kernel, "own_edges", [strip, strip], [], None, source, rho)
+        lefts, rights = call(
+            edges_kernel, "edges", [strip, strip], [], None, up, dn, *own_strips, aliases={2: 0, 3: 1}
+        )
         from_left_strip = ring(rights, "gy", 1)
         from_right_strip = ring(lefts, "gy", -1)
         main = call(
@@ -746,7 +807,7 @@
             lambda *refs: top_kernel(grid, (tiles_x, tiles_y), *refs),
             "top",
             [array(NZ, 32, LANES)],
-            [s4] * 11 + [s3] * 2 + [s2] * 2 + [s1] * 2 + [s0, sh] * 2,
+            [s4] * 10 + [(2,) + s4] + [s3] * 2 + [s2] * 2 + [s1] * 2 + [s0, sh] * 2,
             index, gathered, *main_state, *fine[1:], *coarser[1:],
         )
         return pressure

time: 84.2 us -> 83.5 us (level)
    pallas_call x6 -> x7, Pallas kernels: 18.1 us -> 17.6 us  [call(): pl.pallas_call(kernel, out_shape=outs, in_specs=ins, out_specs=[vmem] * l...]
where the time goes in v4:
time: 83.5 us; the launch traced here: 83.3 us
  blocking collectives  29.4 us (35%)
  starting transfers between devices  24.6 us (29%)
  Pallas kernels  17.6 us (21%)
  waiting for transfers between devices  10.2 us (12%)
  other arithmetic  1.14 us (1%)
    all_to_all x2, blocking collectives, gather(): return lax.all_to_all(blocks, axis, 0, 0).reshape(size * x.shape[0], LANES)  29.4 us
    ppermute x10, starting transfers between devices, ring(): return lax.ppermute(x, axis, [(i, (i + step) % size) for i in range(size)])  24.6 us
    pallas_call x7, Pallas kernels, call(): pl.pallas_call(kernel, out_shape=outs, in_specs=ins, out_specs=[vmem] * l...  17.6 us
    ppermute x10, waiting for transfers between devices, ring(): return lax.ppermute(x, axis, [(i, (i + step) % size) for i in range(size)])  10.2 us
  transfers between devices with their start and end apart: 10, of which 5 were waited for; matrix products, arithmetic and copies ran while one was open for 0% of the time, Pallas kernels for 4%

profile of v4, /device:TPU:1, one launch (start us, length us, event | category | flops | bytes accessed | tf_op | source)
XLA Modules:
  0.0 83.3 jit_solution(14210869471725946606)
XLA Ops:
  0.0 1.1 %maximum_bitcast_fusion = f32[32,32,128]{2,0,1:T(8,128)S(1)} fusion(f32[16,32,128]{2,1,0:T(8,128)} %rho_ref.3, f32[16,32,128]{2,1,0:T(8,128)} %f_ref.3), kind=kLoop, calls=%fused_computation | loop fusion | flops 131072 | bytes 1048576 | tf_op jit(solution)/shard_map/transpose | solution.py:763
  1.1 0.0 copy-start.1
  1.1 0.1 copy.16
  1.2 0.0 copy-start
  1.2 2.1 %collective-permute-start = (f32[352,128]{1,0:T(8,128)S(1)}, f32[352,128]{1,0:T(8,128)S(1)}, u32[]{:S(2)}, u32[]{:S(2)}) collective-permute-start(f32[352,128]{1,0:T(8,128)S(1)} %bitcast.9), channel_id=1, source_target_pairs={{0,16},{16,32},{32,48},{48,64},{64,80},{80,96},{96,112},{112,128},... | collective-permute-start | bytes 540680 | tf_op jit(solution)/shard_map/ppermute | solution.py:724
  3.3 0.1 copy.17
  3.4 3.8 %collective-permute-start.1 = (f32[352,128]{1,0:T(8,128)S(1)}, f32[352,128]{1,0:T(8,128)S(1)}, u32[]{:S(2)}, u32[]{:S(2)}) collective-permute-start(f32[352,128]{1,0:T(8,128)S(1)} %bitcast.10), channel_id=1, source_target_pairs={{0,240},{16,0},{32,16},{48,32},{64,48},{80,64},{96,80},{112,96},{1... | collective-permute-start | bytes 540680 | tf_op jit(solution)/shard_map/ppermute | solution.py:724
  7.2 0.0 copy-done.1
  7.2 0.0 copy-done
  7.2 0.3 own_edges.1
  7.5 2.4 %collective-permute-done.refs_1_.up_ref = f32[352,128]{1,0:T(8,128)S(1)} collective-permute-done((f32[352,128]{1,0:T(8,128)S(1)}, f32[352,128]{1,0:T(8,128)S(1)}, u32[]{:S(2)}, u32[]{:S(2)}) %collective-permute-start) | collective-permute-done | bytes 180256 | tf_op jit(solution)/shard_map/ppermute | solution.py:724
  9.9 0.0 collective-permute-done.1.refs_2_.dn_ref
  9.9 0.3 edges.1
  10.3 3.4 %collective-permute-start.3 = (f32[4,64,128]{2,1,0:T(8,128)S(1)}, f32[4,64,128]{2,1,0:T(8,128)S(1)}, u32[]{:S(2)}, u32[]{:S(2)}) collective-permute-start(f32[4,64,128]{2,1,0:T(8,128)S(1)} %get-tuple-element.74.refs_3_), channel_id=1, source_target_pairs={{0,15},{1,0},{2,1},{3,2},{4,3},{5,4},{6,5},{7,6},{8,7},{9,8},{10,9... | collective-permute-start | bytes 393224 | tf_op jit(solution)/shard_map/ppermute | solution.py:724
  13.7 0.8 collective-permute-start.2
  14.5 1.1 %inner.1 = (f32[16,64,128]{2,1,0:T(8,128)S(1)}, f32[16,64,128]{2,1,0:T(8,128)S(1)}, f32[16,64,128]{2,1,0:T(8,128)S(1)}, f32[16,64,128]{2,1,0:T(8,128)S(1)}, f32[...) custom-call(f32[16,32,128]{2,1,0:T(8,128)S(1)} %copy-done.1, ...), custom_call_target="tpu_custom_call" | custom-call | flops 4000000 | bytes 4000000 | tf_op jit(solution)/shard_map/inner/pallas_call | solution.py:742
  15.6 0.1 pad_add_fusion.refs_0_
  15.7 1.8 %outer.1 = (f32[16,64,128]{2,1,0:T(8,128)S(1)}, f32[16,64,128]{2,1,0:T(8,128)S(1)}, f32[16,64,128]{2,1,0:T(8,128)S(1)}, f32[16,64,128]{2,1,0:T(8,128)S(1)}, f32[...) custom-call(s32[2]{0:T(128)S(1)} %pad_add_fusion.refs_0_, ...), custom_call_target="tpu_custom_call", output_to_operand_aliasing={{0}: (3, {}), {1}: (4, {}), {2}: (5, {}), {3}: (6, {}), {4}... | custom-call | flops 4000000 | bytes 4000000 | tf_op jit(solution)/shard_map/outer/pallas_call | solution.py:742
  17.5 0.0 collective-permute-done.3.refs_6_
  17.5 0.8 collective-permute-done.2.refs_5_
  18.4 3.2 %fine.1 = (f32[8,8,128]{2,1,0:T(8,128)S(1)}, f32[16,40,128]{2,1,0:T(8,128)S(1)}, f32[16,40,128]{2,1,0:T(8,128)S(1)}, f32[16,40,128]{2,1,0:T(8,128)S(1)}, f32[16,...) custom-call(s32[2]{0:T(128)S(1)} %pad_add_fusion.refs_0_, ...), custom_call_target="tpu_custom_call" | custom-call | flops 4000000 | bytes 4000000 | tf_op jit(solution)/shard_map/fine/pallas_call | solution.py:742
  21.6 0.1 collective-permute-start.4
  21.6 5.1 %collective-permute-start.7 = (f32[8,8,128]{2,1,0:T(8,128)S(1)}, f32[8,8,128]{2,1,0:T(8,128)S(1)}, u32[]{:S(2)}, u32[]{:S(2)}) collective-permute-start(f32[8,8,128]{2,1,0:T(8,128)S(1)} %get-tuple-element.76), channel_id=1, source_target_pairs={{0,224},{16,240},{32,0},{48,16},{64,32},{80,48},{96,64},{112,80},{... | collective-permute-start | bytes 98312 | tf_op jit(solution)/shard_map/ppermute | solution.py:724
  26.7 2.5 %collective-permute-start.6 = (f32[8,8,128]{2,1,0:T(8,128)S(1)}, f32[8,8,128]{2,1,0:T(8,128)S(1)}, u32[]{:S(2)}, u32[]{:S(2)}) collective-permute-start(f32[8,8,128]{2,1,0:T(8,128)S(1)} %get-tuple-element.76), channel_id=1, source_target_pairs={{0,240},{16,0},{32,16},{48,32},{64,48},{80,64},{96,80},{112,96},{1... | collective-permute-start | bytes 98312 | tf_op jit(solution)/shard_map/ppermute | solution.py:724
  29.2 0.0 collective-permute-start.5
  29.2 0.0 collective-permute-done.4
  29.2 6.1 %collective-permute-done.5 = f32[8,8,128]{2,1,0:T(8,128)S(1)} collective-permute-done((f32[8,8,128]{2,1,0:T(8,128)S(1)}, f32[8,8,128]{2,1,0:T(8,128)S(1)}, u32[]{:S(2)}, u32[]{:S(2)}) %collective-permute-start.5) | collective-permute-done | bytes 32800 | tf_op jit(solution)/shard_map/ppermute | solution.py:724
  35.3 0.0 collective-permute-done.6
  35.3 0.0 collective-permute-done.7
  35.4 2.8 %collective-permute-start.8 = (f32[4,40,128]{2,1,0:T(8,128)S(1)}, f32[4,40,128]{2,1,0:T(8,128)S(1)}, u32[]{:S(2)}, u32[]{:S(2)}) collective-permute-start(f32[4,40,128]{2,1,0:T(8,128)S(1)} %get-tuple-element.115.refs_2_), channel_id=1, source_target_pairs={{0,1},{1,2},{2,3},{3,4},{4,5},{5,6},{6,7},{7,8},{8,9},{9,10},{10,1... | collective-permute-start | bytes 245768 | tf_op jit(solution)/shard_map/ppermute | solution.py:724
  38.2 4.0 %collective-permute-start.9 = (f32[4,40,128]{2,1,0:T(8,128)S(1)}, f32[4,40,128]{2,1,0:T(8,128)S(1)}, u32[]{:S(2)}, u32[]{:S(2)}) collective-permute-start(f32[4,40,128]{2,1,0:T(8,128)S(1)} %get-tuple-element.116.refs_1_), channel_id=1, source_target_pairs={{0,15},{1,0},{2,1},{3,2},{4,3},{5,4},{6,5},{7,6},{8,7},{9,8},{10,9... | collective-permute-start | bytes 245768 | tf_op jit(solution)/shard_map/ppermute | solution.py:724
  42.2 0.7 collective-permute-done.8.refs_3_
  42.9 0.2 collective-permute-done.9.refs_4_
  43.1 3.4 %coarser.1 = (f32[4,128]{1,0:T(4,128)S(1)}, f32[16,40,128]{2,1,0:T(8,128)S(1)}, f32[16,40,128]{2,1,0:T(8,128)S(1)}, f32[16,40,128]{2,1,0:T(8,128)S(1)}, f32[16,4...) custom-call(s32[2]{0:T(128)S(1)} %pad_add_fusion.refs_0_, ...), custom_call_target="tpu_custom_call" | custom-call | flops 4000000 | bytes 4000000 | tf_op jit(solution)/shard_map/coarser/pallas_call | solution.py:742
  46.5 15.8 %all_to_all.10 = f32[16,4,128]{2,1,0:T(4,128)S(1)} all-to-all(f32[16,4,128]{2,1,0:T(4,128)S(1)} %broadcast_in_dim.6), channel_id=1, replica_groups=mesh['gx'=16,'gy'=16] {'gy'}, dimensions={0} | all-to-all | bytes 65536 | tf_op jit(solution)/shard_map/all_to_all | solution.py:730
  62.3 13.6 %all_to_all.11 = f32[16,64,128]{2,1,0:T(8,128)S(1)} all-to-all(f32[16,64,128]{2,1,0:T(8,128)S(1)} %broadcast_in_dim.15), channel_id=1, replica_groups=mesh['gx'=16,'gy'=16] {'gx'}, dimensions={0} | all-to-all | bytes 1048576 | tf_op jit(solution)/shard_map/all_to_all | solution.py:730
  75.9 7.4 %top.1 = f32[16,32,128]{2,1,0:T(8,128)} custom-call(s32[2]{0:T(128)S(1)} %pad_add_fusion.refs_0_, f32[1024,128]{1,0:T(8,128)S(1)} %bitcast.8, f32[16,64,128]{2,1,0:T(8,128)S(1)} %get-tuple-element.78.refs_2_, f32[16,64,128]{2,1,0:T(8,128)S(1)} %get-tuple-element.79.refs_3_, f32[16,64,128]{2,1,0:T(8,128)S(1)} %get-tuple-element.80.refs_4_, ...), custom_call_target="tpu_custom_call" | custom-call | flops 4000000 | bytes 4000000 | tf_op jit(solution)/shard_map/top/pallas_call | solution.py:742
  (8 shorter events, 0.1 us)
Async XLA Ops:
  1.1 6.1 %copy-start.1 = (f32[16,32,128]{2,1,0:T(8,128)S(1)}, f32[16,32,128]{2,1,0:T(8,128)}, u32[]{:S(2)}) copy-start(f32[16,32,128]{2,1,0:T(8,128)} %f_ref.3) | copy-start | bytes 786436
  1.2 6.0 %copy-start = (f32[16,32,128]{2,1,0:T(8,128)S(1)}, f32[16,32,128]{2,1,0:T(8,128)}, u32[]{:S(2)}) copy-start(f32[16,32,128]{2,1,0:T(8,128)} %rho_ref.3) | copy-start | bytes 786436
  1.2 8.7 %collective-permute-start = (f32[352,128]{1,0:T(8,128)S(1)}, f32[352,128]{1,0:T(8,128)S(1)}, u32[]{:S(2)}, u32[]{:S(2)}) collective-permute-start(f32[352,128]{1,0:T(8,128)S(1)} %bitcast.9), channel_id=1, source_target_pairs={{0,16},{16,32},{32,48},{48,64},{64,80},{80,96},{96,112},{112,128},... | collective-permute-start | bytes 540680 | tf_op jit(solution)/shard_map/ppermute | solution.py:724
  3.4 6.5 %collective-permute-start.1 = (f32[352,128]{1,0:T(8,128)S(1)}, f32[352,128]{1,0:T(8,128)S(1)}, u32[]{:S(2)}, u32[]{:S(2)}) collective-permute-start(f32[352,128]{1,0:T(8,128)S(1)} %bitcast.10), channel_id=1, source_target_pairs={{0,240},{16,0},{32,16},{48,32},{64,48},{80,64},{96,80},{112,96},{1... | collective-permute-start | bytes 540680 | tf_op jit(solution)/shard_map/ppermute | solution.py:724
  10.3 7.2 %collective-permute-start.3 = (f32[4,64,128]{2,1,0:T(8,128)S(1)}, f32[4,64,128]{2,1,0:T(8,128)S(1)}, u32[]{:S(2)}, u32[]{:S(2)}) collective-permute-start(f32[4,64,128]{2,1,0:T(8,128)S(1)} %get-tuple-element.74.refs_3_), channel_id=1, source_target_pairs={{0,15},{1,0},{2,1},{3,2},{4,3},{5,4},{6,5},{7,6},{8,7},{9,8},{10,9... | collective-permute-start | bytes 393224 | tf_op jit(solution)/shard_map/ppermute | solution.py:724
  13.7 4.6 %collective-permute-start.2 = (f32[4,64,128]{2,1,0:T(8,128)S(1)}, f32[4,64,128]{2,1,0:T(8,128)S(1)}, u32[]{:S(2)}, u32[]{:S(2)}) collective-permute-start(f32[4,64,128]{2,1,0:T(8,128)S(1)} %get-tuple-element.75.refs_4_), channel_id=1, source_target_pairs={{0,1},{1,2},{2,3},{3,4},{4,5},{5,6},{6,7},{7,8},{8,9},{9,10},{10,1... | collective-permute-start | bytes 393224 | tf_op jit(solution)/shard_map/ppermute | solution.py:724
  21.6 7.7 %collective-permute-start.4 = (f32[8,8,128]{2,1,0:T(8,128)S(1)}, f32[8,8,128]{2,1,0:T(8,128)S(1)}, u32[]{:S(2)}, u32[]{:S(2)}) collective-permute-start(f32[8,8,128]{2,1,0:T(8,128)S(1)} %get-tuple-element.76), channel_id=1, source_target_pairs={{0,32},{16,48},{32,64},{48,80},{64,96},{80,112},{96,128},{112,144}... | collective-permute-start | bytes 98312 | tf_op jit(solution)/shard_map/ppermute | solution.py:724
  21.6 13.7 %collective-permute-start.7 = (f32[8,8,128]{2,1,0:T(8,128)S(1)}, f32[8,8,128]{2,1,0:T(8,128)S(1)}, u32[]{:S(2)}, u32[]{:S(2)}) collective-permute-start(f32[8,8,128]{2,1,0:T(8,128)S(1)} %get-tuple-element.76), channel_id=1, source_target_pairs={{0,224},{16,240},{32,0},{48,16},{64,32},{80,48},{96,64},{112,80},{... | collective-permute-start | bytes 98312 | tf_op jit(solution)/shard_map/ppermute | solution.py:724
  26.7 8.6 %collective-permute-start.6 = (f32[8,8,128]{2,1,0:T(8,128)S(1)}, f32[8,8,128]{2,1,0:T(8,128)S(1)}, u32[]{:S(2)}, u32[]{:S(2)}) collective-permute-start(f32[8,8,128]{2,1,0:T(8,128)S(1)} %get-tuple-element.76), channel_id=1, source_target_pairs={{0,240},{16,0},{32,16},{48,32},{64,48},{80,64},{96,80},{112,96},{1... | collective-permute-start | bytes 98312 | tf_op jit(solution)/shard_map/ppermute | solution.py:724
  29.2 6.1 %collective-permute-start.5 = (f32[8,8,128]{2,1,0:T(8,128)S(1)}, f32[8,8,128]{2,1,0:T(8,128)S(1)}, u32[]{:S(2)}, u32[]{:S(2)}) collective-permute-start(f32[8,8,128]{2,1,0:T(8,128)S(1)} %get-tuple-element.76), channel_id=1, source_target_pairs={{0,16},{16,32},{32,48},{48,64},{64,80},{80,96},{96,112},{112,128},... | collective-permute-start | bytes 98312 | tf_op jit(solution)/shard_map/ppermute | solution.py:724
  35.4 7.5 %collective-permute-start.8 = (f32[4,40,128]{2,1,0:T(8,128)S(1)}, f32[4,40,128]{2,1,0:T(8,128)S(1)}, u32[]{:S(2)}, u32[]{:S(2)}) collective-permute-start(f32[4,40,128]{2,1,0:T(8,128)S(1)} %get-tuple-element.115.refs_2_), channel_id=1, source_target_pairs={{0,1},{1,2},{2,3},{3,4},{4,5},{5,6},{6,7},{7,8},{8,9},{9,10},{10,1... | collective-permute-start | bytes 245768 | tf_op jit(solution)/shard_map/ppermute | solution.py:724
  38.2 4.9 %collective-permute-start.9 = (f32[4,40,128]{2,1,0:T(8,128)S(1)}, f32[4,40,128]{2,1,0:T(8,128)S(1)}, u32[]{:S(2)}, u32[]{:S(2)}) collective-permute-start(f32[4,40,128]{2,1,0:T(8,128)S(1)} %get-tuple-element.116.refs_1_), channel_id=1, source_target_pairs={{0,15},{1,0},{2,1},{3,2},{4,3},{5,4},{6,5},{7,6},{8,7},{9,8},{10,9... | collective-permute-start | bytes 245768 | tf_op jit(solution)/shard_map/ppermute | solution.py:724

commit v5 on v4

--- a/solution.py
+++ b/solution.py
@@ -302,40 +302,34 @@
     pack_rows(PIECES[2], (f_ref, rho_ref, None, None), left_ref, right_ref)
 
 
-def edges_kernel(up_ref, dn_ref, _, __, left_ref, right_ref):
+def edges_kernel(up_ref, dn_ref, own_left, own_right, left_ref, right_ref):
+    left_ref[:, pl.ds(16, 32), :] = own_left[:, pl.ds(16, 32), :]
+    right_ref[:, pl.ds(16, 32), :] = own_right[:, pl.ds(16, 32), :]
     for piece in PIECES:
         if piece[2] != "own":
             pack_rows(piece, (None, None, up_ref, dn_ref), left_ref, right_ref)
 
 
-def inner_kernel(f_ref, rho_ref, fm, vm, axm, aym, dm, em, gm, rm, firstm, um, resm):
-    for k in range(NZ):
-        fm[k, pl.ds(16, 32), :] = f_ref[k, :, :]
-        rm[k, pl.ds(16, 32), :] = rho_ref[k, :, :]
-    main = Level(0, [rm], [axm], [aym], [dm], [em], [gm])
-    main.faces([(17, 16), (32, 16)])
-    main.factor_and_first([(17, 16), (31, 16)], None, [fm], [firstm])
-    main.relax([(18, 16), (30, 16)], [fm], [firstm], [vm], u=[um])
-    main.residual([(19, 16), (29, 16)], [fm], [um], [resm])
-
-
-def outer_kernel(grid, index_ref, near_ref, far_ref, *refs):
-    fm, vm, axm, aym, dm, em, gm, rm, firstm, um, resm = refs[11:]
+def main_kernel(
+    grid, index_ref, f_ref, rho_ref, up_ref, dn_ref,
+    fm, vm, axm, aym, dm, em, gm, rm, resm,
+    firstm, um,
+):
     ix, iy = index_ref[0], index_ref[1]
     inside = inside_of(0, ix, iy, grid + (32, 128))
-    for k in range(NZ):
-        for piece in PIECES:
-            if piece[2] == "own":
-                continue
-            first, count = piece[:2]
-            fm[k, pl.ds(first, count), :] = piece_of(piece, 0, k, None, near_ref, far_ref)
-            x = piece_of(piece, 1, k, None, near_ref, far_ref)
-            rm[k, pl.ds(first, count), :] = jnp.where(inside(first, count), x, 0.0)
+    for field, (own, target) in enumerate(((f_ref, fm), (rho_ref, rm))):
+        for k in range(NZ):
+            for piece in PIECES:
+                first, count, source, _ = piece
+                x = piece_of(piece, field, k, own, up_ref, dn_ref)
+                if field == 1 and source != "own":
+                    x = jnp.where(inside(first, count), x, 0.0)
+                target[k, pl.ds(first, count), :] = x
     main = Level(0, [rm], [axm], [aym], [dm], [em], [gm])
-    main.faces([(1, 16), (48, 16)])
-    main.factor_and_first([(1, 16), (47, 16)], inside, [fm], [firstm])
-    main.relax([(2, 16), (46, 16)], [fm], [firstm], [vm], u=[um])
-    main.residual([(3, 16), (45, 16)], [fm], [um], [resm])
+    main.faces([(6, 16, 3), (51, 8)])
+    main.factor_and_first([(6, 16, 3), (50, 8)], inside, [fm], [firstm])
+    main.relax([(7, 16, 3), (49, 8)], [fm], [firstm], [vm], u=[um])
+    main.residual([(8, 16, 3)], [fm], [um], [resm])
 
 
 def fine_kernel(
@@ -734,7 +728,7 @@
     return jax.ShapeDtypeStruct(shape, jnp.float32)
 
 
-def call(kernel, name, outs, scratch, index, *operands, aliases=None, cost=4000000):
+def call(kernel, name, outs, scratch, index, *operands, cost=4000000):
     vmem = pl.BlockSpec(memory_space=pltpu.VMEM)
     ins = [vmem] * len(operands)
     if index is not None:
@@ -746,7 +740,6 @@
         out_specs=[vmem] * len(outs),
         scratch_shapes=[pltpu.VMEM(shape, jnp.float32) for shape in scratch],
         compiler_params=pltpu.CompilerParams(vmem_limit_bytes=VMEM_BYTES),
-        input_output_aliases=aliases or {},
         cost_estimate=pl.CostEstimate(flops=cost, bytes_accessed=cost, transcendentals=0),
         name=name,
     )(*operands)
@@ -767,19 +760,15 @@
         dn = ring(lows, "gx", -1)
         s0, s1, s2, s3 = [x.shape for x in big]
         sh = (NZ, SIDE_ROWS, LANES)
-        inner = call(inner_kernel, "inner", [big[0]] * 11, [], None, source, rho)
         strip = array(4, ROWS[0], LANES)
         own_strips = call(own_edges_kernel, "own_edges", [strip, strip], [], None, source, rho)
-        lefts, rights = call(
-            edges_kernel, "edges", [strip, strip], [], None, up, dn, *own_strips, aliases={2: 0, 3: 1}
-        )
+        lefts, rights = call(edges_kernel, "edges", [strip, strip], [], None, up, dn, *own_strips)
         from_left_strip = ring(rights, "gy", 1)
         from_right_strip = ring(lefts, "gy", -1)
         main = call(
-            lambda *refs: outer_kernel(grid, *refs), "outer", [big[0]] * 11, [], index, up, dn, *inner,
-            aliases={3 + n: n for n in range(11)},
+            lambda *refs: main_kernel(grid, *refs), "main", [big[0]] * 9, [s0] * 2, index, source, rho, up, dn
         )
-        main_state, rho_main, residual_main = main[:7], main[7], main[10]
+        main_state, rho_main, residual_main = main[:7], main[7], main[8]
         fine = call(
             lambda *refs: fine_kernel(grid, *refs),
             "fine",

time: 83.5 us -> 83.4 us (level)
    pallas_call x7 -> x6, Pallas kernels: 17.6 us -> 17.8 us  [call(): pl.pallas_call(kernel, out_shape=outs, in_specs=ins, out_specs=[vmem] * l...]
where the time goes in v5:
time: 83.4 us; the launch traced here: 83.2 us
  blocking collectives  29.4 us (35%)
  starting transfers between devices  24.6 us (29%)
  Pallas kernels  17.8 us (21%)
  waiting for transfers between devices  9.96 us (12%)
  other arithmetic  1.14 us (1%)
    all_to_all x2, blocking collectives, gather(): return lax.all_to_all(blocks, axis, 0, 0).reshape(size * x.shape[0], LANES)  29.4 us
    ppermute x10, starting transfers between devices, ring(): return lax.ppermute(x, axis, [(i, (i + step) % size) for i in range(size)])  24.6 us
    pallas_call x6, Pallas kernels, call(): pl.pallas_call(kernel, out_shape=outs, in_specs=ins, out_specs=[vmem] * l...  17.8 us
    ppermute x10, waiting for transfers between devices, ring(): return lax.ppermute(x, axis, [(i, (i + step) % size) for i in range(size)])  9.96 us
  transfers between devices with their start and end apart: 10, of which 5 were waited for; matrix products, arithmetic and copies ran while one was open for 0% of the time, Pallas kernels for 4%

profile of v5, /device:TPU:1, one launch (start us, length us, event | category | flops | bytes accessed | tf_op | source)
XLA Modules:
  0.0 83.2 jit_solution(15376250292579167937)
XLA Ops:
  0.0 1.1 %maximum_bitcast_fusion = f32[32,32,128]{2,0,1:T(8,128)S(1)} fusion(f32[16,32,128]{2,1,0:T(8,128)} %rho_ref.1, f32[16,32,128]{2,1,0:T(8,128)} %f_ref.1), kind=kLoop, calls=%fused_computation | loop fusion | flops 131072 | bytes 1048576 | tf_op jit(solution)/shard_map/transpose | solution.py:756
  1.1 0.0 copy-start.1
  1.1 0.1 copy.3
  1.2 0.0 copy-start
  1.2 2.1 %collective-permute-start = (f32[352,128]{1,0:T(8,128)S(1)}, f32[352,128]{1,0:T(8,128)S(1)}, u32[]{:S(2)}, u32[]{:S(2)}) collective-permute-start(f32[352,128]{1,0:T(8,128)S(1)} %bitcast.9), channel_id=1, source_target_pairs={{0,16},{16,32},{32,48},{48,64},{64,80},{80,96},{96,112},{112,128},... | collective-permute-start | bytes 540680 | tf_op jit(solution)/shard_map/ppermute | solution.py:718
  3.3 0.1 copy.4
  3.4 3.8 %collective-permute-start.1 = (f32[352,128]{1,0:T(8,128)S(1)}, f32[352,128]{1,0:T(8,128)S(1)}, u32[]{:S(2)}, u32[]{:S(2)}) collective-permute-start(f32[352,128]{1,0:T(8,128)S(1)} %bitcast.10), channel_id=1, source_target_pairs={{0,240},{16,0},{32,16},{48,32},{64,48},{80,64},{96,80},{112,96},{1... | collective-permute-start | bytes 540680 | tf_op jit(solution)/shard_map/ppermute | solution.py:718
  7.2 0.0 copy-done.1
  7.2 0.0 copy-done
  7.2 0.3 own_edges.1
  7.5 2.4 %collective-permute-done.refs_3_.up_ref = f32[352,128]{1,0:T(8,128)S(1)} collective-permute-done((f32[352,128]{1,0:T(8,128)S(1)}, f32[352,128]{1,0:T(8,128)S(1)}, u32[]{:S(2)}, u32[]{:S(2)}) %collective-permute-start) | collective-permute-done | bytes 180256 | tf_op jit(solution)/shard_map/ppermute | solution.py:718
  9.9 0.0 collective-permute-done.1.refs_4_.dn_ref
  9.9 0.4 edges.1
  10.3 3.4 %collective-permute-start.3 = (f32[4,64,128]{2,1,0:T(8,128)S(1)}, f32[4,64,128]{2,1,0:T(8,128)S(1)}, u32[]{:S(2)}, u32[]{:S(2)}) collective-permute-start(f32[4,64,128]{2,1,0:T(8,128)S(1)} %get-tuple-element.52.refs_3_), channel_id=1, source_target_pairs={{0,15},{1,0},{2,1},{3,2},{4,3},{5,4},{6,5},{7,6},{8,7},{9,8},{10,9... | collective-permute-start | bytes 393224 | tf_op jit(solution)/shard_map/ppermute | solution.py:718
  13.7 0.8 collective-permute-start.2
  14.5 0.1 pad_add_fusion.refs_0_
  14.6 3.3 %main.1 = (f32[16,64,128]{2,1,0:T(8,128)S(1)}, f32[16,64,128]{2,1,0:T(8,128)S(1)}, f32[16,64,128]{2,1,0:T(8,128)S(1)}, f32[16,64,128]{2,1,0:T(8,128)S(1)}, f32[1...) custom-call(s32[2]{0:T(128)S(1)} %pad_add_fusion.refs_0_, ...), custom_call_target="tpu_custom_call" | custom-call | flops 4000000 | bytes 4000000 | tf_op jit(solution)/shard_map/main/pallas_call | solution.py:736
  17.8 0.0 collective-permute-done.3.refs_6_
  17.8 0.5 collective-permute-done.2.refs_5_
  18.4 3.2 %fine.1 = (f32[8,8,128]{2,1,0:T(8,128)S(1)}, f32[16,40,128]{2,1,0:T(8,128)S(1)}, f32[16,40,128]{2,1,0:T(8,128)S(1)}, f32[16,40,128]{2,1,0:T(8,128)S(1)}, f32[16,...) custom-call(s32[2]{0:T(128)S(1)} %pad_add_fusion.refs_0_, ...), custom_call_target="tpu_custom_call" | custom-call | flops 4000000 | bytes 4000000 | tf_op jit(solution)/shard_map/fine/pallas_call | solution.py:736
  21.5 0.1 collective-permute-start.4
  21.6 5.1 %collective-permute-start.7 = (f32[8,8,128]{2,1,0:T(8,128)S(1)}, f32[8,8,128]{2,1,0:T(8,128)S(1)}, u32[]{:S(2)}, u32[]{:S(2)}) collective-permute-start(f32[8,8,128]{2,1,0:T(8,128)S(1)} %get-tuple-element.54), channel_id=1, source_target_pairs={{0,224},{16,240},{32,0},{48,16},{64,32},{80,48},{96,64},{112,80},{... | collective-permute-start | bytes 98312 | tf_op jit(solution)/shard_map/ppermute | solution.py:718
  26.7 2.5 %collective-permute-start.6 = (f32[8,8,128]{2,1,0:T(8,128)S(1)}, f32[8,8,128]{2,1,0:T(8,128)S(1)}, u32[]{:S(2)}, u32[]{:S(2)}) collective-permute-start(f32[8,8,128]{2,1,0:T(8,128)S(1)} %get-tuple-element.54), channel_id=1, source_target_pairs={{0,240},{16,0},{32,16},{48,32},{64,48},{80,64},{96,80},{112,96},{1... | collective-permute-start | bytes 98312 | tf_op jit(solution)/shard_map/ppermute | solution.py:718
  29.2 0.0 collective-permute-start.5
  29.2 0.0 collective-permute-done.4
  29.2 6.1 %collective-permute-done.5 = f32[8,8,128]{2,1,0:T(8,128)S(1)} collective-permute-done((f32[8,8,128]{2,1,0:T(8,128)S(1)}, f32[8,8,128]{2,1,0:T(8,128)S(1)}, u32[]{:S(2)}, u32[]{:S(2)}) %collective-permute-start.5) | collective-permute-done | bytes 32800 | tf_op jit(solution)/shard_map/ppermute | solution.py:718
  35.3 0.0 collective-permute-done.6
  35.3 0.0 collective-permute-done.7
  35.4 2.8 %collective-permute-start.8 = (f32[4,40,128]{2,1,0:T(8,128)S(1)}, f32[4,40,128]{2,1,0:T(8,128)S(1)}, u32[]{:S(2)}, u32[]{:S(2)}) collective-permute-start(f32[4,40,128]{2,1,0:T(8,128)S(1)} %get-tuple-element.93.refs_2_), channel_id=1, source_target_pairs={{0,1},{1,2},{2,3},{3,4},{4,5},{5,6},{6,7},{7,8},{8,9},{9,10},{10,1... | collective-permute-start | bytes 245768 | tf_op jit(solution)/shard_map/ppermute | solution.py:718
  38.2 4.0 %collective-permute-start.9 = (f32[4,40,128]{2,1,0:T(8,128)S(1)}, f32[4,40,128]{2,1,0:T(8,128)S(1)}, u32[]{:S(2)}, u32[]{:S(2)}) collective-permute-start(f32[4,40,128]{2,1,0:T(8,128)S(1)} %get-tuple-element.94.refs_1_), channel_id=1, source_target_pairs={{0,15},{1,0},{2,1},{3,2},{4,3},{5,4},{6,5},{7,6},{8,7},{9,8},{10,9... | collective-permute-start | bytes 245768 | tf_op jit(solution)/shard_map/ppermute | solution.py:718
  42.1 0.7 collective-permute-done.8.refs_3_
  42.9 0.2 collective-permute-done.9.refs_4_
  43.1 3.3 %coarser.1 = (f32[4,128]{1,0:T(4,128)S(1)}, f32[16,40,128]{2,1,0:T(8,128)S(1)}, f32[16,40,128]{2,1,0:T(8,128)S(1)}, f32[16,40,128]{2,1,0:T(8,128)S(1)}, f32[16,4...) custom-call(s32[2]{0:T(128)S(1)} %pad_add_fusion.refs_0_, ...), custom_call_target="tpu_custom_call" | custom-call | flops 4000000 | bytes 4000000 | tf_op jit(solution)/shard_map/coarser/pallas_call | solution.py:736
  46.4 15.8 %all_to_all.10 = f32[16,4,128]{2,1,0:T(4,128)S(1)} all-to-all(f32[16,4,128]{2,1,0:T(4,128)S(1)} %broadcast_in_dim.6), channel_id=1, replica_groups=mesh['gx'=16,'gy'=16] {'gy'}, dimensions={0} | all-to-all | bytes 65536 | tf_op jit(solution)/shard_map/all_to_all | solution.py:724
  62.3 13.6 %all_to_all.11 = f32[16,64,128]{2,1,0:T(8,128)S(1)} all-to-all(f32[16,64,128]{2,1,0:T(8,128)S(1)} %broadcast_in_dim.15), channel_id=1, replica_groups=mesh['gx'=16,'gy'=16] {'gx'}, dimensions={0} | all-to-all | bytes 1048576 | tf_op jit(solution)/shard_map/all_to_all | solution.py:724
  75.8 7.4 %top.1 = f32[16,32,128]{2,1,0:T(8,128)} custom-call(s32[2]{0:T(128)S(1)} %pad_add_fusion.refs_0_, f32[1024,128]{1,0:T(8,128)S(1)} %bitcast.8, f32[16,64,128]{2,1,0:T(8,128)S(1)} %get-tuple-element.56.refs_2_, f32[16,64,128]{2,1,0:T(8,128)S(1)} %get-tuple-element.57.refs_3_, f32[16,64,128]{2,1,0:T(8,128)S(1)} %get-tuple-element.58.refs_4_, ...), custom_call_target="tpu_custom_call" | custom-call | flops 4000000 | bytes 4000000 | tf_op jit(solution)/shard_map/top/pallas_call | solution.py:736
  (8 shorter events, 0.1 us)
Async XLA Ops:
  1.1 6.1 %copy-start.1 = (f32[16,32,128]{2,1,0:T(8,128)S(1)}, f32[16,32,128]{2,1,0:T(8,128)}, u32[]{:S(2)}) copy-start(f32[16,32,128]{2,1,0:T(8,128)} %rho_ref.1) | copy-start | bytes 786436
  1.2 6.0 %copy-start = (f32[16,32,128]{2,1,0:T(8,128)S(1)}, f32[16,32,128]{2,1,0:T(8,128)}, u32[]{:S(2)}) copy-start(f32[16,32,128]{2,1,0:T(8,128)} %f_ref.1) | copy-start | bytes 786436
  1.2 8.7 %collective-permute-start = (f32[352,128]{1,0:T(8,128)S(1)}, f32[352,128]{1,0:T(8,128)S(1)}, u32[]{:S(2)}, u32[]{:S(2)}) collective-permute-start(f32[352,128]{1,0:T(8,128)S(1)} %bitcast.9), channel_id=1, source_target_pairs={{0,16},{16,32},{32,48},{48,64},{64,80},{80,96},{96,112},{112,128},... | collective-permute-start | bytes 540680 | tf_op jit(solution)/shard_map/ppermute | solution.py:718
  3.4 6.5 %collective-permute-start.1 = (f32[352,128]{1,0:T(8,128)S(1)}, f32[352,128]{1,0:T(8,128)S(1)}, u32[]{:S(2)}, u32[]{:S(2)}) collective-permute-start(f32[352,128]{1,0:T(8,128)S(1)} %bitcast.10), channel_id=1, source_target_pairs={{0,240},{16,0},{32,16},{48,32},{64,48},{80,64},{96,80},{112,96},{1... | collective-permute-start | bytes 540680 | tf_op jit(solution)/shard_map/ppermute | solution.py:718
  10.3 7.5 %collective-permute-start.3 = (f32[4,64,128]{2,1,0:T(8,128)S(1)}, f32[4,64,128]{2,1,0:T(8,128)S(1)}, u32[]{:S(2)}, u32[]{:S(2)}) collective-permute-start(f32[4,64,128]{2,1,0:T(8,128)S(1)} %get-tuple-element.52.refs_3_), channel_id=1, source_target_pairs={{0,15},{1,0},{2,1},{3,2},{4,3},{5,4},{6,5},{7,6},{8,7},{9,8},{10,9... | collective-permute-start | bytes 393224 | tf_op jit(solution)/shard_map/ppermute | solution.py:718
  13.7 4.6 %collective-permute-start.2 = (f32[4,64,128]{2,1,0:T(8,128)S(1)}, f32[4,64,128]{2,1,0:T(8,128)S(1)}, u32[]{:S(2)}, u32[]{:S(2)}) collective-permute-start(f32[4,64,128]{2,1,0:T(8,128)S(1)} %get-tuple-element.53.refs_4_), channel_id=1, source_target_pairs={{0,1},{1,2},{2,3},{3,4},{4,5},{5,6},{6,7},{7,8},{8,9},{9,10},{10,1... | collective-permute-start | bytes 393224 | tf_op jit(solution)/shard_map/ppermute | solution.py:718
  21.5 7.7 %collective-permute-start.4 = (f32[8,8,128]{2,1,0:T(8,128)S(1)}, f32[8,8,128]{2,1,0:T(8,128)S(1)}, u32[]{:S(2)}, u32[]{:S(2)}) collective-permute-start(f32[8,8,128]{2,1,0:T(8,128)S(1)} %get-tuple-element.54), channel_id=1, source_target_pairs={{0,32},{16,48},{32,64},{48,80},{64,96},{80,112},{96,128},{112,144}... | collective-permute-start | bytes 98312 | tf_op jit(solution)/shard_map/ppermute | solution.py:718
  21.6 13.7 %collective-permute-start.7 = (f32[8,8,128]{2,1,0:T(8,128)S(1)}, f32[8,8,128]{2,1,0:T(8,128)S(1)}, u32[]{:S(2)}, u32[]{:S(2)}) collective-permute-start(f32[8,8,128]{2,1,0:T(8,128)S(1)} %get-tuple-element.54), channel_id=1, source_target_pairs={{0,224},{16,240},{32,0},{48,16},{64,32},{80,48},{96,64},{112,80},{... | collective-permute-start | bytes 98312 | tf_op jit(solution)/shard_map/ppermute | solution.py:718
  26.7 8.6 %collective-permute-start.6 = (f32[8,8,128]{2,1,0:T(8,128)S(1)}, f32[8,8,128]{2,1,0:T(8,128)S(1)}, u32[]{:S(2)}, u32[]{:S(2)}) collective-permute-start(f32[8,8,128]{2,1,0:T(8,128)S(1)} %get-tuple-element.54), channel_id=1, source_target_pairs={{0,240},{16,0},{32,16},{48,32},{64,48},{80,64},{96,80},{112,96},{1... | collective-permute-start | bytes 98312 | tf_op jit(solution)/shard_map/ppermute | solution.py:718
  29.2 6.1 %collective-permute-start.5 = (f32[8,8,128]{2,1,0:T(8,128)S(1)}, f32[8,8,128]{2,1,0:T(8,128)S(1)}, u32[]{:S(2)}, u32[]{:S(2)}) collective-permute-start(f32[8,8,128]{2,1,0:T(8,128)S(1)} %get-tuple-element.54), channel_id=1, source_target_pairs={{0,16},{16,32},{32,48},{48,64},{64,80},{80,96},{96,112},{112,128},... | collective-permute-start | bytes 98312 | tf_op jit(solution)/shard_map/ppermute | solution.py:718
  35.4 7.5 %collective-permute-start.8 = (f32[4,40,128]{2,1,0:T(8,128)S(1)}, f32[4,40,128]{2,1,0:T(8,128)S(1)}, u32[]{:S(2)}, u32[]{:S(2)}) collective-permute-start(f32[4,40,128]{2,1,0:T(8,128)S(1)} %get-tuple-element.93.refs_2_), channel_id=1, source_target_pairs={{0,1},{1,2},{2,3},{3,4},{4,5},{5,6},{6,7},{7,8},{8,9},{9,10},{10,1... | collective-permute-start | bytes 245768 | tf_op jit(solution)/shard_map/ppermute | solution.py:718
  38.2 4.9 %collective-permute-start.9 = (f32[4,40,128]{2,1,0:T(8,128)S(1)}, f32[4,40,128]{2,1,0:T(8,128)S(1)}, u32[]{:S(2)}, u32[]{:S(2)}) collective-permute-start(f32[4,40,128]{2,1,0:T(8,128)S(1)} %get-tuple-element.94.refs_1_), channel_id=1, source_target_pairs={{0,15},{1,0},{2,1},{3,2},{4,3},{5,4},{6,5},{7,6},{8,7},{9,8},{10,9... | collective-permute-start | bytes 245768 | tf_op jit(solution)/shard_map/ppermute | solution.py:718

commit v6 on v5

--- a/solution.py
+++ b/solution.py
@@ -326,10 +326,10 @@
                     x = jnp.where(inside(first, count), x, 0.0)
                 target[k, pl.ds(first, count), :] = x
     main = Level(0, [rm], [axm], [aym], [dm], [em], [gm])
-    main.faces([(6, 16, 3), (51, 8)])
-    main.factor_and_first([(6, 16, 3), (50, 8)], inside, [fm], [firstm])
-    main.relax([(7, 16, 3), (49, 8)], [fm], [firstm], [vm], u=[um])
-    main.residual([(8, 16, 3)], [fm], [um], [resm])
+    main.faces([(6, 16), (22, 16), (38, 16), (51, 8)])
+    main.factor_and_first([(6, 16), (22, 16), (38, 16), (50, 8)], inside, [fm], [firstm])
+    main.relax([(7, 16), (23, 16), (39, 16), (49, 8)], [fm], [firstm], [vm], u=[um])
+    main.residual([(8, 16), (24, 16), (40, 16)], [fm], [um], [resm])
 
 
 def fine_kernel(

time: 83.4 us -> 83.4 us (level)
  Pallas kernels: 17.8 us -> 16.9 us
  waiting for transfers between devices: 9.96 us -> 10.8 us
    ppermute x10, waiting for transfers between devices: 9.96 us -> 10.8 us  [ring(): return lax.ppermute(x, axis, [(i, (i + step) % size) for i in range(size)])]
    pallas_call x6, Pallas kernels: 17.8 us -> 16.9 us  [call(): pl.pallas_call(kernel, out_shape=outs, in_specs=ins, out_specs=[vmem] * l...]
  transfers between devices with their start and end apart: 10 -> 10, of which waited for: 5 -> 6; matrix products, arithmetic and copies ran while one was open for 0% -> 0% of each run, Pallas kernels for 4% -> 3%
where the time goes in v6:
time: 83.4 us; the launch traced here: 83.2 us
  blocking collectives  29.4 us (35%)
  starting transfers between devices  24.6 us (29%)
  Pallas kernels  16.9 us (20%)
  waiting for transfers between devices  10.8 us (13%)
  other arithmetic  1.14 us (1%)
    all_to_all x2, blocking collectives, gather(): return lax.all_to_all(blocks, axis, 0, 0).reshape(size * x.shape[0], LANES)  29.4 us
    ppermute x10, starting transfers between devices, ring(): return lax.ppermute(x, axis, [(i, (i + step) % size) for i in range(size)])  24.6 us
    pallas_call x6, Pallas kernels, call(): pl.pallas_call(kernel, out_shape=outs, in_specs=ins, out_specs=[vmem] * l...  16.9 us
    ppermute x10, waiting for transfers between devices, ring(): return lax.ppermute(x, axis, [(i, (i + step) % size) for i in range(size)])  10.8 us
  transfers between devices with their start and end apart: 10, of which 6 were waited for; matrix products, arithmetic and copies ran while one was open for 0% of the time, Pallas kernels for 3%

profile of v6, /device:TPU:1, one launch (start us, length us, event | category | flops | bytes accessed | tf_op | source)
XLA Modules:
  0.0 83.2 jit_solution(4601633260939132821)
XLA Ops:
  0.0 1.1 %maximum_bitcast_fusion = f32[32,32,128]{2,0,1:T(8,128)S(1)} fusion(f32[16,32,128]{2,1,0:T(8,128)} %rho_ref.1, f32[16,32,128]{2,1,0:T(8,128)} %f_ref.1), kind=kLoop, calls=%fused_computation | loop fusion | flops 131072 | bytes 1048576 | tf_op jit(solution)/shard_map/transpose | solution.py:756
  1.1 0.0 copy-start.1
  1.1 0.1 copy.3
  1.2 0.0 copy-start
  1.2 2.1 %collective-permute-start = (f32[352,128]{1,0:T(8,128)S(1)}, f32[352,128]{1,0:T(8,128)S(1)}, u32[]{:S(2)}, u32[]{:S(2)}) collective-permute-start(f32[352,128]{1,0:T(8,128)S(1)} %bitcast.9), channel_id=1, source_target_pairs={{0,16},{16,32},{32,48},{48,64},{64,80},{80,96},{96,112},{112,128},... | collective-permute-start | bytes 540680 | tf_op jit(solution)/shard_map/ppermute | solution.py:718
  3.3 0.1 copy.4
  3.4 3.8 %collective-permute-start.1 = (f32[352,128]{1,0:T(8,128)S(1)}, f32[352,128]{1,0:T(8,128)S(1)}, u32[]{:S(2)}, u32[]{:S(2)}) collective-permute-start(f32[352,128]{1,0:T(8,128)S(1)} %bitcast.10), channel_id=1, source_target_pairs={{0,240},{16,0},{32,16},{48,32},{64,48},{80,64},{96,80},{112,96},{1... | collective-permute-start | bytes 540680 | tf_op jit(solution)/shard_map/ppermute | solution.py:718
  7.2 0.0 copy-done.1
  7.2 0.0 copy-done
  7.2 0.3 own_edges.1
  7.5 2.4 %collective-permute-done.refs_3_.up_ref = f32[352,128]{1,0:T(8,128)S(1)} collective-permute-done((f32[352,128]{1,0:T(8,128)S(1)}, f32[352,128]{1,0:T(8,128)S(1)}, u32[]{:S(2)}, u32[]{:S(2)}) %collective-permute-start) | collective-permute-done | bytes 180256 | tf_op jit(solution)/shard_map/ppermute | solution.py:718
  9.9 0.0 collective-permute-done.1.refs_4_.dn_ref
  9.9 0.4 edges.1
  10.3 3.4 %collective-permute-start.3 = (f32[4,64,128]{2,1,0:T(8,128)S(1)}, f32[4,64,128]{2,1,0:T(8,128)S(1)}, u32[]{:S(2)}, u32[]{:S(2)}) collective-permute-start(f32[4,64,128]{2,1,0:T(8,128)S(1)} %get-tuple-element.52.refs_3_), channel_id=1, source_target_pairs={{0,15},{1,0},{2,1},{3,2},{4,3},{5,4},{6,5},{7,6},{8,7},{9,8},{10,9... | collective-permute-start | bytes 393224 | tf_op jit(solution)/shard_map/ppermute | solution.py:718
  13.7 0.8 collective-permute-start.2
  14.5 0.1 pad_add_fusion.refs_0_
  14.6 2.4 %main.1 = (f32[16,64,128]{2,1,0:T(8,128)S(1)}, f32[16,64,128]{2,1,0:T(8,128)S(1)}, f32[16,64,128]{2,1,0:T(8,128)S(1)}, f32[16,64,128]{2,1,0:T(8,128)S(1)}, f32[1...) custom-call(s32[2]{0:T(128)S(1)} %pad_add_fusion.refs_0_, ...), custom_call_target="tpu_custom_call" | custom-call | flops 4000000 | bytes 4000000 | tf_op jit(solution)/shard_map/main/pallas_call | solution.py:736
  17.0 0.1 collective-permute-done.3.refs_6_
  17.1 1.3 %collective-permute-done.2.refs_5_ = f32[4,64,128]{2,1,0:T(8,128)S(1)} collective-permute-done((f32[4,64,128]{2,1,0:T(8,128)S(1)}, f32[4,64,128]{2,1,0:T(8,128)S(1)}, u32[]{:S(2)}, u32[]{:S(2)}) %collective-permute-start.2) | collective-permute-done | bytes 131104 | tf_op jit(solution)/shard_map/ppermute | solution.py:718
  18.4 3.2 %fine.1 = (f32[8,8,128]{2,1,0:T(8,128)S(1)}, f32[16,40,128]{2,1,0:T(8,128)S(1)}, f32[16,40,128]{2,1,0:T(8,128)S(1)}, f32[16,40,128]{2,1,0:T(8,128)S(1)}, f32[16,...) custom-call(s32[2]{0:T(128)S(1)} %pad_add_fusion.refs_0_, ...), custom_call_target="tpu_custom_call" | custom-call | flops 4000000 | bytes 4000000 | tf_op jit(solution)/shard_map/fine/pallas_call | solution.py:736
  21.5 0.1 collective-permute-start.4
  21.6 5.1 %collective-permute-start.7 = (f32[8,8,128]{2,1,0:T(8,128)S(1)}, f32[8,8,128]{2,1,0:T(8,128)S(1)}, u32[]{:S(2)}, u32[]{:S(2)}) collective-permute-start(f32[8,8,128]{2,1,0:T(8,128)S(1)} %get-tuple-element.54), channel_id=1, source_target_pairs={{0,224},{16,240},{32,0},{48,16},{64,32},{80,48},{96,64},{112,80},{... | collective-permute-start | bytes 98312 | tf_op jit(solution)/shard_map/ppermute | solution.py:718
  26.7 2.5 %collective-permute-start.6 = (f32[8,8,128]{2,1,0:T(8,128)S(1)}, f32[8,8,128]{2,1,0:T(8,128)S(1)}, u32[]{:S(2)}, u32[]{:S(2)}) collective-permute-start(f32[8,8,128]{2,1,0:T(8,128)S(1)} %get-tuple-element.54), channel_id=1, source_target_pairs={{0,240},{16,0},{32,16},{48,32},{64,48},{80,64},{96,80},{112,96},{1... | collective-permute-start | bytes 98312 | tf_op jit(solution)/shard_map/ppermute | solution.py:718
  29.2 0.0 collective-permute-start.5
  29.2 0.0 collective-permute-done.4
  29.2 6.1 %collective-permute-done.5 = f32[8,8,128]{2,1,0:T(8,128)S(1)} collective-permute-done((f32[8,8,128]{2,1,0:T(8,128)S(1)}, f32[8,8,128]{2,1,0:T(8,128)S(1)}, u32[]{:S(2)}, u32[]{:S(2)}) %collective-permute-start.5) | collective-permute-done | bytes 32800 | tf_op jit(solution)/shard_map/ppermute | solution.py:718
  35.3 0.0 collective-permute-done.6
  35.3 0.0 collective-permute-done.7
  35.4 2.8 %collective-permute-start.8 = (f32[4,40,128]{2,1,0:T(8,128)S(1)}, f32[4,40,128]{2,1,0:T(8,128)S(1)}, u32[]{:S(2)}, u32[]{:S(2)}) collective-permute-start(f32[4,40,128]{2,1,0:T(8,128)S(1)} %get-tuple-element.93.refs_2_), channel_id=1, source_target_pairs={{0,1},{1,2},{2,3},{3,4},{4,5},{5,6},{6,7},{7,8},{8,9},{9,10},{10,1... | collective-permute-start | bytes 245768 | tf_op jit(solution)/shard_map/ppermute | solution.py:718
  38.2 4.0 %collective-permute-start.9 = (f32[4,40,128]{2,1,0:T(8,128)S(1)}, f32[4,40,128]{2,1,0:T(8,128)S(1)}, u32[]{:S(2)}, u32[]{:S(2)}) collective-permute-start(f32[4,40,128]{2,1,0:T(8,128)S(1)} %get-tuple-element.94.refs_1_), channel_id=1, source_target_pairs={{0,15},{1,0},{2,1},{3,2},{4,3},{5,4},{6,5},{7,6},{8,7},{9,8},{10,9... | collective-permute-start | bytes 245768 | tf_op jit(solution)/shard_map/ppermute | solution.py:718
  42.1 0.7 collective-permute-done.8.refs_3_
  42.9 0.2 collective-permute-done.9.refs_4_
  43.1 3.3 %coarser.1 = (f32[4,128]{1,0:T(4,128)S(1)}, f32[16,40,128]{2,1,0:T(8,128)S(1)}, f32[16,40,128]{2,1,0:T(8,128)S(1)}, f32[16,40,128]{2,1,0:T(8,128)S(1)}, f32[16,4...) custom-call(s32[2]{0:T(128)S(1)} %pad_add_fusion.refs_0_, ...), custom_call_target="tpu_custom_call" | custom-call | flops 4000000 | bytes 4000000 | tf_op jit(solution)/shard_map/coarser/pallas_call | solution.py:736
  46.4 15.8 %all_to_all.10 = f32[16,4,128]{2,1,0:T(4,128)S(1)} all-to-all(f32[16,4,128]{2,1,0:T(4,128)S(1)} %broadcast_in_dim.6), channel_id=1, replica_groups=mesh['gx'=16,'gy'=16] {'gy'}, dimensions={0} | all-to-all | bytes 65536 | tf_op jit(solution)/shard_map/all_to_all | solution.py:724
  62.3 13.6 %all_to_all.11 = f32[16,64,128]{2,1,0:T(8,128)S(1)} all-to-all(f32[16,64,128]{2,1,0:T(8,128)S(1)} %broadcast_in_dim.15), channel_id=1, replica_groups=mesh['gx'=16,'gy'=16] {'gx'}, dimensions={0} | all-to-all | bytes 1048576 | tf_op jit(solution)/shard_map/all_to_all | solution.py:724
  75.8 7.4 %top.1 = f32[16,32,128]{2,1,0:T(8,128)} custom-call(s32[2]{0:T(128)S(1)} %pad_add_fusion.refs_0_, f32[1024,128]{1,0:T(8,128)S(1)} %bitcast.8, f32[16,64,128]{2,1,0:T(8,128)S(1)} %get-tuple-element.56.refs_2_, f32[16,64,128]{2,1,0:T(8,128)S(1)} %get-tuple-element.57.refs_3_, f32[16,64,128]{2,1,0:T(8,128)S(1)} %get-tuple-element.58.refs_4_, ...), custom_call_target="tpu_custom_call" | custom-call | flops 4000000 | bytes 4000000 | tf_op jit(solution)/shard_map/top/pallas_call | solution.py:736
  (8 shorter events, 0.1 us)
Async XLA Ops:
  1.1 6.1 %copy-start.1 = (f32[16,32,128]{2,1,0:T(8,128)S(1)}, f32[16,32,128]{2,1,0:T(8,128)}, u32[]{:S(2)}) copy-start(f32[16,32,128]{2,1,0:T(8,128)} %rho_ref.1) | copy-start | bytes 786436
  1.2 6.0 %copy-start = (f32[16,32,128]{2,1,0:T(8,128)S(1)}, f32[16,32,128]{2,1,0:T(8,128)}, u32[]{:S(2)}) copy-start(f32[16,32,128]{2,1,0:T(8,128)} %f_ref.1) | copy-start | bytes 786436
  1.2 8.7 %collective-permute-start = (f32[352,128]{1,0:T(8,128)S(1)}, f32[352,128]{1,0:T(8,128)S(1)}, u32[]{:S(2)}, u32[]{:S(2)}) collective-permute-start(f32[352,128]{1,0:T(8,128)S(1)} %bitcast.9), channel_id=1, source_target_pairs={{0,16},{16,32},{32,48},{48,64},{64,80},{80,96},{96,112},{112,128},... | collective-permute-start | bytes 540680 | tf_op jit(solution)/shard_map/ppermute | solution.py:718
  3.4 6.5 %collective-permute-start.1 = (f32[352,128]{1,0:T(8,128)S(1)}, f32[352,128]{1,0:T(8,128)S(1)}, u32[]{:S(2)}, u32[]{:S(2)}) collective-permute-start(f32[352,128]{1,0:T(8,128)S(1)} %bitcast.10), channel_id=1, source_target_pairs={{0,240},{16,0},{32,16},{48,32},{64,48},{80,64},{96,80},{112,96},{1... | collective-permute-start | bytes 540680 | tf_op jit(solution)/shard_map/ppermute | solution.py:718
  10.3 6.8 %collective-permute-start.3 = (f32[4,64,128]{2,1,0:T(8,128)S(1)}, f32[4,64,128]{2,1,0:T(8,128)S(1)}, u32[]{:S(2)}, u32[]{:S(2)}) collective-permute-start(f32[4,64,128]{2,1,0:T(8,128)S(1)} %get-tuple-element.52.refs_3_), channel_id=1, source_target_pairs={{0,15},{1,0},{2,1},{3,2},{4,3},{5,4},{6,5},{7,6},{8,7},{9,8},{10,9... | collective-permute-start | bytes 393224 | tf_op jit(solution)/shard_map/ppermute | solution.py:718
  13.7 4.6 %collective-permute-start.2 = (f32[4,64,128]{2,1,0:T(8,128)S(1)}, f32[4,64,128]{2,1,0:T(8,128)S(1)}, u32[]{:S(2)}, u32[]{:S(2)}) collective-permute-start(f32[4,64,128]{2,1,0:T(8,128)S(1)} %get-tuple-element.53.refs_4_), channel_id=1, source_target_pairs={{0,1},{1,2},{2,3},{3,4},{4,5},{5,6},{6,7},{7,8},{8,9},{9,10},{10,1... | collective-permute-start | bytes 393224 | tf_op jit(solution)/shard_map/ppermute | solution.py:718
  21.5 7.7 %collective-permute-start.4 = (f32[8,8,128]{2,1,0:T(8,128)S(1)}, f32[8,8,128]{2,1,0:T(8,128)S(1)}, u32[]{:S(2)}, u32[]{:S(2)}) collective-permute-start(f32[8,8,128]{2,1,0:T(8,128)S(1)} %get-tuple-element.54), channel_id=1, source_target_pairs={{0,32},{16,48},{32,64},{48,80},{64,96},{80,112},{96,128},{112,144}... | collective-permute-start | bytes 98312 | tf_op jit(solution)/shard_map/ppermute | solution.py:718
  21.6 13.7 %collective-permute-start.7 = (f32[8,8,128]{2,1,0:T(8,128)S(1)}, f32[8,8,128]{2,1,0:T(8,128)S(1)}, u32[]{:S(2)}, u32[]{:S(2)}) collective-permute-start(f32[8,8,128]{2,1,0:T(8,128)S(1)} %get-tuple-element.54), channel_id=1, source_target_pairs={{0,224},{16,240},{32,0},{48,16},{64,32},{80,48},{96,64},{112,80},{... | collective-permute-start | bytes 98312 | tf_op jit(solution)/shard_map/ppermute | solution.py:718
  26.7 8.6 %collective-permute-start.6 = (f32[8,8,128]{2,1,0:T(8,128)S(1)}, f32[8,8,128]{2,1,0:T(8,128)S(1)}, u32[]{:S(2)}, u32[]{:S(2)}) collective-permute-start(f32[8,8,128]{2,1,0:T(8,128)S(1)} %get-tuple-element.54), channel_id=1, source_target_pairs={{0,240},{16,0},{32,16},{48,32},{64,48},{80,64},{96,80},{112,96},{1... | collective-permute-start | bytes 98312 | tf_op jit(solution)/shard_map/ppermute | solution.py:718
  29.2 6.1 %collective-permute-start.5 = (f32[8,8,128]{2,1,0:T(8,128)S(1)}, f32[8,8,128]{2,1,0:T(8,128)S(1)}, u32[]{:S(2)}, u32[]{:S(2)}) collective-permute-start(f32[8,8,128]{2,1,0:T(8,128)S(1)} %get-tuple-element.54), channel_id=1, source_target_pairs={{0,16},{16,32},{32,48},{48,64},{64,80},{80,96},{96,112},{112,128},... | collective-permute-start | bytes 98312 | tf_op jit(solution)/shard_map/ppermute | solution.py:718
  35.4 7.5 %collective-permute-start.8 = (f32[4,40,128]{2,1,0:T(8,128)S(1)}, f32[4,40,128]{2,1,0:T(8,128)S(1)}, u32[]{:S(2)}, u32[]{:S(2)}) collective-permute-start(f32[4,40,128]{2,1,0:T(8,128)S(1)} %get-tuple-element.93.refs_2_), channel_id=1, source_target_pairs={{0,1},{1,2},{2,3},{3,4},{4,5},{5,6},{6,7},{7,8},{8,9},{9,10},{10,1... | collective-permute-start | bytes 245768 | tf_op jit(solution)/shard_map/ppermute | solution.py:718
  38.2 4.9 %collective-permute-start.9 = (f32[4,40,128]{2,1,0:T(8,128)S(1)}, f32[4,40,128]{2,1,0:T(8,128)S(1)}, u32[]{:S(2)}, u32[]{:S(2)}) collective-permute-start(f32[4,40,128]{2,1,0:T(8,128)S(1)} %get-tuple-element.94.refs_1_), channel_id=1, source_target_pairs={{0,15},{1,0},{2,1},{3,2},{4,3},{5,4},{6,5},{7,6},{8,7},{9,8},{10,9... | collective-permute-start | bytes 245768 | tf_op jit(solution)/shard_map/ppermute | solution.py:718

commit v7 on v6

--- a/solution.py
+++ b/solution.py
@@ -703,8 +703,8 @@
     sides.relax([(7, 16), (17, 16)], [fh], [vah], [vbh])
     sides.relax([(8, 24)], [fh], [vbh], [vah])
     main = Level(0, None, [axm], [aym], [dm], [em], [gm])
-    main.relax([(15, 16, 2), (41, 8)], [fm], [vam], [vbm])
-    main.relax([(16, 16, 2)], [fm], [vbm], [vam])
+    main.relax([(15, 16), (31, 16), (41, 8)], [fm], [vam], [vbm])
+    main.relax([(16, 16), (32, 16)], [fm], [vbm], [vam])
     for k in range(NZ):
         for row, start, low, high in ((0, 16, 112, 80), (16, 16 - SPLIT + 16, 48, 16)):
             side = vah[k, pl.ds(start, 16), :]

time: 83.4 us -> 83.1 us (level)
  no operation moved by 1% of the time
where the time goes in v7:
time: 83.1 us; the launch traced here: 83 us
  blocking collectives  29.4 us (35%)
  starting transfers between devices  24.6 us (30%)
  Pallas kernels  16.6 us (20%)
  waiting for transfers between devices  10.8 us (13%)
  other arithmetic  1.14 us (1%)
    all_to_all x2, blocking collectives, gather(): return lax.all_to_all(blocks, axis, 0, 0).reshape(size * x.shape[0], LANES)  29.4 us
    ppermute x10, starting transfers between devices, ring(): return lax.ppermute(x, axis, [(i, (i + step) % size) for i in range(size)])  24.6 us
    pallas_call x6, Pallas kernels, call(): pl.pallas_call(kernel, out_shape=outs, in_specs=ins, out_specs=[vmem] * l...  16.6 us
    ppermute x10, waiting for transfers between devices, ring(): return lax.ppermute(x, axis, [(i, (i + step) % size) for i in range(size)])  10.8 us
  transfers between devices with their start and end apart: 10, of which 6 were waited for; matrix products, arithmetic and copies ran while one was open for 0% of the time, Pallas kernels for 3%

profile of v7, /device:TPU:1, one launch (start us, length us, event | category | flops | bytes accessed | tf_op | source)
XLA Modules:
  0.0 83.0 jit_solution(9120723477236667236)
XLA Ops:
  0.0 1.1 %maximum_bitcast_fusion = f32[32,32,128]{2,0,1:T(8,128)S(1)} fusion(f32[16,32,128]{2,1,0:T(8,128)} %rho_ref.1, f32[16,32,128]{2,1,0:T(8,128)} %f_ref.1), kind=kLoop, calls=%fused_computation | loop fusion | flops 131072 | bytes 1048576 | tf_op jit(solution)/shard_map/transpose | solution.py:756
  1.1 0.0 copy-start.1
  1.1 0.1 copy.3
  1.2 0.0 copy-start
  1.2 2.1 %collective-permute-start = (f32[352,128]{1,0:T(8,128)S(1)}, f32[352,128]{1,0:T(8,128)S(1)}, u32[]{:S(2)}, u32[]{:S(2)}) collective-permute-start(f32[352,128]{1,0:T(8,128)S(1)} %bitcast.9), channel_id=1, source_target_pairs={{0,16},{16,32},{32,48},{48,64},{64,80},{80,96},{96,112},{112,128},... | collective-permute-start | bytes 540680 | tf_op jit(solution)/shard_map/ppermute | solution.py:718
  3.3 0.1 copy.4
  3.4 3.8 %collective-permute-start.1 = (f32[352,128]{1,0:T(8,128)S(1)}, f32[352,128]{1,0:T(8,128)S(1)}, u32[]{:S(2)}, u32[]{:S(2)}) collective-permute-start(f32[352,128]{1,0:T(8,128)S(1)} %bitcast.10), channel_id=1, source_target_pairs={{0,240},{16,0},{32,16},{48,32},{64,48},{80,64},{96,80},{112,96},{1... | collective-permute-start | bytes 540680 | tf_op jit(solution)/shard_map/ppermute | solution.py:718
  7.2 0.0 copy-done.1
  7.2 0.0 copy-done
  7.2 0.3 own_edges.1
  7.5 2.4 %collective-permute-done.refs_3_.up_ref = f32[352,128]{1,0:T(8,128)S(1)} collective-permute-done((f32[352,128]{1,0:T(8,128)S(1)}, f32[352,128]{1,0:T(8,128)S(1)}, u32[]{:S(2)}, u32[]{:S(2)}) %collective-permute-start) | collective-permute-done | bytes 180256 | tf_op jit(solution)/shard_map/ppermute | solution.py:718
  9.9 0.0 collective-permute-done.1.refs_4_.dn_ref
  9.9 0.4 edges.1
  10.3 3.4 %collective-permute-start.3 = (f32[4,64,128]{2,1,0:T(8,128)S(1)}, f32[4,64,128]{2,1,0:T(8,128)S(1)}, u32[]{:S(2)}, u32[]{:S(2)}) collective-permute-start(f32[4,64,128]{2,1,0:T(8,128)S(1)} %get-tuple-element.52.refs_3_), channel_id=1, source_target_pairs={{0,15},{1,0},{2,1},{3,2},{4,3},{5,4},{6,5},{7,6},{8,7},{9,8},{10,9... | collective-permute-start | bytes 393224 | tf_op jit(solution)/shard_map/ppermute | solution.py:718
  13.7 0.8 collective-permute-start.2
  14.5 0.1 pad_add_fusion.refs_0_
  14.6 2.4 %main.1 = (f32[16,64,128]{2,1,0:T(8,128)S(1)}, f32[16,64,128]{2,1,0:T(8,128)S(1)}, f32[16,64,128]{2,1,0:T(8,128)S(1)}, f32[16,64,128]{2,1,0:T(8,128)S(1)}, f32[1...) custom-call(s32[2]{0:T(128)S(1)} %pad_add_fusion.refs_0_, ...), custom_call_target="tpu_custom_call" | custom-call | flops 4000000 | bytes 4000000 | tf_op jit(solution)/shard_map/main/pallas_call | solution.py:736
  17.0 0.1 collective-permute-done.3.refs_6_
  17.1 1.3 %collective-permute-done.2.refs_5_ = f32[4,64,128]{2,1,0:T(8,128)S(1)} collective-permute-done((f32[4,64,128]{2,1,0:T(8,128)S(1)}, f32[4,64,128]{2,1,0:T(8,128)S(1)}, u32[]{:S(2)}, u32[]{:S(2)}) %collective-permute-start.2) | collective-permute-done | bytes 131104 | tf_op jit(solution)/shard_map/ppermute | solution.py:718
  18.4 3.2 %fine.1 = (f32[8,8,128]{2,1,0:T(8,128)S(1)}, f32[16,40,128]{2,1,0:T(8,128)S(1)}, f32[16,40,128]{2,1,0:T(8,128)S(1)}, f32[16,40,128]{2,1,0:T(8,128)S(1)}, f32[16,...) custom-call(s32[2]{0:T(128)S(1)} %pad_add_fusion.refs_0_, ...), custom_call_target="tpu_custom_call" | custom-call | flops 4000000 | bytes 4000000 | tf_op jit(solution)/shard_map/fine/pallas_call | solution.py:736
  21.5 0.1 collective-permute-start.4
  21.6 5.1 %collective-permute-start.7 = (f32[8,8,128]{2,1,0:T(8,128)S(1)}, f32[8,8,128]{2,1,0:T(8,128)S(1)}, u32[]{:S(2)}, u32[]{:S(2)}) collective-permute-start(f32[8,8,128]{2,1,0:T(8,128)S(1)} %get-tuple-element.54), channel_id=1, source_target_pairs={{0,224},{16,240},{32,0},{48,16},{64,32},{80,48},{96,64},{112,80},{... | collective-permute-start | bytes 98312 | tf_op jit(solution)/shard_map/ppermute | solution.py:718
  26.7 2.5 %collective-permute-start.6 = (f32[8,8,128]{2,1,0:T(8,128)S(1)}, f32[8,8,128]{2,1,0:T(8,128)S(1)}, u32[]{:S(2)}, u32[]{:S(2)}) collective-permute-start(f32[8,8,128]{2,1,0:T(8,128)S(1)} %get-tuple-element.54), channel_id=1, source_target_pairs={{0,240},{16,0},{32,16},{48,32},{64,48},{80,64},{96,80},{112,96},{1... | collective-permute-start | bytes 98312 | tf_op jit(solution)/shard_map/ppermute | solution.py:718
  29.2 0.0 collective-permute-start.5
  29.2 0.0 collective-permute-done.4
  29.2 6.1 %collective-permute-done.5 = f32[8,8,128]{2,1,0:T(8,128)S(1)} collective-permute-done((f32[8,8,128]{2,1,0:T(8,128)S(1)}, f32[8,8,128]{2,1,0:T(8,128)S(1)}, u32[]{:S(2)}, u32[]{:S(2)}) %collective-permute-start.5) | collective-permute-done | bytes 32800 | tf_op jit(solution)/shard_map/ppermute | solution.py:718
  35.3 0.0 collective-permute-done.6
  35.3 0.0 collective-permute-done.7
  35.4 2.8 %collective-permute-start.8 = (f32[4,40,128]{2,1,0:T(8,128)S(1)}, f32[4,40,128]{2,1,0:T(8,128)S(1)}, u32[]{:S(2)}, u32[]{:S(2)}) collective-permute-start(f32[4,40,128]{2,1,0:T(8,128)S(1)} %get-tuple-element.93.refs_2_), channel_id=1, source_target_pairs={{0,1},{1,2},{2,3},{3,4},{4,5},{5,6},{6,7},{7,8},{8,9},{9,10},{10,1... | collective-permute-start | bytes 245768 | tf_op jit(solution)/shard_map/ppermute | solution.py:718
  38.2 4.0 %collective-permute-start.9 = (f32[4,40,128]{2,1,0:T(8,128)S(1)}, f32[4,40,128]{2,1,0:T(8,128)S(1)}, u32[]{:S(2)}, u32[]{:S(2)}) collective-permute-start(f32[4,40,128]{2,1,0:T(8,128)S(1)} %get-tuple-element.94.refs_1_), channel_id=1, source_target_pairs={{0,15},{1,0},{2,1},{3,2},{4,3},{5,4},{6,5},{7,6},{8,7},{9,8},{10,9... | collective-permute-start | bytes 245768 | tf_op jit(solution)/shard_map/ppermute | solution.py:718
  42.1 0.7 collective-permute-done.8.refs_3_
  42.9 0.2 collective-permute-done.9.refs_4_
  43.1 3.3 %coarser.1 = (f32[4,128]{1,0:T(4,128)S(1)}, f32[16,40,128]{2,1,0:T(8,128)S(1)}, f32[16,40,128]{2,1,0:T(8,128)S(1)}, f32[16,40,128]{2,1,0:T(8,128)S(1)}, f32[16,4...) custom-call(s32[2]{0:T(128)S(1)} %pad_add_fusion.refs_0_, ...), custom_call_target="tpu_custom_call" | custom-call | flops 4000000 | bytes 4000000 | tf_op jit(solution)/shard_map/coarser/pallas_call | solution.py:736
  46.4 15.8 %all_to_all.10 = f32[16,4,128]{2,1,0:T(4,128)S(1)} all-to-all(f32[16,4,128]{2,1,0:T(4,128)S(1)} %broadcast_in_dim.6), channel_id=1, replica_groups=mesh['gx'=16,'gy'=16] {'gy'}, dimensions={0} | all-to-all | bytes 65536 | tf_op jit(solution)/shard_map/all_to_all | solution.py:724
  62.3 13.6 %all_to_all.11 = f32[16,64,128]{2,1,0:T(8,128)S(1)} all-to-all(f32[16,64,128]{2,1,0:T(8,128)S(1)} %broadcast_in_dim.15), channel_id=1, replica_groups=mesh['gx'=16,'gy'=16] {'gx'}, dimensions={0} | all-to-all | bytes 1048576 | tf_op jit(solution)/shard_map/all_to_all | solution.py:724
  75.8 7.1 %top.1 = f32[16,32,128]{2,1,0:T(8,128)} custom-call(s32[2]{0:T(128)S(1)} %pad_add_fusion.refs_0_, f32[1024,128]{1,0:T(8,128)S(1)} %bitcast.8, f32[16,64,128]{2,1,0:T(8,128)S(1)} %get-tuple-element.56.refs_2_, f32[16,64,128]{2,1,0:T(8,128)S(1)} %get-tuple-element.57.refs_3_, f32[16,64,128]{2,1,0:T(8,128)S(1)} %get-tuple-element.58.refs_4_, ...), custom_call_target="tpu_custom_call" | custom-call | flops 4000000 | bytes 4000000 | tf_op jit(solution)/shard_map/top/pallas_call | solution.py:736
  (8 shorter events, 0.1 us)
Async XLA Ops:
  1.1 6.1 %copy-start.1 = (f32[16,32,128]{2,1,0:T(8,128)S(1)}, f32[16,32,128]{2,1,0:T(8,128)}, u32[]{:S(2)}) copy-start(f32[16,32,128]{2,1,0:T(8,128)} %rho_ref.1) | copy-start | bytes 786436
  1.2 6.0 %copy-start = (f32[16,32,128]{2,1,0:T(8,128)S(1)}, f32[16,32,128]{2,1,0:T(8,128)}, u32[]{:S(2)}) copy-start(f32[16,32,128]{2,1,0:T(8,128)} %f_ref.1) | copy-start | bytes 786436
  1.2 8.7 %collective-permute-start = (f32[352,128]{1,0:T(8,128)S(1)}, f32[352,128]{1,0:T(8,128)S(1)}, u32[]{:S(2)}, u32[]{:S(2)}) collective-permute-start(f32[352,128]{1,0:T(8,128)S(1)} %bitcast.9), channel_id=1, source_target_pairs={{0,16},{16,32},{32,48},{48,64},{64,80},{80,96},{96,112},{112,128},... | collective-permute-start | bytes 540680 | tf_op jit(solution)/shard_map/ppermute | solution.py:718
  3.4 6.5 %collective-permute-start.1 = (f32[352,128]{1,0:T(8,128)S(1)}, f32[352,128]{1,0:T(8,128)S(1)}, u32[]{:S(2)}, u32[]{:S(2)}) collective-permute-start(f32[352,128]{1,0:T(8,128)S(1)} %bitcast.10), channel_id=1, source_target_pairs={{0,240},{16,0},{32,16},{48,32},{64,48},{80,64},{96,80},{112,96},{1... | collective-permute-start | bytes 540680 | tf_op jit(solution)/shard_map/ppermute | solution.py:718
  10.3 6.8 %collective-permute-start.3 = (f32[4,64,128]{2,1,0:T(8,128)S(1)}, f32[4,64,128]{2,1,0:T(8,128)S(1)}, u32[]{:S(2)}, u32[]{:S(2)}) collective-permute-start(f32[4,64,128]{2,1,0:T(8,128)S(1)} %get-tuple-element.52.refs_3_), channel_id=1, source_target_pairs={{0,15},{1,0},{2,1},{3,2},{4,3},{5,4},{6,5},{7,6},{8,7},{9,8},{10,9... | collective-permute-start | bytes 393224 | tf_op jit(solution)/shard_map/ppermute | solution.py:718
  13.7 4.6 %collective-permute-start.2 = (f32[4,64,128]{2,1,0:T(8,128)S(1)}, f32[4,64,128]{2,1,0:T(8,128)S(1)}, u32[]{:S(2)}, u32[]{:S(2)}) collective-permute-start(f32[4,64,128]{2,1,0:T(8,128)S(1)} %get-tuple-element.53.refs_4_), channel_id=1, source_target_pairs={{0,1},{1,2},{2,3},{3,4},{4,5},{5,6},{6,7},{7,8},{8,9},{9,10},{10,1... | collective-permute-start | bytes 393224 | tf_op jit(solution)/shard_map/ppermute | solution.py:718
  21.5 7.7 %collective-permute-start.4 = (f32[8,8,128]{2,1,0:T(8,128)S(1)}, f32[8,8,128]{2,1,0:T(8,128)S(1)}, u32[]{:S(2)}, u32[]{:S(2)}) collective-permute-start(f32[8,8,128]{2,1,0:T(8,128)S(1)} %get-tuple-element.54), channel_id=1, source_target_pairs={{0,32},{16,48},{32,64},{48,80},{64,96},{80,112},{96,128},{112,144}... | collective-permute-start | bytes 98312 | tf_op jit(solution)/shard_map/ppermute | solution.py:718
  21.6 13.7 %collective-permute-start.7 = (f32[8,8,128]{2,1,0:T(8,128)S(1)}, f32[8,8,128]{2,1,0:T(8,128)S(1)}, u32[]{:S(2)}, u32[]{:S(2)}) collective-permute-start(f32[8,8,128]{2,1,0:T(8,128)S(1)} %get-tuple-element.54), channel_id=1, source_target_pairs={{0,224},{16,240},{32,0},{48,16},{64,32},{80,48},{96,64},{112,80},{... | collective-permute-start | bytes 98312 | tf_op jit(solution)/shard_map/ppermute | solution.py:718
  26.7 8.6 %collective-permute-start.6 = (f32[8,8,128]{2,1,0:T(8,128)S(1)}, f32[8,8,128]{2,1,0:T(8,128)S(1)}, u32[]{:S(2)}, u32[]{:S(2)}) collective-permute-start(f32[8,8,128]{2,1,0:T(8,128)S(1)} %get-tuple-element.54), channel_id=1, source_target_pairs={{0,240},{16,0},{32,16},{48,32},{64,48},{80,64},{96,80},{112,96},{1... | collective-permute-start | bytes 98312 | tf_op jit(solution)/shard_map/ppermute | solution.py:718
  29.2 6.1 %collective-permute-start.5 = (f32[8,8,128]{2,1,0:T(8,128)S(1)}, f32[8,8,128]{2,1,0:T(8,128)S(1)}, u32[]{:S(2)}, u32[]{:S(2)}) collective-permute-start(f32[8,8,128]{2,1,0:T(8,128)S(1)} %get-tuple-element.54), channel_id=1, source_target_pairs={{0,16},{16,32},{32,48},{48,64},{64,80},{80,96},{96,112},{112,128},... | collective-permute-start | bytes 98312 | tf_op jit(solution)/shard_map/ppermute | solution.py:718
  35.4 7.5 %collective-permute-start.8 = (f32[4,40,128]{2,1,0:T(8,128)S(1)}, f32[4,40,128]{2,1,0:T(8,128)S(1)}, u32[]{:S(2)}, u32[]{:S(2)}) collective-permute-start(f32[4,40,128]{2,1,0:T(8,128)S(1)} %get-tuple-element.93.refs_2_), channel_id=1, source_target_pairs={{0,1},{1,2},{2,3},{3,4},{4,5},{5,6},{6,7},{7,8},{8,9},{9,10},{10,1... | collective-permute-start | bytes 245768 | tf_op jit(solution)/shard_map/ppermute | solution.py:718
  38.2 4.9 %collective-permute-start.9 = (f32[4,40,128]{2,1,0:T(8,128)S(1)}, f32[4,40,128]{2,1,0:T(8,128)S(1)}, u32[]{:S(2)}, u32[]{:S(2)}) collective-permute-start(f32[4,40,128]{2,1,0:T(8,128)S(1)} %get-tuple-element.94.refs_1_), channel_id=1, source_target_pairs={{0,15},{1,0},{2,1},{3,2},{4,3},{5,4},{6,5},{7,6},{8,7},{9,8},{10,9... | collective-permute-start | bytes 245768 | tf_op jit(solution)/shard_map/ppermute | solution.py:718
